TPU v7x, 256 devices: a whole 4x4x8 slice. The times are simulated.
256 devices in a mesh: dp: 8 (over z), expert: 16 (over y, x), pipe: 2 (over core).
Axes of the slice: x: 4, y: 4, z: 8, core: 2. Of those that a mesh axis runs over, the one named last changes fastest.
Arguments:
- layer_io: bfloat16 [2, 2, 4096, 7168], P('pipe', None, ('dp', 'expert')), may hold values from -6 to 6
- route_ids: int32 [2, 2, 4096, 8], P('pipe', None, ('dp', 'expert')), may hold values from 0 to 63, all different within a row
- route_weights: float32 [2, 2, 4096, 8], P('pipe', None, ('dp', 'expert')), may hold values from 0.1 to 0.5
- gate_weight: bfloat16 [2, 16, 7168, 1024], P('pipe', 'expert', 'dp'), may hold values from -0.0625 to 0.0625
- up_weight: bfloat16 [2, 16, 7168, 1024], P('pipe', 'expert', 'dp'), may hold values from -0.0625 to 0.0625
- down_weight: bfloat16 [2, 16, 1024, 7168], P('pipe', 'expert', None, 'dp'), may hold values from -0.1875 to 0.1875
Outputs:
- layer_out: bfloat16 [2, 2, 4096, 7168], P('pipe', None, ('dp', 'expert'))
- grad_gate_weight: bfloat16 [2, 16, 7168, 1024], P('pipe', 'expert', 'dp')
- grad_up_weight: bfloat16 [2, 16, 7168, 1024], P('pipe', 'expert', 'dp')
- grad_down_weight: bfloat16 [2, 16, 1024, 7168], P('pipe', 'expert', None, 'dp')
All inputs are finite; a program needn't handle non-finite values.
Results may differ from a plain program's by a relative error of at most 0.039.
Values may be sent and summed in bfloat16 or wider, within the bound.
No kernel may reach another device: no remote copies, remote signals or barrier semaphores. Data moves between devices by JAX's collectives and lax.ppermute only.
A program may use at most 128 MiB of HBM per device.

v0:
```python
import jax
import jax.numpy as jnp
from jax import lax
from jax.sharding import PartitionSpec as P

ROUTED = 64
MICRO = 2
CAPACITY = 2


highest = lax.Precision.HIGHEST


def passed_along(block, axis, distance):
    devices = range(lax.axis_size(axis))
    route = [(i - distance, i) for i in devices if i - distance in devices]
    return lax.ppermute(block, axis, route)


def route_tables(chosen_ids, weights, experts):
    tokens, top_count = chosen_ids.shape
    flat_ids = chosen_ids.reshape(tokens * top_count)
    onehot = (flat_ids[:, None] == jnp.arange(ROUTED, dtype=jnp.int32)[None, :]).astype(jnp.int32)
    before = jnp.cumsum(onehot, axis=0) - onehot
    position = jnp.sum(before * onehot, axis=1)
    keep_mask = (flat_ids < experts) & (position < CAPACITY)
    target = jnp.where(keep_mask, flat_ids * CAPACITY + position, -1)
    places = jnp.arange(experts * CAPACITY, dtype=jnp.int32)
    chosen = (
        (target[:, None] == places[None, :])
        .astype(jnp.float32)
        .reshape(tokens, top_count, experts * CAPACITY)
    )
    placing = jnp.sum(chosen, axis=1)
    mixing = jnp.sum(chosen * weights[:, :, None], axis=1)
    return (placing, mixing)


def swap_rows(rows):
    return lax.all_to_all(rows, ("dp", "expert"), split_axis=0, concat_axis=0, tiled=True)


def pass_section(values, offset):
    return passed_along(values, "pipe", offset)


def send_rows(matrix, values, groups):
    width = values.shape[1]
    part_width = width // groups
    slots = matrix.shape[1]
    buffer = jnp.einsum(
        "ts,tgd->gsd",
        matrix,
        values.reshape(values.shape[0], groups, part_width),
        precision=highest,
    ).astype(jnp.bfloat16)
    moved = swap_rows(buffer.reshape(groups * slots, part_width))
    return moved


def receive_rows(rows, matrix, groups):
    part_width = rows.shape[1]
    slots = matrix.shape[1]
    moved = swap_rows(rows).reshape(groups, slots, part_width).astype(jnp.float32)
    mixed = jnp.einsum("ts,gsd->tgd", matrix, moved, precision=highest)
    return mixed.reshape(matrix.shape[0], groups * part_width)


def expert_forward(rows_in, gate_up, down_part, own_rows):
    hidden_width = down_part.shape[0]
    summed = lax.psum(
        jnp.dot(rows_in, gate_up, preferred_element_type=jnp.float32).astype(jnp.bfloat16), "dp"
    ).astype(jnp.float32)
    hidden_all = (jax.nn.silu(summed[:, :hidden_width]) * summed[:, hidden_width:]).astype(
        jnp.bfloat16
    )
    own_sums = lax.dynamic_slice_in_dim(summed, lax.axis_index("dp") * own_rows, own_rows, 0)
    output = jnp.dot(hidden_all, down_part, preferred_element_type=jnp.float32).astype(jnp.bfloat16)
    return (output, own_sums, hidden_all)


def expert_backward(grad_rows, rows_in, own_sums, hidden_all, gate_up, down_part):
    hidden_width = down_part.shape[0]
    grad_hidden = lax.psum_scatter(
        lax.dot_general(
            grad_rows, down_part, (((1,), (1,)), ((), ())), preferred_element_type=jnp.float32
        ).astype(jnp.bfloat16),
        "dp",
        scatter_dimension=0,
        tiled=True,
    ).astype(jnp.float32)
    gate = own_sums[:, :hidden_width]
    up = own_sums[:, hidden_width:]
    sigmoid_gate = jax.nn.sigmoid(gate)
    grad_gate = (grad_hidden * up * sigmoid_gate * (1.0 + gate * (1.0 - sigmoid_gate))).astype(
        jnp.bfloat16
    )
    grad_up = (grad_hidden * gate * sigmoid_gate).astype(jnp.bfloat16)
    grads_own = jnp.concatenate([grad_gate, grad_up], axis=1)
    grads_all = lax.all_gather(grads_own, "dp", axis=0, tiled=True)
    back_rows = lax.dot_general(
        grads_all, gate_up, (((1,), (1,)), ((), ())), preferred_element_type=jnp.float32
    ).astype(jnp.bfloat16)
    weight_gate_up = lax.dot_general(
        rows_in, grads_all, (((0,), (0,)), ((), ())), preferred_element_type=jnp.float32
    )
    weight_down = lax.dot_general(
        hidden_all, grad_rows, (((0,), (0,)), ((), ())), preferred_element_type=jnp.float32
    )
    return (back_rows, weight_gate_up, weight_down)


def shards(layer_io, route_ids, route_weights, gate_weight, up_weight, down_weight):
    groups = lax.axis_size("dp")
    experts = lax.axis_size("expert")
    section = lax.axis_index("pipe")
    first_section = section == 0
    own_io = layer_io[0]
    tokens = own_io.shape[1]
    width = own_io.shape[2]
    hidden_width = gate_weight.shape[3]
    gate_up = jnp.concatenate([gate_weight[0, 0], up_weight[0, 0]], axis=1)
    down_part = down_weight[0, 0]
    own_rows = experts * CAPACITY
    blank = jnp.zeros((tokens, width), jnp.bfloat16)
    records = []
    finals = []
    previous = blank
    for forward_step in range(MICRO + 1):
        micro_index = jnp.clip(forward_step - section, 0, MICRO - 1)
        arrived = blank if forward_step == 0 else pass_section(previous, 1)
        fresh = own_io[forward_step] if forward_step < MICRO else blank
        inputs = jnp.where(first_section, fresh, arrived)
        chosen_ids = lax.dynamic_index_in_dim(route_ids[0], micro_index, 0, keepdims=False)
        weights = lax.dynamic_index_in_dim(route_weights[0], micro_index, 0, keepdims=False)
        placing, mixing = route_tables(chosen_ids, weights, experts)
        rows_in = send_rows(placing, inputs.astype(jnp.float32), groups)
        output, own_sums, hidden_all = expert_forward(rows_in, gate_up, down_part, own_rows)
        mixed = receive_rows(output, mixing, groups)
        previous = (inputs.astype(jnp.float32) + mixed).astype(jnp.bfloat16)
        finals.append(previous)
        records.append((placing, mixing, rows_in, own_sums, hidden_all))
    grad_gate_up = jnp.zeros(gate_up.shape, jnp.float32)
    grad_down = jnp.zeros(down_part.shape, jnp.float32)
    returned = []
    upstream_prev = blank
    for back_step in range(MICRO + 1):
        arrived = blank if back_step == 0 else pass_section(upstream_prev, -1)
        fresh = own_io[MICRO - 1 - back_step] if back_step < MICRO else blank
        upstream = jnp.where(first_section, arrived, fresh)
        placing, mixing, rows_in, own_sums, hidden_all = records[MICRO - back_step]
        grad_rows = send_rows(mixing, upstream.astype(jnp.float32), groups)
        back_rows, part_gate_up, part_down = expert_backward(
            grad_rows, rows_in, own_sums, hidden_all, gate_up, down_part
        )
        grad_gate_up = grad_gate_up + part_gate_up
        grad_down = grad_down + part_down
        upstream_prev = (
            upstream.astype(jnp.float32) + receive_rows(back_rows, placing, groups)
        ).astype(jnp.bfloat16)
        returned.append(upstream_prev)
    final_stack = jnp.stack([finals[micro_index + 1] for micro_index in range(MICRO)])
    grad_stack = jnp.stack([returned[MICRO - micro_index] for micro_index in range(MICRO)])
    layer_out = jnp.where(first_section, grad_stack, final_stack)[None]
    grad_gate_out = grad_gate_up[:, :hidden_width].astype(jnp.bfloat16)[None, None]
    grad_up_out = grad_gate_up[:, hidden_width:].astype(jnp.bfloat16)[None, None]
    grad_down_out = grad_down.astype(jnp.bfloat16)[None, None]
    return (layer_out, grad_gate_out, grad_up_out, grad_down_out)


def solution(mesh):
    return jax.shard_map(
        shards,
        mesh=mesh,
        in_specs=(
            P("pipe", None, ("dp", "expert"), None),
            P("pipe", None, ("dp", "expert"), None),
            P("pipe", None, ("dp", "expert"), None),
            P("pipe", "expert", "dp", None),
            P("pipe", "expert", "dp", None),
            P("pipe", "expert", None, "dp"),
        ),
        out_specs=(
            P("pipe", None, ("dp", "expert"), None),
            P("pipe", "expert", "dp", None),
            P("pipe", "expert", "dp", None),
            P("pipe", "expert", None, "dp"),
        ),
        check_vma=False,
    )
```

profile of v0, /device:TPU:1, one launch (start us, length us, event | category | flops | bytes accessed | tf_op | source)
XLA Modules:
  0.0 831.0 jit_solution(5919845884118491454)
XLA Ops:
  13.2 33.2 %all_to_all.126 = bf16[128,2,896]{2,1,0:T(2,128)(2,1)S(1)} all-to-all(bf16[128,2,896]{2,1,0:T(2,128)(2,1)S(1)} %all_to_all.87), channel_id=1, replica_groups=mesh['dp'=8,'expert'=16,'pipe'=2] {'dp','expert'}, dimensions={0} | all-to-all | bytes 917504 | tf_op jit(solution)/shard_map/all_to_all | solution.py:40
  46.6 4.4 convolution_convert_fusion.2
  51.1 67.0 %all-reduce.4.cloned.1.call-done = bf16[256,2048]{1,0:T(8,128)(2,1)} async-done(((bf16[256,2048]{1,0:T(8,128)(2,1)}), bf16[256,2048]{1,0:T(8,128)(2,1)}) %all-reduce.4.cloned.1.call-update) | async-done | bytes 1048592 | tf_op jit(solution)/shard_map/psum | solution.py:71
  123.7 10.7 %all-to-all-start.2 = ((bf16[128,2,896]{2,1,0:T(2,128)(2,1)}), bf16[128,2,896]{2,1,0:T(2,128)(2,1)S(1)}, u32[]{:S(2)}, u32[]{:S(2)}) async-start(bf16[128,2,896]{2,1,0:T(2,128)(2,1)} %all_to_all.90), calls=%async_computation.3 | async-start | bytes 917504 | tf_op jit(solution)/shard_map/all_to_all | solution.py:40
  135.6 13.4 %all-to-all-done.2 = bf16[128,2,896]{2,1,0:T(2,128)(2,1)S(1)} async-done(((bf16[128,2,896]{2,1,0:T(2,128)(2,1)}), bf16[128,2,896]{2,1,0:T(2,128)(2,1)S(1)}, u32[]{:S(2)}, u32[]{:S(2)}) %all-to-all-start.2) | async-done | bytes 458784 | tf_op jit(solution)/shard_map/all_to_all | solution.py:40
  153.2 7.6 collective-permute-done
  165.1 26.4 %all_to_all.127 = bf16[128,2,896]{2,1,0:T(2,128)(2,1)} all-to-all(bf16[128,2,896]{2,1,0:T(2,128)(2,1)} %all_to_all.92), channel_id=1, replica_groups=mesh['dp'=8,'expert'=16,'pipe'=2] {'dp','expert'}, dimensions={0} | all-to-all | bytes 917504 | tf_op jit(solution)/shard_map/all_to_all | solution.py:40
  193.5 4.4 convolution_convert_fusion.1
  197.9 64.3 %all-reduce.6.cloned.1.call-done = bf16[256,2048]{1,0:T(8,128)(2,1)} async-done(((bf16[256,2048]{1,0:T(8,128)(2,1)}), bf16[256,2048]{1,0:T(8,128)(2,1)}) %all-reduce.6.cloned.1.call-update) | async-done | bytes 1048592 | tf_op jit(solution)/shard_map/psum | solution.py:71
  269.6 11.1 %all-to-all-start.4 = ((bf16[128,2,896]{2,1,0:T(2,128)(2,1)}), bf16[128,2,896]{2,1,0:T(2,128)(2,1)}, u32[]{:S(2)}, u32[]{:S(2)}) async-start(bf16[128,2,896]{2,1,0:T(2,128)(2,1)} %all_to_all.95), calls=%async_computation.5 | async-start | bytes 917504 | tf_op jit(solution)/shard_map/all_to_all | solution.py:40
  281.9 13.1 %all-to-all-done.4 = bf16[128,2,896]{2,1,0:T(2,128)(2,1)} async-done(((bf16[128,2,896]{2,1,0:T(2,128)(2,1)}), bf16[128,2,896]{2,1,0:T(2,128)(2,1)}, u32[]{:S(2)}, u32[]{:S(2)}) %all-to-all-start.4) | async-done | bytes 458784 | tf_op jit(solution)/shard_map/all_to_all | solution.py:40
  301.0 7.6 collective-permute-done.1
  312.9 7.2 all-to-all-start.5
  324.5 14.4 %all-to-all-done.5 = bf16[128,2,896]{2,1,0:T(2,128)(2,1)} async-done(((bf16[128,2,896]{2,1,0:T(2,128)(2,1)}), bf16[128,2,896]{2,1,0:T(2,128)(2,1)}, u32[]{:S(2)}, u32[]{:S(2)}) %all-to-all-start.5) | async-done | bytes 458784 | tf_op jit(solution)/shard_map/all_to_all | solution.py:40
  338.9 7.2 all-to-all-start
  348.4 4.4 convolution_convert_fusion
  352.9 12.0 %all-to-all-done = bf16[128,2,896]{2,1,0:T(2,128)(2,1)} async-done(((bf16[128,2,896]{2,1,0:T(2,128)(2,1)}), bf16[128,2,896]{2,1,0:T(2,128)(2,1)}, u32[]{:S(2)}, u32[]{:S(2)}) %all-to-all-start) | async-done | bytes 458784 | tf_op jit(solution)/shard_map/all_to_all | solution.py:40
  364.9 2.0 all_to_all.86
  366.9 2.6 fusion.15
  369.6 55.3 %all-reduce.8.cloned.1.call-done = bf16[256,2048]{1,0:T(8,128)(2,1)} async-done(((bf16[256,2048]{1,0:T(8,128)(2,1)}), bf16[256,2048]{1,0:T(8,128)(2,1)}) %all-reduce.8.cloned.1.call-update) | async-done | bytes 1048592 | tf_op jit(solution)/shard_map/psum | solution.py:71
  424.9 2.8 convert_element_type.236
  427.7 35.2 %reduce-scatter.4.cloned.1.call-done = bf16[32,1024]{1,0:T(8,128)(2,1)} async-done(((bf16[256,1024]{1,0:T(8,128)(2,1)}), bf16[32,1024]{1,0:T(8,128)(2,1)}) %reduce-scatter.4.cloned.1.call-update) | async-done | bytes 65552 | tf_op jit(solution)/shard_map/reduce_scatter | solution.py:84
  464.6 37.6 %all-gather.4.cloned.1.call-done = bf16[256,2048]{1,0:T(8,128)(2,1)} async-done(((bf16[32,2048]{1,0:T(8,128)(2,1)}), bf16[256,2048]{1,0:T(8,128)(2,1)}) %all-gather.4.cloned.1.call-update) | async-done | bytes 1048592 | tf_op jit(solution)/shard_map/all_gather | solution.py:100
  502.2 4.4 convolution_convert_fusion.11
  508.6 26.4 %all_to_all.128 = bf16[128,2,896]{2,1,0:T(2,128)(2,1)} all-to-all(bf16[128,2,896]{2,1,0:T(2,128)(2,1)} %all_to_all.100), channel_id=1, replica_groups=mesh['dp'=8,'expert'=16,'pipe'=2] {'dp','expert'}, dimensions={0} | all-to-all | bytes 917504 | tf_op jit(solution)/shard_map/all_to_all | solution.py:40
  538.6 8.4 %collective-permute-start.2 = (bf16[32,7168]{1,0:T(8,128)(2,1)S(1)}, bf16[32,7168]{1,0:T(8,128)(2,1)S(1)}, u32[]{:S(2)}, u32[]{:S(2)}) collective-permute-start(bf16[32,7168]{1,0:T(8,128)(2,1)S(1)} %fusion.1), channel_id=1, source_target_pairs={{1,0},{3,2},{5,4},{7,6},{9,8},{11,10},{13,12},{15,14},{17,16},{19,... | collective-permute-start | bytes 1376264 | tf_op jit(solution)/shard_map/ppermute | solution.py:17
  550.9 24.9 %all_to_all.129 = bf16[128,2,896]{2,1,0:T(2,128)(2,1)} all-to-all(bf16[128,2,896]{2,1,0:T(2,128)(2,1)} %all_to_all.102), channel_id=1, replica_groups=mesh['dp'=8,'expert'=16,'pipe'=2] {'dp','expert'}, dimensions={0} | all-to-all | bytes 917504 | tf_op jit(solution)/shard_map/all_to_all | solution.py:40
  578.6 27.0 %reduce-scatter.6.cloned.1.call-done = bf16[32,1024]{1,0:T(8,128)(2,1)} async-done(((bf16[256,1024]{1,0:T(8,128)(2,1)}), bf16[32,1024]{1,0:T(8,128)(2,1)}) %reduce-scatter.6.cloned.1.call-update) | async-done | bytes 65552 | tf_op jit(solution)/shard_map/reduce_scatter | solution.py:84
  607.4 37.6 %all-gather.6.cloned.1.call-done = bf16[256,2048]{1,0:T(8,128)(2,1)} async-done(((bf16[32,2048]{1,0:T(8,128)(2,1)}), bf16[256,2048]{1,0:T(8,128)(2,1)}) %all-gather.6.cloned.1.call-update) | async-done | bytes 1048592 | tf_op jit(solution)/shard_map/all_gather | solution.py:100
  645.0 4.4 convolution_convert_fusion.10
  651.3 26.3 %all_to_all.130 = bf16[128,2,896]{2,1,0:T(2,128)(2,1)S(1)} all-to-all(bf16[128,2,896]{2,1,0:T(2,128)(2,1)} %all_to_all.105), channel_id=1, replica_groups=mesh['dp'=8,'expert'=16,'pipe'=2] {'dp','expert'}, dimensions={0} | all-to-all | bytes 917504 | tf_op jit(solution)/shard_map/all_to_all | solution.py:40
  680.2 8.4 %collective-permute-start.3 = (bf16[32,7168]{1,0:T(8,128)(2,1)S(1)}, bf16[32,7168]{1,0:T(8,128)(2,1)S(1)}, u32[]{:S(2)}, u32[]{:S(2)}) collective-permute-start(bf16[32,7168]{1,0:T(8,128)(2,1)S(1)} %add_convert_fusion.4), channel_id=1, source_target_pairs={{1,0},{3,2},{5,4},{7,6},{9,8},{11,10},{13,12},{15,14},{17,16},{19,... | collective-permute-start | bytes 1376264 | tf_op jit(solution)/shard_map/ppermute | solution.py:17
  691.5 7.2 all-to-all-start.9
  700.7 15.6 %all-to-all-done.9 = bf16[128,2,896]{2,1,0:T(2,128)(2,1)} async-done(((bf16[128,2,896]{2,1,0:T(2,128)(2,1)}), bf16[128,2,896]{2,1,0:T(2,128)(2,1)}, u32[]{:S(2)}, u32[]{:S(2)}) %all-to-all-start.9) | async-done | bytes 458784 | tf_op jit(solution)/shard_map/all_to_all | solution.py:40
  718.2 2.6 fusion.21
  724.2 7.2 all-to-all-start.11
  731.7 3.7 fusion.92
  735.4 12.8 %all-to-all-done.11 = bf16[128,2,896]{2,1,0:T(2,128)(2,1)} async-done(((bf16[128,2,896]{2,1,0:T(2,128)(2,1)}), bf16[128,2,896]{2,1,0:T(2,128)(2,1)}, u32[]{:S(2)}, u32[]{:S(2)}) %all-to-all-start.11) | async-done | bytes 458784 | tf_op jit(solution)/shard_map/all_to_all | solution.py:40
  753.8 2.3 fusion.43
  756.1 5.4 fusion.90
  762.9 4.2 fusion.91
  769.1 21.1 %all-gather.8.cloned.1.call-done = bf16[256,2048]{1,0:T(8,128)(2,1)} async-done(((bf16[32,2048]{1,0:T(8,128)(2,1)}), bf16[256,2048]{1,0:T(8,128)(2,1)}) %all-gather.8.cloned.1.call-update) | async-done | bytes 1048592 | tf_op jit(solution)/shard_map/all_gather | solution.py:100
  790.2 3.7 convolution_convert_fusion.9
  794.8 11.7 %all-to-all-start.10 = ((bf16[128,2,896]{2,1,0:T(2,128)(2,1)}), bf16[128,2,896]{2,1,0:T(2,128)(2,1)S(1)}, u32[]{:S(2)}, u32[]{:S(2)}) async-start(bf16[128,2,896]{2,1,0:T(2,128)(2,1)} %all_to_all.110), calls=%async_computation.13 | async-start | bytes 917504 | tf_op jit(solution)/shard_map/all_to_all | solution.py:40
  806.5 6.6 add_convert_fusion
  813.1 2.2 slice_bitcast_fusion
  815.4 5.8 all-to-all-done.10
  821.9 2.4 maximum_select_fusion
  (166 shorter events, 90.2 us)
Async XLA Ops:
  7.2 114.8 %copy-start = (bf16[1,1,1024,896]{3,2,1,0:T(8,128)(2,1)S(1)}, bf16[1,1,1024,896]{3,2,1,0:T(8,128)(2,1)}, u32[]{:S(2)}) copy-start(bf16[1,1,1024,896]{3,2,1,0:T(8,128)(2,1)} %param.11) | copy-start | bytes 5505028
  7.2 110.9 %all-reduce.4.cloned.1.call-start = ((), (), s32[]{:S(2)}) async-start(), calls=%async_computation.16 | async-start | bytes 2097152 | tf_op jit(solution)/shard_map/psum | solution.py:71
  46.6 4.5 copy-start.14
  119.5 1.3 copy-start.2
  121.2 0.8 copy-start.7
  122.0 29.0 %copy-start.4 = (bf16[1,2,32,7168]{3,2,1,0:T(8,128)(2,1)S(1)}, bf16[1,2,32,7168]{3,2,1,0:T(8,128)(2,1)}, u32[]{:S(2)}) copy-start(bf16[1,2,32,7168]{3,2,1,0:T(8,128)(2,1)} %param.6) | copy-start | bytes 2752516
  123.7 25.3 %all-to-all-start.2 = ((bf16[128,2,896]{2,1,0:T(2,128)(2,1)}), bf16[128,2,896]{2,1,0:T(2,128)(2,1)S(1)}, u32[]{:S(2)}, u32[]{:S(2)}) async-start(bf16[128,2,896]{2,1,0:T(2,128)(2,1)} %all_to_all.90), calls=%async_computation.3 | async-start | bytes 917504 | tf_op jit(solution)/shard_map/all_to_all | solution.py:40
  134.3 128.0 %all-reduce.6.cloned.1.call-start = ((), (), s32[]{:S(2)}) async-start(), calls=%async_computation.17 | async-start | bytes 2097152 | tf_op jit(solution)/shard_map/psum | solution.py:71
  151.5 9.3 %collective-permute-start = (bf16[32,7168]{1,0:T(8,128)(2,1)S(1)}, bf16[32,7168]{1,0:T(8,128)(2,1)}, u32[]{:S(2)}, u32[]{:S(2)}) collective-permute-start(bf16[32,7168]{1,0:T(8,128)(2,1)S(1)} %fusion), channel_id=1, source_target_pairs={{0,1},{2,3},{4,5},{6,7},{8,9},{10,11},{12,13},{14,15},{16,17},{18,... | collective-permute-start | bytes 1376264 | tf_op jit(solution)/shard_map/ppermute | solution.py:17
  263.8 1.3 copy-start.3
  265.4 0.8 copy-start.9
  269.6 25.4 %all-to-all-start.4 = ((bf16[128,2,896]{2,1,0:T(2,128)(2,1)}), bf16[128,2,896]{2,1,0:T(2,128)(2,1)}, u32[]{:S(2)}, u32[]{:S(2)}) async-start(bf16[128,2,896]{2,1,0:T(2,128)(2,1)} %all_to_all.95), calls=%async_computation.5 | async-start | bytes 917504 | tf_op jit(solution)/shard_map/all_to_all | solution.py:40
  299.3 9.2 %collective-permute-start.1 = (bf16[32,7168]{1,0:T(8,128)(2,1)}, bf16[32,7168]{1,0:T(8,128)(2,1)}, u32[]{:S(2)}, u32[]{:S(2)}) collective-permute-start(bf16[32,7168]{1,0:T(8,128)(2,1)} %add_convert_fusion.5), channel_id=1, source_target_pairs={{0,1},{2,3},{4,5},{6,7},{8,9},{10,11},{12,13},{14,15},{16,17},{18,... | collective-permute-start | bytes 1376264 | tf_op jit(solution)/shard_map/ppermute | solution.py:17
  312.9 26.0 %all-to-all-start.5 = ((bf16[128,2,896]{2,1,0:T(2,128)(2,1)}), bf16[128,2,896]{2,1,0:T(2,128)(2,1)}, u32[]{:S(2)}, u32[]{:S(2)}) async-start(bf16[128,2,896]{2,1,0:T(2,128)(2,1)} %all_to_all.97), calls=%async_computation.6 | async-start | bytes 917504 | tf_op jit(solution)/shard_map/all_to_all | solution.py:40
  338.9 26.0 %all-to-all-start = ((bf16[128,2,896]{2,1,0:T(2,128)(2,1)}), bf16[128,2,896]{2,1,0:T(2,128)(2,1)}, u32[]{:S(2)}, u32[]{:S(2)}) async-start(bf16[128,2,896]{2,1,0:T(2,128)(2,1)} %all_to_all.84), calls=%async_computation | async-start | bytes 917504 | tf_op jit(solution)/shard_map/all_to_all | solution.py:40
  346.2 78.7 %all-reduce.8.cloned.1.call-start = ((), (), s32[]{:S(2)}) async-start(), calls=%async_computation.18 | async-start | bytes 2097152 | tf_op jit(solution)/shard_map/psum | solution.py:71
  352.9 110.0 %reduce-scatter.4.cloned.1.call-start = ((), (), s32[]{:S(2)}) async-start(), calls=%async_computation.15 | async-start | bytes 589824 | tf_op jit(solution)/shard_map/reduce_scatter | solution.py:84
  369.5 132.7 %all-gather.4.cloned.1.call-start = ((), (), s32[]{:S(2)}) async-start(), calls=%async_computation.19 | async-start | bytes 1179648 | tf_op jit(solution)/shard_map/all_gather | solution.py:100
  464.6 141.1 %reduce-scatter.6.cloned.1.call-start = ((), (), s32[]{:S(2)}) async-start(), calls=%async_computation.20 | async-start | bytes 589824 | tf_op jit(solution)/shard_map/reduce_scatter | solution.py:84
  538.6 9.8 %collective-permute-start.2 = (bf16[32,7168]{1,0:T(8,128)(2,1)S(1)}, bf16[32,7168]{1,0:T(8,128)(2,1)S(1)}, u32[]{:S(2)}, u32[]{:S(2)}) collective-permute-start(bf16[32,7168]{1,0:T(8,128)(2,1)S(1)} %fusion.1), channel_id=1, source_target_pairs={{1,0},{3,2},{5,4},{7,6},{9,8},{11,10},{13,12},{15,14},{17,16},{19,... | collective-permute-start | bytes 1376264 | tf_op jit(solution)/shard_map/ppermute | solution.py:17
  577.0 72.4 %copy-start.12 = (bf16[256,896]{1,0:T(8,128)(2,1)}, bf16[256,896]{1,0:T(8,128)(2,1)S(1)}, u32[]{:S(2)}) copy-start(bf16[256,896]{1,0:T(8,128)(2,1)S(1)} %all_to_all.104) | copy-start | bytes 1376260
  578.6 66.4 %all-gather.6.cloned.1.call-start = ((), (), s32[]{:S(2)}) async-start(), calls=%async_computation.21 | async-start | bytes 1179648 | tf_op jit(solution)/shard_map/all_gather | solution.py:100
  680.2 9.8 %copy-start.17 = (bf16[32,7168]{1,0:T(8,128)(2,1)}, bf16[32,7168]{1,0:T(8,128)(2,1)S(1)}, u32[]{:S(2)}) copy-start(bf16[32,7168]{1,0:T(8,128)(2,1)S(1)} %add_convert_fusion.4) | copy-start | bytes 1376260
  680.2 9.8 %collective-permute-start.3 = (bf16[32,7168]{1,0:T(8,128)(2,1)S(1)}, bf16[32,7168]{1,0:T(8,128)(2,1)S(1)}, u32[]{:S(2)}, u32[]{:S(2)}) collective-permute-start(bf16[32,7168]{1,0:T(8,128)(2,1)S(1)} %add_convert_fusion.4), channel_id=1, source_target_pairs={{1,0},{3,2},{5,4},{7,6},{9,8},{11,10},{13,12},{15,14},{17,16},{19,... | collective-permute-start | bytes 1376264 | tf_op jit(solution)/shard_map/ppermute | solution.py:17
  691.5 24.7 %all-to-all-start.9 = ((bf16[128,2,896]{2,1,0:T(2,128)(2,1)}), bf16[128,2,896]{2,1,0:T(2,128)(2,1)}, u32[]{:S(2)}, u32[]{:S(2)}) async-start(bf16[128,2,896]{2,1,0:T(2,128)(2,1)} %all_to_all.107), calls=%async_computation.11 | async-start | bytes 917504 | tf_op jit(solution)/shard_map/all_to_all | solution.py:40
  698.8 53.2 %reduce-scatter.8.cloned.1.call-start = ((), (), s32[]{:S(2)}) async-start(), calls=%async_computation.22 | async-start | bytes 589824 | tf_op jit(solution)/shard_map/reduce_scatter | solution.py:84
  700.7 21.6 %copy-start.11 = (bf16[256,1024]{1,0:T(8,128)(2,1)}, bf16[256,1024]{1,0:T(8,128)(2,1)S(1)}, u32[]{:S(2)}) copy-start(bf16[256,1024]{1,0:T(8,128)(2,1)S(1)} %fusion.39) | copy-start | bytes 1572868
  724.2 24.0 %all-to-all-start.11 = ((bf16[128,2,896]{2,1,0:T(2,128)(2,1)}), bf16[128,2,896]{2,1,0:T(2,128)(2,1)}, u32[]{:S(2)}, u32[]{:S(2)}) async-start(bf16[128,2,896]{2,1,0:T(2,128)(2,1)} %all_to_all.112), calls=%async_computation.14 | async-start | bytes 917504 | tf_op jit(solution)/shard_map/all_to_all | solution.py:40
  731.5 24.6 %copy-start.6 = (bf16[256,896]{1,0:T(8,128)(2,1)S(1)}, bf16[256,896]{1,0:T(8,128)(2,1)}, u32[]{:S(2)}) copy-start(bf16[256,896]{1,0:T(8,128)(2,1)} %all_to_all.99) | copy-start | bytes 1376260
  731.5 58.7 %all-gather.8.cloned.1.call-start = ((), (), s32[]{:S(2)}) async-start(), calls=%async_computation.23 | async-start | bytes 1179648 | tf_op jit(solution)/shard_map/all_gather | solution.py:100
  756.1 5.4 copy-start.10
  756.1 5.4 copy-start.13
  761.5 1.0 copy-start.5
  761.5 1.4 copy-start.18
  762.9 4.2 copy-start.1
  762.9 4.2 copy-start.8
  762.9 4.2 copy-start.16
  769.1 37.4 %copy-start.15 = (bf16[256,896]{1,0:T(8,128)(2,1)S(1)}, bf16[256,896]{1,0:T(8,128)(2,1)}, u32[]{:S(2)}) copy-start(bf16[256,896]{1,0:T(8,128)(2,1)} %copy-done.14) | copy-start | bytes 1376260
  794.8 26.3 %all-to-all-start.10 = ((bf16[128,2,896]{2,1,0:T(2,128)(2,1)}), bf16[128,2,896]{2,1,0:T(2,128)(2,1)S(1)}, u32[]{:S(2)}, u32[]{:S(2)}) async-start(bf16[128,2,896]{2,1,0:T(2,128)(2,1)} %all_to_all.110), calls=%async_computation.13 | async-start | bytes 917504 | tf_op jit(solution)/shard_map/all_to_all | solution.py:40
Sparse Core Ops, SparseCore 0:
  51.2 66.8 all-reduce.3
  198.1 64.1 all-reduce.5
  353.0 71.8 all-reduce.7
  427.8 34.9 reduce-scatter.3
  465.1 37.0 all-gather.3
  578.7 26.8 reduce-scatter.5
  608.0 36.9 all-gather.5
  720.9 29.5 reduce-scatter.7
  753.9 36.2 all-gather.7
where the time goes:
time: 846 us; the launch traced here: 831 us
  waiting for transfers between devices  450 us (53%)
  blocking collectives  137 us (16%)
  starting transfers between devices  82.5 us (10%)
  matrix products  70.2 us (8%)
  local copies, waits for them, and re-layouts  52.6 us (6%)
  other arithmetic  23.7 us (3%)
  between operations  14.6 us (2%)
    psum x3, waiting for transfers between devices, expert_forward(): lax.psum(jnp.dot(rows_in, gate_up, preferred_element_type=jnp.float32).as...  187 us
    all_to_all x5, blocking collectives, swap_rows(): lax.all_to_all(rows, ('dp', 'expert'), split_axis=0, concat_axis=0, tiled...  137 us
    all_gather x3, waiting for transfers between devices, expert_backward(): grads_all = lax.all_gather(grads_own, 'dp', axis=0, tiled=True)  96.3 us
    all_to_all x7, waiting for transfers between devices, swap_rows(): lax.all_to_all(rows, ('dp', 'expert'), split_axis=0, concat_axis=0, tiled...  87 us
    all_to_all x7, starting transfers between devices, swap_rows(): lax.all_to_all(rows, ('dp', 'expert'), split_axis=0, concat_axis=0, tiled...  62.4 us
    reduce_scatter x3, waiting for transfers between devices, expert_backward(): lax.psum_scatter(lax.dot_general(grad_rows, down_part, (((1,), (1,)), (()...  62.1 us
    all_to_all x18, local copies, waits for them, and re-layouts, swap_rows(): lax.all_to_all(rows, ('dp', 'expert'), split_axis=0, concat_axis=0, tiled...  26.9 us
    ppermute x4, starting transfers between devices, passed_along(): return lax.ppermute(block, axis, route)  19.3 us
  transfers between devices with their start and end apart: 20, of which 19 were waited for; matrix products, arithmetic and copies ran while one was open for 6% of the time, Pallas kernels for 0%

commit v1 on v0

v1 whole, which is shorter than its diff:
```python
import jax
import jax.numpy as jnp
from jax import lax
from jax.sharding import PartitionSpec as P

CAPACITY = 2
LAYERS = 2
ROUTE_COLUMNS = 128

highest = lax.Precision.HIGHEST
bf16 = jnp.bfloat16
f32 = jnp.float32


def swap(values, axes):
    return lax.all_to_all(values, axes, split_axis=0, concat_axis=0, tiled=True)


def trade_cores(values):
    return lax.ppermute(values, "pipe", [(0, 1), (1, 0)])


def dot(a, b, contract):
    return lax.dot_general(a, b, ((contract[:1], contract[1:]), ((), ())), preferred_element_type=f32)


def route_columns(ids, weights, experts):
    tokens = ids.shape[1]
    hit = ids[..., None] == jnp.arange(experts, dtype=jnp.int32)
    chosen = jnp.any(hit, axis=2).astype(f32)
    weight = jnp.sum(jnp.where(hit, weights[..., None], 0.0), axis=2)
    earlier = (jnp.arange(tokens)[:, None] > jnp.arange(tokens)[None, :]).astype(f32)
    before = jnp.einsum("ts,mse->mte", earlier, chosen)
    code = jnp.where((chosen > 0) & (before < CAPACITY), before + 1.0, 0.0)
    high = lax.reduce_precision(weight, 8, 7)
    rest = weight - high
    middle = lax.reduce_precision(rest, 8, 7)
    low = rest - middle
    columns = jnp.concatenate([code, high, middle, low], axis=-1).astype(bf16)
    return jnp.pad(columns, ((0, 0), (0, 0), (0, ROUTE_COLUMNS - columns.shape[-1])))


def routing(columns, groups, experts):
    tokens = columns.shape[0]
    rows = experts * groups * CAPACITY
    row = jnp.arange(rows, dtype=jnp.int32)
    per_expert = groups * CAPACITY
    spread = (row[:, None] // per_expert == jnp.arange(experts)[None, :]).astype(bf16)
    parts = [columns[:, i * experts : (i + 1) * experts] for i in range(4)]
    code, high, middle, low = [dot(spread, part, (1, 1)) for part in parts]
    same_block = (row[:, None] % per_expert) // CAPACITY == (
        jnp.arange(tokens, dtype=jnp.int32)[None, :] // (tokens // groups)
    )
    slot = (row % CAPACITY + 1).astype(f32)
    mask = same_block & (code == slot[:, None])
    return mask.astype(bf16), jnp.where(mask, high + middle + low, 0.0)


def sum_over_dp(partial, groups):
    rows, width = partial.shape
    moved = swap(partial.reshape(groups, rows // groups, width), "dp")
    return jnp.sum(moved.astype(f32), axis=0)


def gather_over_dp(own, groups):
    moved = swap(jnp.broadcast_to(own[None], (groups,) + own.shape), "dp")
    return moved.reshape(groups * own.shape[0], own.shape[1])


def to_experts(rows, experts):
    moved = swap(rows.reshape(experts, rows.shape[0] // experts, rows.shape[1]), "expert")
    return moved.reshape(rows.shape)


def gradients_of(grad_hidden, gate, up):
    sig = jax.nn.sigmoid(gate)
    grad_gate = (grad_hidden * up * sig * (1.0 + gate * (1.0 - sig))).astype(bf16)
    grad_up = (grad_hidden * gate * sig).astype(bf16)
    return jnp.concatenate([grad_gate, grad_up], axis=1)


def shards(layer_io, route_ids, route_weights, gate_weight, up_weight, down_weight):
    groups = lax.axis_size("dp")
    experts = lax.axis_size("expert")
    first = lax.axis_index("pipe") == 0
    micro, tokens, width = layer_io.shape[1:]
    part = width // groups
    hidden_width = gate_weight.shape[3]

    other = [trade_cores(w) for w in (gate_weight[0, 0], up_weight[0, 0], down_weight[0, 0])]
    mine = [gate_weight[0, 0], up_weight[0, 0], down_weight[0, 0]]
    layer_weights = [
        [jnp.where(first, a, b) for a, b in zip(mine, other)],
        [jnp.where(first, b, a) for a, b in zip(mine, other)],
    ]
    gate_up = [jnp.concatenate(w[:2], axis=1) for w in layer_weights]
    down = [w[2] for w in layer_weights]

    columns = route_columns(route_ids[0], route_weights[0], experts)
    pieces = layer_io[0].reshape(micro, tokens, groups, part).transpose(2, 0, 1, 3)
    columns = jnp.broadcast_to(columns[None], (groups,) + columns.shape)
    sent = jnp.concatenate([pieces, columns], axis=3)
    got = swap(sent.reshape(groups * micro, tokens, part + ROUTE_COLUMNS), ("dp", "pipe"))
    got = got.reshape(groups, LAYERS, tokens, part + ROUTE_COLUMNS)
    inputs = got[:, 0, :, :part].reshape(groups * tokens, part)
    cotangent = got[:, 1, :, :part].reshape(groups * tokens, part)
    tables = [
        routing(got[:, l, :, part:].reshape(groups * tokens, ROUTE_COLUMNS), groups, experts)
        for l in range(LAYERS)
    ]

    def dispatch(placing, values):
        return to_experts(dot(placing, values, (1, 0)).astype(bf16), experts)

    def dispatch_scaled(placing, mixing, values):
        scale = jnp.sum(mixing, axis=1, keepdims=True)
        return to_experts((dot(placing, values, (1, 0)) * scale).astype(bf16), experts)

    def grad_hidden_of(grad_out, l):
        return sum_over_dp(dot(grad_out, down[l], (1, 1)).astype(bf16), groups)

    current = inputs
    rows, sums, hidden = [], [], []
    grad_out, grad_hidden = [None] * LAYERS, [None] * LAYERS
    for l in range(LAYERS):
        placing, mixing = tables[l]
        rows.append(dispatch(placing, current))
        sums.append(sum_over_dp(dot(rows[l], gate_up[l], (1, 0)).astype(bf16), groups))
        gate, up = sums[l][:, :hidden_width], sums[l][:, hidden_width:]
        hidden.append(gather_over_dp((jax.nn.silu(gate) * up).astype(bf16), groups))
        result = to_experts(dot(hidden[l], down[l], (1, 0)).astype(bf16), experts)
        mixed = lax.dot_general(
            mixing, result.astype(f32), (((0,), (0,)), ((), ())), precision=highest
        )
        current = (current.astype(f32) + mixed).astype(bf16)
    output = current

    upstream = cotangent
    grads = [None] * LAYERS
    for l in reversed(range(LAYERS)):
        placing, mixing = tables[l]
        grad_out[l] = dispatch_scaled(placing, mixing, upstream)
        grad_hidden[l] = grad_hidden_of(grad_out[l], l)
        gate, up = sums[l][:, :hidden_width], sums[l][:, hidden_width:]
        grads[l] = gather_over_dp(gradients_of(grad_hidden[l], gate, up), groups)
        back = to_experts(dot(grads[l], gate_up[l], (1, 1)).astype(bf16), experts)
        upstream = (upstream.astype(f32) + dot(placing, back, (0, 0))).astype(bf16)

    ends = jnp.stack([upstream.reshape(groups, tokens, part), output.reshape(groups, tokens, part)], axis=1)
    home = swap(ends.reshape(groups * LAYERS, tokens, part), ("dp", "pipe"))
    home = home.reshape(groups, micro, tokens, part).transpose(1, 2, 0, 3).reshape(micro, tokens, width)

    def own_and_other(pair):
        own = jnp.where(first, pair[0], pair[1])
        return own, trade_cores(jnp.where(first, pair[1], pair[0]))

    def weight_grad(left, right):
        return dot(left[0], right[0], (0, 0)) + dot(left[1], right[1], (0, 0))

    both_rows, both_grads = own_and_other(rows), own_and_other(grads)
    both_hidden, both_out = own_and_other(hidden), own_and_other(grad_out)
    grad_gate = weight_grad(both_rows, [g[:, :hidden_width] for g in both_grads])
    grad_up = weight_grad(both_rows, [g[:, hidden_width:] for g in both_grads])
    grad_down = weight_grad(both_hidden, both_out)
    return (
        home[None],
        grad_gate.astype(bf16)[None, None],
        grad_up.astype(bf16)[None, None],
        grad_down.astype(bf16)[None, None],
    )


def solution(mesh):
    tokens = P("pipe", None, ("dp", "expert"), None)
    inner = P("pipe", "expert", "dp", None)
    outer = P("pipe", "expert", None, "dp")
    return jax.shard_map(
        shards,
        mesh=mesh,
        in_specs=(tokens, tokens, tokens, inner, inner, outer),
        out_specs=(tokens, inner, inner, outer),
        check_vma=False,
    )
```

time: 846 us -> 404 us (0.48); the launches traced: 831 us -> 402 us
  waiting for transfers between devices: 450 us -> 164 us
  blocking collectives: 137 us -> 49.7 us
  local copies, waits for them, and re-layouts: 52.6 us -> 10.5 us
  matrix products: 70.2 us -> 53.9 us
  starting transfers between devices: 82.5 us -> 98.1 us
  between operations: 14.6 us -> 1.11 us
    psum x3 -> x0, waiting for transfers between devices: 187 us -> none  [expert_forward(): lax.psum(jnp.dot(rows_in, gate_up, preferred_element_type=jnp.float32).as...]
    all_gather x3 -> x0, waiting for transfers between devices: 96.3 us -> none  [expert_backward(): grads_all = lax.all_gather(grads_own, 'dp', axis=0, tiled=True)]
    all_to_all x5 -> x3, blocking collectives: 137 us -> 49.7 us  [swap(): return lax.all_to_all(values, axes, split_axis=0, concat_axis=0, tiled=True)]
    all_to_all x7 -> x15, waiting for transfers between devices: 87 us -> 164 us  [swap(): return lax.all_to_all(values, axes, split_axis=0, concat_axis=0, tiled=True)]
    reduce_scatter x3 -> x0, waiting for transfers between devices: 62.1 us -> none  [expert_backward(): lax.psum_scatter(lax.dot_general(grad_rows, down_part, (((1,), (1,)), (()...]
    all_to_all x18 -> x0, local copies, waits for them, and re-layouts: 26.9 us -> none  [swap_rows(): lax.all_to_all(rows, ('dp', 'expert'), split_axis=0, concat_axis=0, tiled...]
    ppermute x4 -> x7, waiting for transfers between devices: 18 us -> 0.02 us  [trade_cores(): return lax.ppermute(values, 'pipe', [(0, 1), (1, 0)])]
    dot_general x30 -> x31, matrix products: 70.2 us -> 53.9 us  [the longest x28 49.8 us: dot(): lax.dot_general(a, b, ((contract[:1], contract[1:]), ((), ())), preferred...]
  transfers between devices with their start and end apart: 20 -> 22, of which waited for: 19 -> 13; matrix products, arithmetic and copies ran while one was open for 6% -> 17% of each run, Pallas kernels for 0% -> 0%
where the time goes in v1:
time: 404 us; the launch traced here: 402 us
  waiting for transfers between devices  164 us (41%)
  starting transfers between devices  98.1 us (24%)
  matrix products  53.9 us (13%)
  blocking collectives  49.7 us (12%)
  other arithmetic  24.9 us (6%)
  local copies, waits for them, and re-layouts  10.5 us (3%)
    all_to_all x15, waiting for transfers between devices, swap(): return lax.all_to_all(values, axes, split_axis=0, concat_axis=0, tiled=True)  164 us
    all_to_all x15, starting transfers between devices, swap(): return lax.all_to_all(values, axes, split_axis=0, concat_axis=0, tiled=True)  73.8 us
    dot_general x28, matrix products, dot(): lax.dot_general(a, b, ((contract[:1], contract[1:]), ((), ())), preferred...  49.8 us
    all_to_all x3, blocking collectives, swap(): return lax.all_to_all(values, axes, split_axis=0, concat_axis=0, tiled=True)  49.7 us
    ppermute x7, starting transfers between devices, trade_cores(): return lax.ppermute(values, 'pipe', [(0, 1), (1, 0)])  24.3 us
    select_n x2, other arithmetic, shards(): jnp.where(first, b, a)  8.28 us
  transfers between devices with their start and end apart: 22, of which 13 were waited for; matrix products, arithmetic and copies ran while one was open for 17% of the time, Pallas kernels for 0%

profile of v1, /device:TPU:1, one launch (start us, length us, event | category | flops | bytes accessed | tf_op | source)
XLA Modules:
  0.0 402.1 jit_solution(11616999926207728234)
XLA Ops:
  5.5 10.0 %all-to-all-start = ((bf16[16,32,1024]{2,1,0:T(8,128)(2,1)}), bf16[16,32,1024]{2,1,0:T(8,128)(2,1)S(1)}, u32[]{:S(2)}, u32[]{:S(2)}) async-start(bf16[16,32,1024]{2,1,0:T(8,128)(2,1)} %bitcast.6), calls=%async_computation | async-start | bytes 2097152 | tf_op jit(solution)/shard_map/all_to_all | solution.py:16
  16.0 27.4 %all-to-all-done = bf16[16,32,1024]{2,1,0:T(8,128)(2,1)S(1)} async-done(((bf16[16,32,1024]{2,1,0:T(8,128)(2,1)}), bf16[16,32,1024]{2,1,0:T(8,128)(2,1)S(1)}, u32[]{:S(2)}, u32[]{:S(2)}) %all-to-all-start) | async-done | bytes 1048608 | tf_op jit(solution)/shard_map/all_to_all | solution.py:16
  45.0 6.8 %all-to-all-start.3 = ((bf16[16,16,896]{2,1,0:T(8,128)(2,1)}), bf16[16,16,896]{2,1,0:T(8,128)(2,1)S(1)}, u32[]{:S(2)}, u32[]{:S(2)}) async-start(bf16[16,16,896]{2,1,0:T(8,128)(2,1)} %bitcast.16), calls=%async_computation.3 | async-start | bytes 917504 | tf_op jit(solution)/shard_map/all_to_all | solution.py:16
  51.7 4.1 %broadcast_select_fusion = (bf16[896,1024]{1,0:T(8,128)(2,1)}, bf16[896,1024]{1,0:T(8,128)(2,1)}) fusion(bf16[896,1024]{1,0:T(8,128)(2,1)} %collective-permute-done.2, pred[]{:T(512)S(6)} %eq.140, bf16[1,1,896,1024]{3,2,1,0:T(8,128)(2,1)} %param.10), kind=kLoop, calls=%fused_computation.11 | loop fusion | flops 1835008 | bytes 7340033 | tf_op jit(solution)/shard_map/jit(_where)/select_n | solution.py:94
  55.9 4.2 %broadcast_select_fusion.1 = (bf16[896,1024]{1,0:T(8,128)(2,1)}, bf16[896,1024]{1,0:T(8,128)(2,1)}) fusion(bf16[896,1024]{1,0:T(8,128)(2,1)} %collective-permute-done.1, pred[]{:T(512)S(6)} %eq.140, bf16[1,1,896,1024]{3,2,1,0:T(8,128)(2,1)} %param.9), kind=kLoop, calls=%fused_computation.12 | loop fusion | flops 1835008 | bytes 7340033 | tf_op jit(solution)/shard_map/jit(_where)/select_n | solution.py:94
  60.0 2.4 all-to-all-done.3
  62.4 4.3 %convolution_convert_fusion.1 = bf16[256,2048]{1,0:T(8,128)(2,1)} fusion(bf16[256,896]{1,0:T(8,128)(2,1)S(1)} %bitcast.136, bf16[896,1024]{1,0:T(8,128)(2,1)} %get-tuple-element.7, bf16[896,1024]{1,0:T(8,128)(2,1)} %get-tuple-element.5), kind=kOutput, calls=%fused_computation.6 | convolution fusion | flops 947388416 | bytes 5177344 | tf_op jit(solution)/shard_map/dot_general | solution.py:24
  66.7 3.6 all-to-all-start.4
  71.4 28.0 %all-to-all-done.4 = bf16[8,32,2048]{2,1,0:T(8,128)(2,1)S(1)} async-done(((bf16[8,32,2048]{2,1,0:T(8,128)(2,1)}), bf16[8,32,2048]{2,1,0:T(8,128)(2,1)S(1)}, u32[]{:S(2)}, u32[]{:S(2)}) %all-to-all-start.4) | async-done | bytes 1048608 | tf_op jit(solution)/shard_map/all_to_all | solution.py:16
  100.4 3.5 all-to-all-start.5
  106.5 15.4 %all-to-all-done.5 = bf16[8,32,1024]{2,1,0:T(8,128)(2,1)S(1)} async-done(((bf16[8,32,1024]{2,1,0:T(8,128)(2,1)}), bf16[8,32,1024]{2,1,0:T(8,128)(2,1)S(1)}, u32[]{:S(2)}, u32[]{:S(2)}) %all-to-all-start.5) | async-done | bytes 524320 | tf_op jit(solution)/shard_map/all_to_all | solution.py:16
  121.8 3.6 convolution_convert_fusion.6
  125.4 4.3 %all-to-all-start.6 = ((bf16[16,16,896]{2,1,0:T(8,128)(2,1)}), bf16[16,16,896]{2,1,0:T(8,128)(2,1)S(1)}, u32[]{:S(2)}, u32[]{:S(2)}) async-start(bf16[16,16,896]{2,1,0:T(8,128)(2,1)} %bitcast.177), calls=%async_computation.6 | async-start | bytes 917504 | tf_op jit(solution)/shard_map/all_to_all | solution.py:16
  131.8 8.4 %all-to-all-done.6 = bf16[16,16,896]{2,1,0:T(8,128)(2,1)S(1)} async-done(((bf16[16,16,896]{2,1,0:T(8,128)(2,1)}), bf16[16,16,896]{2,1,0:T(8,128)(2,1)S(1)}, u32[]{:S(2)}, u32[]{:S(2)}) %all-to-all-start.6) | async-done | bytes 458784 | tf_op jit(solution)/shard_map/all_to_all | solution.py:16
  140.2 3.6 all-to-all-start.1
  146.5 6.7 %all-to-all-done.1 = bf16[16,16,896]{2,1,0:T(8,128)(2,1)S(1)} async-done(((bf16[16,16,896]{2,1,0:T(8,128)(2,1)}), bf16[16,16,896]{2,1,0:T(8,128)(2,1)S(1)}, u32[]{:S(2)}, u32[]{:S(2)}) %all-to-all-start.1) | async-done | bytes 458784 | tf_op jit(solution)/shard_map/all_to_all | solution.py:16
  153.2 3.6 all-to-all-start.7
  156.8 3.1 convolution_convert_fusion.3
  159.8 5.8 %all-to-all-done.7 = bf16[16,16,896]{2,1,0:T(8,128)(2,1)S(1)} async-done(((bf16[16,16,896]{2,1,0:T(8,128)(2,1)}), bf16[16,16,896]{2,1,0:T(8,128)(2,1)S(1)}, u32[]{:S(2)}, u32[]{:S(2)}) %all-to-all-start.7) | async-done | bytes 458784 | tf_op jit(solution)/shard_map/all_to_all | solution.py:16
  165.6 3.5 all-to-all-start.2
  169.1 4.3 %convolution_convert_fusion = bf16[256,2048]{1,0:T(8,128)(2,1)} fusion(bf16[256,896]{1,0:T(8,128)(2,1)S(1)} %bitcast.139, bf16[896,1024]{1,0:T(8,128)(2,1)} %get-tuple-element.6, bf16[896,1024]{1,0:T(8,128)(2,1)} %get-tuple-element.4), kind=kOutput, calls=%fused_computation.5 | convolution fusion | flops 947388416 | bytes 5177344 | tf_op jit(solution)/shard_map/dot_general | solution.py:24
  173.4 9.9 %all-to-all-done.2 = bf16[8,32,1024]{2,1,0:T(8,128)(2,1)S(1)} async-done(((bf16[8,32,1024]{2,1,0:T(8,128)(2,1)}), bf16[8,32,1024]{2,1,0:T(8,128)(2,1)S(1)}, u32[]{:S(2)}, u32[]{:S(2)}) %all-to-all-start.2) | async-done | bytes 524320 | tf_op jit(solution)/shard_map/all_to_all | solution.py:16
  184.1 3.6 all-to-all-start.8
  189.5 23.8 %all-to-all-done.8 = bf16[8,32,2048]{2,1,0:T(8,128)(2,1)S(1)} async-done(((bf16[8,32,2048]{2,1,0:T(8,128)(2,1)}), bf16[8,32,2048]{2,1,0:T(8,128)(2,1)S(1)}, u32[]{:S(2)}, u32[]{:S(2)}) %all-to-all-start.8) | async-done | bytes 1048608 | tf_op jit(solution)/shard_map/all_to_all | solution.py:16
  214.7 26.6 %all_to_all.90 = bf16[8,32,2048]{2,1,0:T(8,128)(2,1)S(1)} all-to-all(bf16[8,32,2048]{2,1,0:T(8,128)(2,1)S(1)} %broadcast_in_dim.43), channel_id=1, replica_groups=mesh['dp'=8,'expert'=16,'pipe'=2] {'dp'}, dimensions={0} | all-to-all | bytes 2097152 | tf_op jit(solution)/shard_map/all_to_all | solution.py:16
  242.6 11.2 %all_to_all.91 = bf16[16,16,896]{2,1,0:T(8,128)(2,1)S(1)} all-to-all(bf16[16,16,896]{2,1,0:T(8,128)(2,1)S(1)} %bitcast.178), channel_id=1, replica_groups=mesh['dp'=8,'expert'=16,'pipe'=2] {'expert'}, dimensions={0} | all-to-all | bytes 917504 | tf_op jit(solution)/shard_map/all_to_all | solution.py:16
  255.3 11.9 %all_to_all.92 = bf16[16,16,896]{2,1,0:T(8,128)(2,1)} all-to-all(bf16[16,16,896]{2,1,0:T(8,128)(2,1)S(1)} %bitcast.160), channel_id=1, replica_groups=mesh['dp'=8,'expert'=16,'pipe'=2] {'expert'}, dimensions={0} | all-to-all | bytes 917504 | tf_op jit(solution)/shard_map/all_to_all | solution.py:16
  268.0 3.9 all-to-all-start.15
  272.0 3.8 convolution_convert_fusion.2
  275.7 8.5 %all-to-all-done.15 = bf16[8,32,1024]{2,1,0:T(8,128)(2,1)S(1)} async-done(((bf16[8,32,1024]{2,1,0:T(8,128)(2,1)}), bf16[8,32,1024]{2,1,0:T(8,128)(2,1)S(1)}, u32[]{:S(2)}, u32[]{:S(2)}) %all-to-all-start.15) | async-done | bytes 524320 | tf_op jit(solution)/shard_map/all_to_all | solution.py:16
  284.2 4.1 %all-to-all-start.12 = ((bf16[8,32,1024]{2,1,0:T(8,128)(2,1)}), bf16[8,32,1024]{2,1,0:T(8,128)(2,1)}, u32[]{:S(2)}, u32[]{:S(2)}) async-start(bf16[8,32,1024]{2,1,0:T(8,128)(2,1)} %bitcast.175), calls=%async_computation.12 | async-start | bytes 1048576 | tf_op jit(solution)/shard_map/all_to_all | solution.py:16
  288.4 3.0 convolution_convert_fusion.4
  291.4 9.1 %all-to-all-done.12 = bf16[8,32,1024]{2,1,0:T(8,128)(2,1)} async-done(((bf16[8,32,1024]{2,1,0:T(8,128)(2,1)}), bf16[8,32,1024]{2,1,0:T(8,128)(2,1)}, u32[]{:S(2)}, u32[]{:S(2)}) %all-to-all-start.12) | async-done | bytes 524320 | tf_op jit(solution)/shard_map/all_to_all | solution.py:16
  300.5 4.2 %all-to-all-start.16 = ((bf16[16,16,896]{2,1,0:T(8,128)(2,1)}), bf16[16,16,896]{2,1,0:T(8,128)(2,1)}, u32[]{:S(2)}, u32[]{:S(2)}) async-start(bf16[16,16,896]{2,1,0:T(8,128)(2,1)} %bitcast.176), calls=%async_computation.16 | async-start | bytes 917504 | tf_op jit(solution)/shard_map/all_to_all | solution.py:16
  307.6 5.8 %all-to-all-done.16 = bf16[16,16,896]{2,1,0:T(8,128)(2,1)} async-done(((bf16[16,16,896]{2,1,0:T(8,128)(2,1)}), bf16[16,16,896]{2,1,0:T(8,128)(2,1)}, u32[]{:S(2)}, u32[]{:S(2)}) %all-to-all-start.16) | async-done | bytes 458784 | tf_op jit(solution)/shard_map/all_to_all | solution.py:16
  315.3 4.3 %all-to-all-start.13 = ((bf16[8,32,2048]{2,1,0:T(8,128)(2,1)}), bf16[8,32,2048]{2,1,0:T(8,128)(2,1)}, u32[]{:S(2)}, u32[]{:S(2)}) async-start(bf16[8,32,2048]{2,1,0:T(8,128)(2,1)} %broadcast_in_dim.44), calls=%async_computation.13 | async-start | bytes 2097152 | tf_op jit(solution)/shard_map/all_to_all | solution.py:16
  320.5 10.1 %collective-permute-start.3 = (bf16[256,896]{1,0:T(8,128)(2,1)}, bf16[256,896]{1,0:T(8,128)(2,1)}, u32[]{:S(2)}, u32[]{:S(2)}) collective-permute-start(bf16[256,896]{1,0:T(8,128)(2,1)} %broadcast_select_fusion.16), channel_id=1, source_target_pairs={{0,1},{1,0},{2,3},{3,2},{4,5},{5,4},{6,7},{7,6},{8,9},{9,8},{10,11... | collective-permute-start | bytes 1376264 | tf_op jit(solution)/shard_map/ppermute | solution.py:20
  332.3 2.4 fusion.10
  337.0 4.4 %fusion.11 = bf16[256,896]{1,0:T(8,128)(2,1)} fusion(bf16[256,2048]{1,0:T(8,128)(2,1)} %bitcast.33, bf16[896,1024]{1,0:T(8,128)(2,1)} %get-tuple-element.7, bf16[896,1024]{1,0:T(8,128)(2,1)} %get-tuple-element.5), kind=kOutput, calls=%fused_computation.38 | convolution fusion | flops 947093504 | bytes 5177344 | tf_op jit(solution)/shard_map/dot_general | solution.py:24
  341.4 4.2 %all-to-all-start.14 = ((bf16[16,16,896]{2,1,0:T(8,128)(2,1)}), bf16[16,16,896]{2,1,0:T(8,128)(2,1)}, u32[]{:S(2)}, u32[]{:S(2)}) async-start(bf16[16,16,896]{2,1,0:T(8,128)(2,1)} %bitcast.34), calls=%async_computation.14 | async-start | bytes 917504 | tf_op jit(solution)/shard_map/all_to_all | solution.py:16
  345.7 2.4 broadcast_select_fusion.6
  348.0 12.6 %collective-permute-start.4 = (bf16[256,2048]{1,0:T(8,128)(2,1)}, bf16[256,2048]{1,0:T(8,128)(2,1)}, u32[]{:S(2)}, u32[]{:S(2)}) collective-permute-start(bf16[256,2048]{1,0:T(8,128)(2,1)} %get-tuple-element.8), channel_id=1, source_target_pairs={{0,1},{1,0},{2,3},{3,2},{4,5},{5,4},{6,7},{7,6},{8,9},{9,8},{10,11... | collective-permute-start | bytes 3145736 | tf_op jit(solution)/shard_map/ppermute | solution.py:20
  362.0 2.1 pad_maximum_fusion.11
  364.1 10.8 %all-to-all-start.17 = ((bf16[16,32,896]{2,1,0:T(8,128)(2,1)}), bf16[16,32,896]{2,1,0:T(8,128)(2,1)S(1)}, u32[]{:S(2)}, u32[]{:S(2)}) async-start(bf16[16,32,896]{2,1,0:T(8,128)(2,1)} %bitcast.154), calls=%async_computation.17 | async-start | bytes 1835008 | tf_op jit(solution)/shard_map/all_to_all | solution.py:16
  376.7 3.2 fusion.4
  381.3 3.1 fusion.2
  384.3 3.1 fusion.3
  387.4 12.8 %all-to-all-done.17 = bf16[16,32,896]{2,1,0:T(8,128)(2,1)S(1)} async-done(((bf16[16,32,896]{2,1,0:T(8,128)(2,1)}), bf16[16,32,896]{2,1,0:T(8,128)(2,1)S(1)}, u32[]{:S(2)}, u32[]{:S(2)}) %all-to-all-start.17) | async-done | bytes 917536 | tf_op jit(solution)/shard_map/all_to_all | solution.py:16
  (99 shorter events, 40.0 us)
Async XLA Ops:
  5.5 37.9 %all-to-all-start = ((bf16[16,32,1024]{2,1,0:T(8,128)(2,1)}), bf16[16,32,1024]{2,1,0:T(8,128)(2,1)S(1)}, u32[]{:S(2)}, u32[]{:S(2)}) async-start(bf16[16,32,1024]{2,1,0:T(8,128)(2,1)} %bitcast.6), calls=%async_computation | async-start | bytes 2097152 | tf_op jit(solution)/shard_map/all_to_all | solution.py:16
  15.5 36.2 %collective-permute-start.2 = (bf16[896,1024]{1,0:T(8,128)(2,1)}, bf16[896,1024]{1,0:T(8,128)(2,1)}, u32[]{:S(2)}, u32[]{:S(2)}) collective-permute-start(bf16[896,1024]{1,0:T(8,128)(2,1)} %bitcast.19), channel_id=1, source_target_pairs={{0,1},{1,0},{2,3},{3,2},{4,5},{5,4},{6,7},{7,6},{8,9},{9,8},{10,11... | collective-permute-start | bytes 5505032 | tf_op jit(solution)/shard_map/ppermute | solution.py:20
  15.7 40.2 %collective-permute-start.1 = (bf16[896,1024]{1,0:T(8,128)(2,1)}, bf16[896,1024]{1,0:T(8,128)(2,1)}, u32[]{:S(2)}, u32[]{:S(2)}) collective-permute-start(bf16[896,1024]{1,0:T(8,128)(2,1)} %bitcast.18), channel_id=1, source_target_pairs={{0,1},{1,0},{2,3},{3,2},{4,5},{5,4},{6,7},{7,6},{8,9},{9,8},{10,11... | collective-permute-start | bytes 5505032 | tf_op jit(solution)/shard_map/ppermute | solution.py:20
  43.7 210.4 %copy-start.12 = (pred[256,256]{0,1:T(32,128)(4,1)}, pred[256,256]{0,1:T(32,128)(4,1)S(1)}, u32[]{:S(2)}) copy-start(pred[256,256]{0,1:T(32,128)(4,1)S(1)} %fusion.16) | copy-start | bytes 196612
  45.0 17.4 %all-to-all-start.3 = ((bf16[16,16,896]{2,1,0:T(8,128)(2,1)}), bf16[16,16,896]{2,1,0:T(8,128)(2,1)S(1)}, u32[]{:S(2)}, u32[]{:S(2)}) async-start(bf16[16,16,896]{2,1,0:T(8,128)(2,1)} %bitcast.16), calls=%async_computation.3 | async-start | bytes 917504 | tf_op jit(solution)/shard_map/all_to_all | solution.py:16
  66.7 32.7 %all-to-all-start.4 = ((bf16[8,32,2048]{2,1,0:T(8,128)(2,1)}), bf16[8,32,2048]{2,1,0:T(8,128)(2,1)S(1)}, u32[]{:S(2)}, u32[]{:S(2)}) async-start(bf16[8,32,2048]{2,1,0:T(8,128)(2,1)} %bitcast.171), calls=%async_computation.4 | async-start | bytes 2097152 | tf_op jit(solution)/shard_map/all_to_all | solution.py:16
  70.2 36.2 %collective-permute-start = (bf16[1024,896]{1,0:T(8,128)(2,1)}, bf16[1024,896]{1,0:T(8,128)(2,1)}, u32[]{:S(2)}, u32[]{:S(2)}) collective-permute-start(bf16[1024,896]{1,0:T(8,128)(2,1)} %bitcast.182), channel_id=1, source_target_pairs={{0,1},{1,0},{2,3},{3,2},{4,5},{5,4},{6,7},{7,6},{8,9},{9,8},{10,11... | collective-permute-start | bytes 5505032 | tf_op jit(solution)/shard_map/ppermute | solution.py:20
  99.5 31.2 %copy-start.5 = (f32[32,2048]{1,0:T(8,128)}, f32[32,2048]{1,0:T(8,128)S(1)}, u32[]{:S(2)}) copy-start(f32[32,2048]{1,0:T(8,128)S(1)} %convert_reduce_fusion.1) | copy-start | bytes 786436
  100.4 21.4 %all-to-all-start.5 = ((bf16[8,32,1024]{2,1,0:T(8,128)(2,1)}), bf16[8,32,1024]{2,1,0:T(8,128)(2,1)S(1)}, u32[]{:S(2)}, u32[]{:S(2)}) async-start(bf16[8,32,1024]{2,1,0:T(8,128)(2,1)} %broadcast_in_dim.42), calls=%async_computation.5 | async-start | bytes 1048576 | tf_op jit(solution)/shard_map/all_to_all | solution.py:16
  104.2 41.1 %copy-start.13 = (pred[256,256]{0,1:T(32,128)(4,1)}, pred[256,256]{0,1:T(32,128)(4,1)S(1)}, u32[]{:S(2)}) copy-start(pred[256,256]{0,1:T(32,128)(4,1)S(1)} %fusion.15) | copy-start | bytes 196612
  121.8 7.9 %copy-start.11 = (f32[256,256]{0,1:T(8,128)S(1)}, f32[256,256]{0,1:T(8,128)}, u32[]{:S(2)}) copy-start(f32[256,256]{0,1:T(8,128)} %convolution_add_fusion.7) | copy-start | bytes 786436
  125.4 14.8 %all-to-all-start.6 = ((bf16[16,16,896]{2,1,0:T(8,128)(2,1)}), bf16[16,16,896]{2,1,0:T(8,128)(2,1)S(1)}, u32[]{:S(2)}, u32[]{:S(2)}) async-start(bf16[16,16,896]{2,1,0:T(8,128)(2,1)} %bitcast.177), calls=%async_computation.6 | async-start | bytes 917504 | tf_op jit(solution)/shard_map/all_to_all | solution.py:16
  140.2 13.0 %all-to-all-start.1 = ((bf16[16,16,896]{2,1,0:T(8,128)(2,1)}), bf16[16,16,896]{2,1,0:T(8,128)(2,1)S(1)}, u32[]{:S(2)}, u32[]{:S(2)}) async-start(bf16[16,16,896]{2,1,0:T(8,128)(2,1)} %bitcast.10), calls=%async_computation.1 | async-start | bytes 917504 | tf_op jit(solution)/shard_map/all_to_all | solution.py:16
  145.3 14.5 %copy-start.3 = (bf16[256,896]{1,0:T(8,128)(2,1)}, bf16[256,896]{1,0:T(8,128)(2,1)S(1)}, u32[]{:S(2)}) copy-start(bf16[256,896]{1,0:T(8,128)(2,1)S(1)} %fusion.9) | copy-start | bytes 1376260
  153.2 12.4 %all-to-all-start.7 = ((bf16[16,16,896]{2,1,0:T(8,128)(2,1)}), bf16[16,16,896]{2,1,0:T(8,128)(2,1)S(1)}, u32[]{:S(2)}, u32[]{:S(2)}) async-start(bf16[16,16,896]{2,1,0:T(8,128)(2,1)} %bitcast.24), calls=%async_computation.7 | async-start | bytes 917504 | tf_op jit(solution)/shard_map/all_to_all | solution.py:16
  165.6 17.7 %all-to-all-start.2 = ((bf16[8,32,1024]{2,1,0:T(8,128)(2,1)}), bf16[8,32,1024]{2,1,0:T(8,128)(2,1)S(1)}, u32[]{:S(2)}, u32[]{:S(2)}) async-start(bf16[8,32,1024]{2,1,0:T(8,128)(2,1)} %bitcast.174), calls=%async_computation.2 | async-start | bytes 1048576 | tf_op jit(solution)/shard_map/all_to_all | solution.py:16
  183.3 0.8 copy-start.7
  184.1 29.1 %all-to-all-start.8 = ((bf16[8,32,2048]{2,1,0:T(8,128)(2,1)}), bf16[8,32,2048]{2,1,0:T(8,128)(2,1)S(1)}, u32[]{:S(2)}, u32[]{:S(2)}) async-start(bf16[8,32,2048]{2,1,0:T(8,128)(2,1)} %bitcast.172), calls=%async_computation.8 | async-start | bytes 2097152 | tf_op jit(solution)/shard_map/all_to_all | solution.py:16
  213.4 27.9 %copy-start.9 = (bf16[896,1024]{1,0:T(8,128)(2,1)S(1)}, bf16[896,1024]{1,0:T(8,128)(2,1)}, u32[]{:S(2)}) copy-start(bf16[896,1024]{1,0:T(8,128)(2,1)} %get-tuple-element.4) | copy-start | bytes 5505028
  214.5 26.8 %copy-start.8 = (bf16[896,1024]{1,0:T(8,128)(2,1)S(1)}, bf16[896,1024]{1,0:T(8,128)(2,1)}, u32[]{:S(2)}) copy-start(bf16[896,1024]{1,0:T(8,128)(2,1)} %get-tuple-element.6) | copy-start | bytes 5505028
  241.3 12.5 %copy-start.14 = (pred[256,256]{0,1:T(32,128)(4,1)S(1)}, pred[256,256]{0,1:T(32,128)(4,1)}, u32[]{:S(2)}) copy-start(pred[256,256]{0,1:T(32,128)(4,1)} %copy-done.13) | copy-start | bytes 196612
  254.1 0.8 copy-start
  268.0 16.2 %all-to-all-start.15 = ((bf16[8,32,1024]{2,1,0:T(8,128)(2,1)}), bf16[8,32,1024]{2,1,0:T(8,128)(2,1)S(1)}, u32[]{:S(2)}, u32[]{:S(2)}) async-start(bf16[8,32,1024]{2,1,0:T(8,128)(2,1)} %broadcast_in_dim.45), calls=%async_computation.15 | async-start | bytes 1048576 | tf_op jit(solution)/shard_map/all_to_all | solution.py:16
  284.2 16.3 %all-to-all-start.12 = ((bf16[8,32,1024]{2,1,0:T(8,128)(2,1)}), bf16[8,32,1024]{2,1,0:T(8,128)(2,1)}, u32[]{:S(2)}, u32[]{:S(2)}) async-start(bf16[8,32,1024]{2,1,0:T(8,128)(2,1)} %bitcast.175), calls=%async_computation.12 | async-start | bytes 1048576 | tf_op jit(solution)/shard_map/all_to_all | solution.py:16
  300.5 12.8 %all-to-all-start.16 = ((bf16[16,16,896]{2,1,0:T(8,128)(2,1)}), bf16[16,16,896]{2,1,0:T(8,128)(2,1)}, u32[]{:S(2)}, u32[]{:S(2)}) async-start(bf16[16,16,896]{2,1,0:T(8,128)(2,1)} %bitcast.176), calls=%async_computation.16 | async-start | bytes 917504 | tf_op jit(solution)/shard_map/all_to_all | solution.py:16
  315.3 21.7 %all-to-all-start.13 = ((bf16[8,32,2048]{2,1,0:T(8,128)(2,1)}), bf16[8,32,2048]{2,1,0:T(8,128)(2,1)}, u32[]{:S(2)}, u32[]{:S(2)}) async-start(bf16[8,32,2048]{2,1,0:T(8,128)(2,1)} %broadcast_in_dim.44), calls=%async_computation.13 | async-start | bytes 2097152 | tf_op jit(solution)/shard_map/all_to_all | solution.py:16
  320.5 11.8 %copy-start.4 = (bf16[256,896]{1,0:T(8,128)(2,1)S(1)}, bf16[256,896]{1,0:T(8,128)(2,1)}, u32[]{:S(2)}) copy-start(bf16[256,896]{1,0:T(8,128)(2,1)} %copy-done.3) | copy-start | bytes 1376260
  320.5 11.8 %copy-start.10 = (f32[256,256]{0,1:T(8,128)S(1)}, f32[256,256]{0,1:T(8,128)}, u32[]{:S(2)}) copy-start(f32[256,256]{0,1:T(8,128)} %get-tuple-element.23) | copy-start | bytes 786436
  320.5 60.7 %collective-permute-start.3 = (bf16[256,896]{1,0:T(8,128)(2,1)}, bf16[256,896]{1,0:T(8,128)(2,1)}, u32[]{:S(2)}, u32[]{:S(2)}) collective-permute-start(bf16[256,896]{1,0:T(8,128)(2,1)} %broadcast_select_fusion.16), channel_id=1, source_target_pairs={{0,1},{1,0},{2,3},{3,2},{4,5},{5,4},{6,7},{7,6},{8,9},{9,8},{10,11... | collective-permute-start | bytes 1376264 | tf_op jit(solution)/shard_map/ppermute | solution.py:20
  331.5 3.3 copy-start.2
  331.5 45.2 %collective-permute-start.5 = (bf16[256,1024]{1,0:T(8,128)(2,1)}, bf16[256,1024]{1,0:T(8,128)(2,1)}, u32[]{:S(2)}, u32[]{:S(2)}) collective-permute-start(bf16[256,1024]{1,0:T(8,128)(2,1)} %broadcast_select_fusion.12), channel_id=1, source_target_pairs={{0,1},{1,0},{2,3},{3,2},{4,5},{5,4},{6,7},{7,6},{8,9},{9,8},{10,11... | collective-permute-start | bytes 1572872 | tf_op jit(solution)/shard_map/ppermute | solution.py:20
  335.6 41.0 %collective-permute-start.6 = (bf16[256,896]{1,0:T(8,128)(2,1)}, bf16[256,896]{1,0:T(8,128)(2,1)}, u32[]{:S(2)}, u32[]{:S(2)}) collective-permute-start(bf16[256,896]{1,0:T(8,128)(2,1)} %broadcast_select_fusion.15), channel_id=1, source_target_pairs={{0,1},{1,0},{2,3},{3,2},{4,5},{5,4},{6,7},{7,6},{8,9},{9,8},{10,11... | collective-permute-start | bytes 1376264 | tf_op jit(solution)/shard_map/ppermute | solution.py:20
  341.4 19.2 %all-to-all-start.14 = ((bf16[16,16,896]{2,1,0:T(8,128)(2,1)}), bf16[16,16,896]{2,1,0:T(8,128)(2,1)}, u32[]{:S(2)}, u32[]{:S(2)}) async-start(bf16[16,16,896]{2,1,0:T(8,128)(2,1)} %bitcast.34), calls=%async_computation.14 | async-start | bytes 917504 | tf_op jit(solution)/shard_map/all_to_all | solution.py:16
  345.6 15.0 %copy-start.1 = (bf16[256,896]{1,0:T(8,128)(2,1)S(1)}, bf16[256,896]{1,0:T(8,128)(2,1)}, u32[]{:S(2)}) copy-start(bf16[256,896]{1,0:T(8,128)(2,1)} %copy-done) | copy-start | bytes 1376260
  348.0 33.2 %collective-permute-start.4 = (bf16[256,2048]{1,0:T(8,128)(2,1)}, bf16[256,2048]{1,0:T(8,128)(2,1)}, u32[]{:S(2)}, u32[]{:S(2)}) collective-permute-start(bf16[256,2048]{1,0:T(8,128)(2,1)} %get-tuple-element.8), channel_id=1, source_target_pairs={{0,1},{1,0},{2,3},{3,2},{4,5},{5,4},{6,7},{7,6},{8,9},{9,8},{10,11... | collective-permute-start | bytes 3145736 | tf_op jit(solution)/shard_map/ppermute | solution.py:20
  362.0 12.9 %copy-start.6 = (bf16[8,32,1024]{2,1,0:T(8,128)(2,1)S(1)}, bf16[8,32,1024]{2,1,0:T(8,128)(2,1)}, u32[]{:S(2)}) copy-start(bf16[8,32,1024]{2,1,0:T(8,128)(2,1)} %broadcast_select_fusion.13) | copy-start | bytes 1572868
  364.1 36.1 %all-to-all-start.17 = ((bf16[16,32,896]{2,1,0:T(8,128)(2,1)}), bf16[16,32,896]{2,1,0:T(8,128)(2,1)S(1)}, u32[]{:S(2)}, u32[]{:S(2)}) async-start(bf16[16,32,896]{2,1,0:T(8,128)(2,1)} %bitcast.154), calls=%async_computation.17 | async-start | bytes 1835008 | tf_op jit(solution)/shard_map/all_to_all | solution.py:16

commit v2 on v1

--- a/solution.py
+++ b/solution.py
@@ -1,6 +1,10 @@
+import functools
+
 import jax
 import jax.numpy as jnp
 from jax import lax
+from jax.experimental import pallas as pl
+from jax.experimental.pallas import tpu as pltpu
 from jax.sharding import PartitionSpec as P
 
 CAPACITY = 2
@@ -10,6 +14,7 @@
 highest = lax.Precision.HIGHEST
 bf16 = jnp.bfloat16
 f32 = jnp.float32
+i32 = jnp.int32
 
 
 def swap(values, axes):
@@ -24,20 +29,51 @@
     return lax.dot_general(a, b, ((contract[:1], contract[1:]), ((), ())), preferred_element_type=f32)
 
 
-def route_columns(ids, weights, experts):
-    tokens = ids.shape[1]
-    hit = ids[..., None] == jnp.arange(experts, dtype=jnp.int32)
-    chosen = jnp.any(hit, axis=2).astype(f32)
-    weight = jnp.sum(jnp.where(hit, weights[..., None], 0.0), axis=2)
-    earlier = (jnp.arange(tokens)[:, None] > jnp.arange(tokens)[None, :]).astype(f32)
-    before = jnp.einsum("ts,mse->mte", earlier, chosen)
-    code = jnp.where((chosen > 0) & (before < CAPACITY), before + 1.0, 0.0)
-    high = lax.reduce_precision(weight, 8, 7)
-    rest = weight - high
-    middle = lax.reduce_precision(rest, 8, 7)
-    low = rest - middle
-    columns = jnp.concatenate([code, high, middle, low], axis=-1).astype(bf16)
-    return jnp.pad(columns, ((0, 0), (0, 0), (0, ROUTE_COLUMNS - columns.shape[-1])))
+def local(body, dims, operands, name):
+    return pl.pallas_call(
+        body,
+        out_shape=jax.ShapeDtypeStruct(dims, bf16),
+        compiler_params=pltpu.CompilerParams(vmem_limit_bytes=32 * 1024 * 1024),
+        name=name,
+    )(*operands)
+
+
+def exact_parts(values):
+    high = values.astype(bf16)
+    rest = values - high.astype(f32)
+    middle = rest.astype(bf16)
+    return high, middle, (rest - middle.astype(f32)).astype(bf16)
+
+
+def pack_body(experts, groups, io, ids, weights, sent):
+    micro, tokens, width = io.shape
+    part = width // groups
+    column = lax.broadcasted_iota(i32, (tokens, ROUTE_COLUMNS), 1)
+    expert, kind = column % experts, column // experts
+    later = lax.broadcasted_iota(i32, (tokens, tokens), 0)
+    earlier = (lax.broadcasted_iota(i32, (tokens, tokens), 1) < later).astype(f32).astype(bf16)
+    for m in range(micro):
+        chosen = jnp.zeros((tokens, ROUTE_COLUMNS), f32)
+        weight = jnp.zeros((tokens, ROUTE_COLUMNS), f32)
+        for k in range(ids.shape[2]):
+            hit = ids[m, :, k : k + 1] == expert
+            chosen = jnp.where(hit, 1.0, chosen)
+            weight = jnp.where(hit, weights[m, :, k : k + 1], weight)
+        before = dot(earlier, chosen.astype(bf16), (1, 0))
+        code = jnp.where((chosen > 0.0) & (before < CAPACITY), before + 1.0, 0.0)
+        high, middle, low = [piece.astype(f32) for piece in exact_parts(weight)]
+        values = jnp.where(kind == 0, code, jnp.where(kind == 1, high, jnp.where(kind == 2, middle, low)))
+        values = jnp.where(kind < 4, values, 0.0).astype(bf16)
+        for d in range(groups):
+            sent[d, m, :, :part] = io[m, :, d * part : (d + 1) * part]
+            sent[d, m, :, part:] = values
+
+
+def home_body(moved, out):
+    groups, micro, tokens, part = moved.shape
+    for d in range(groups):
+        for m in range(micro):
+            out[m, :, d * part : (d + 1) * part] = moved[d, m]
 
 
 def routing(columns, groups, experts):
@@ -67,6 +103,19 @@
     return moved.reshape(groups * own.shape[0], own.shape[1])
 
 
+def gather_and_sum(own, partial, groups):
+    width = own.shape[1]
+    copies = jnp.broadcast_to(own[None], (groups,) + own.shape)
+    pieces = partial.reshape(groups, partial.shape[0] // groups, partial.shape[1])
+    moved = swap(jnp.concatenate([copies, pieces], axis=2), "dp")
+    gathered = moved[:, :, :width].reshape(groups * own.shape[0], width)
+    return gathered, jnp.sum(moved[:, :, width:].astype(f32), axis=0)
+
+
+def follow(values, earlier):
+    return lax.optimization_barrier((values, earlier[:1, :1]))[0]
+
+
 def to_experts(rows, experts):
     moved = swap(rows.reshape(experts, rows.shape[0] // experts, rows.shape[1]), "expert")
     return moved.reshape(rows.shape)
@@ -96,12 +145,15 @@
     gate_up = [jnp.concatenate(w[:2], axis=1) for w in layer_weights]
     down = [w[2] for w in layer_weights]
 
-    columns = route_columns(route_ids[0], route_weights[0], experts)
-    pieces = layer_io[0].reshape(micro, tokens, groups, part).transpose(2, 0, 1, 3)
-    columns = jnp.broadcast_to(columns[None], (groups,) + columns.shape)
-    sent = jnp.concatenate([pieces, columns], axis=3)
+    sent = local(
+        functools.partial(pack_body, experts, groups),
+        (groups, micro, tokens, part + ROUTE_COLUMNS),
+        (layer_io[0], route_ids[0], route_weights[0]),
+        "pack",
+    )
     got = swap(sent.reshape(groups * micro, tokens, part + ROUTE_COLUMNS), ("dp", "pipe"))
     got = got.reshape(groups, LAYERS, tokens, part + ROUTE_COLUMNS)
+    got, gate_up, down = lax.optimization_barrier((got, gate_up, down))
     inputs = got[:, 0, :, :part].reshape(groups * tokens, part)
     cotangent = got[:, 1, :, :part].reshape(groups * tokens, part)
     tables = [
@@ -109,46 +161,62 @@
         for l in range(LAYERS)
     ]
 
-    def dispatch(placing, values):
-        return to_experts(dot(placing, values, (1, 0)).astype(bf16), experts)
-
-    def dispatch_scaled(placing, mixing, values):
-        scale = jnp.sum(mixing, axis=1, keepdims=True)
-        return to_experts((dot(placing, values, (1, 0)) * scale).astype(bf16), experts)
-
-    def grad_hidden_of(grad_out, l):
-        return sum_over_dp(dot(grad_out, down[l], (1, 1)).astype(bf16), groups)
-
-    current = inputs
-    rows, sums, hidden = [], [], []
-    grad_out, grad_hidden = [None] * LAYERS, [None] * LAYERS
-    for l in range(LAYERS):
-        placing, mixing = tables[l]
-        rows.append(dispatch(placing, current))
-        sums.append(sum_over_dp(dot(rows[l], gate_up[l], (1, 0)).astype(bf16), groups))
-        gate, up = sums[l][:, :hidden_width], sums[l][:, hidden_width:]
-        hidden.append(gather_over_dp((jax.nn.silu(gate) * up).astype(bf16), groups))
-        result = to_experts(dot(hidden[l], down[l], (1, 0)).astype(bf16), experts)
+    scales = [jnp.sum(mixing, axis=1, keepdims=True) for _, mixing in tables]
+
+    def two_to_experts(left, right):
+        shape = (experts, left.shape[0] // experts, part)
+        moved = swap(jnp.concatenate([left.reshape(shape), right.reshape(shape)], axis=1), "expert")
+        return [half.reshape(left.shape) for half in jnp.split(moved, 2, axis=1)]
+
+    def placed(l, values):
+        return dot(tables[l][0], values, (1, 0))
+
+    def mixed_in(l, values, result):
         mixed = lax.dot_general(
-            mixing, result.astype(f32), (((0,), (0,)), ((), ())), precision=highest
+            tables[l][1], result.astype(f32), (((0,), (0,)), ((), ())), precision=highest
         )
-        current = (current.astype(f32) + mixed).astype(bf16)
-    output = current
-
-    upstream = cotangent
-    grads = [None] * LAYERS
-    for l in reversed(range(LAYERS)):
-        placing, mixing = tables[l]
-        grad_out[l] = dispatch_scaled(placing, mixing, upstream)
-        grad_hidden[l] = grad_hidden_of(grad_out[l], l)
-        gate, up = sums[l][:, :hidden_width], sums[l][:, hidden_width:]
-        grads[l] = gather_over_dp(gradients_of(grad_hidden[l], gate, up), groups)
-        back = to_experts(dot(grads[l], gate_up[l], (1, 1)).astype(bf16), experts)
-        upstream = (upstream.astype(f32) + dot(placing, back, (0, 0))).astype(bf16)
+        return (values.astype(f32) + mixed).astype(bf16)
+
+    def halves(sums):
+        return sums[:, :hidden_width], sums[:, hidden_width:]
+
+    rows0, grad_out1 = two_to_experts(
+        placed(0, inputs).astype(bf16), (placed(1, cotangent) * scales[1]).astype(bf16)
+    )
+    partial1 = dot(grad_out1, down[1], (1, 1)).astype(bf16)
+    sums0 = sum_over_dp(dot(rows0, gate_up[0], (1, 0)).astype(bf16), groups)
+    gate0, up0 = halves(sums0)
+    own_hidden0 = follow((jax.nn.silu(gate0) * up0).astype(bf16), partial1)
+    grad_hidden1 = lax.psum_scatter(partial1, "dp", scatter_dimension=0, tiled=True)
+    hidden0 = gather_over_dp(own_hidden0, groups)
+    hidden0, grad_hidden1 = lax.optimization_barrier((hidden0, grad_hidden1))
+    result0 = to_experts(dot(hidden0, down[0], (1, 0)).astype(bf16), experts)
+    middle = mixed_in(0, inputs, result0)
+    rows1 = to_experts(placed(1, middle).astype(bf16), experts)
+    grad_hidden1 = grad_hidden1.astype(f32)
+    sums1 = sum_over_dp(dot(rows1, gate_up[1], (1, 0)).astype(bf16), groups)
+    gate1, up1 = halves(sums1)
+    own_hidden1 = (jax.nn.silu(gate1) * up1).astype(bf16)
+    hidden1 = lax.all_gather(jnp.pad(own_hidden1, ((0, 0), (0, hidden_width))), "dp", axis=0, tiled=True)[:, :hidden_width]
+    grads1 = gather_over_dp(gradients_of(grad_hidden1, gate1, up1), groups)
+    back1 = to_experts(dot(grads1, gate_up[1], (1, 1)).astype(bf16), experts)
+    upstream = (cotangent.astype(f32) + dot(tables[1][0], back1, (0, 0))).astype(bf16)
+    grad_out0 = to_experts((placed(0, upstream) * scales[0]).astype(bf16), experts)
+    grad_out0, hidden1 = lax.optimization_barrier((grad_out0, hidden1))
+    partial0 = dot(grad_out0, down[0], (1, 1)).astype(bf16)
+    grad_hidden0 = sum_over_dp(partial0, groups)
+    grads0 = gather_over_dp(gradients_of(grad_hidden0, gate0, up0), groups)
+    out1 = dot(hidden1, down[1], (1, 0)).astype(bf16)
+    result1, back0 = two_to_experts(out1, dot(grads0, gate_up[0], (1, 1)).astype(bf16))
+    output = mixed_in(1, middle, result1)
+    upstream = (upstream.astype(f32) + dot(tables[0][0], back0, (0, 0))).astype(bf16)
+    rows, grads = [rows0, rows1], [grads0, grads1]
+    hidden, grad_out = [hidden0, hidden1], [grad_out0, grad_out1]
 
     ends = jnp.stack([upstream.reshape(groups, tokens, part), output.reshape(groups, tokens, part)], axis=1)
     home = swap(ends.reshape(groups * LAYERS, tokens, part), ("dp", "pipe"))
-    home = home.reshape(groups, micro, tokens, part).transpose(1, 2, 0, 3).reshape(micro, tokens, width)
+    home = home.reshape(groups, micro, tokens, part)
+    home = local(home_body, (micro, tokens, width), (home,), "home")
 
     def own_and_other(pair):
         own = jnp.where(first, pair[0], pair[1])

time: 404 us -> 372 us (0.921)
  waiting for transfers between devices: 164 us -> 118 us
  blocking collectives: 49.7 us -> 87.8 us
  starting transfers between devices: 98.1 us -> 73.9 us
  between operations: 1.11 us -> 14.5 us
  matrix products: 53.9 us -> 43.6 us
  other arithmetic: 24.9 us -> 18.9 us
    all_to_all x15 -> x9, waiting for transfers between devices: 164 us -> 113 us  [swap(): return lax.all_to_all(values, axes, split_axis=0, concat_axis=0, tiled=True)]
    all_to_all x3 -> x5, blocking collectives: 49.7 us -> 87.8 us  [swap(): return lax.all_to_all(values, axes, split_axis=0, concat_axis=0, tiled=True)]
    all_to_all x15 -> x9, starting transfers between devices: 73.8 us -> 45.4 us  [swap(): return lax.all_to_all(values, axes, split_axis=0, concat_axis=0, tiled=True)]
    dot_general x28, matrix products: 49.8 us -> 41.4 us  [dot(): lax.dot_general(a, b, ((contract[:1], contract[1:]), ((), ())), preferred...]
    reduce_scatter x0 -> x1, waiting for transfers between devices: none -> 5.26 us  [shards(): lax.psum_scatter(partial1, 'dp', scatter_dimension=0, tiled=True)]
    concatenate x2 -> x3, other arithmetic: 0.15 us -> 4.33 us  [the longest x1 3.25 us: shards(): gate_up = [jnp.concatenate(w[:2], axis=1) for w in layer_weights]]
    select_n x2 -> x3, other arithmetic: 8.28 us -> 7.97 us  [shards(): jnp.where(first, b, a)]
  transfers between devices with their start and end apart: 22 -> 18, of which waited for: 13 -> 9; matrix products, arithmetic and copies ran while one was open for 17% -> 14% of each run, Pallas kernels for 0% -> 0%
where the time goes in v2:
time: 372 us; the launch traced here: 371 us
  waiting for transfers between devices  118 us (32%)
  blocking collectives  87.8 us (24%)
  starting transfers between devices  73.9 us (20%)
  matrix products  43.6 us (12%)
  other arithmetic  18.9 us (5%)
  between operations  14.5 us (4%)
  local copies, waits for them, and re-layouts  11.5 us (3%)
    all_to_all x9, waiting for transfers between devices, swap(): return lax.all_to_all(values, axes, split_axis=0, concat_axis=0, tiled=True)  113 us
    all_to_all x5, blocking collectives, swap(): return lax.all_to_all(values, axes, split_axis=0, concat_axis=0, tiled=True)  87.8 us
    all_to_all x9, starting transfers between devices, swap(): return lax.all_to_all(values, axes, split_axis=0, concat_axis=0, tiled=True)  45.4 us
    dot_general x28, matrix products, dot(): lax.dot_general(a, b, ((contract[:1], contract[1:]), ((), ())), preferred...  41.4 us
    ppermute x7, starting transfers between devices, trade_cores(): return lax.ppermute(values, 'pipe', [(0, 1), (1, 0)])  28.2 us
    select_n x3, other arithmetic, shards(): jnp.where(first, b, a)  7.97 us
  transfers between devices with their start and end apart: 18, of which 9 were waited for; matrix products, arithmetic and copies ran while one was open for 14% of the time, Pallas kernels for 0%

profile of v2, /device:TPU:1, one launch (start us, length us, event | category | flops | bytes accessed | tf_op | source)
XLA Modules:
  0.0 370.7 jit_solution(7519195860710373643)
XLA Ops:
  7.2 3.3 collective-permute-start.1
  12.6 1.2 copy-done
  13.7 1.3 pack.1
  15.1 6.9 %all-to-all-start = ((bf16[16,32,1024]{2,1,0:T(8,128)(2,1)}), bf16[16,32,1024]{2,1,0:T(8,128)(2,1)S(1)}, u32[]{:S(2)}, u32[]{:S(2)}) async-start(bf16[16,32,1024]{2,1,0:T(8,128)(2,1)} %bitcast.3), calls=%async_computation | async-start | bytes 2097152 | tf_op jit(solution)/shard_map/all_to_all | solution.py:21
  22.0 2.4 broadcast_select_fusion.2
  24.6 1.7 broadcast_select_fusion.3
  26.3 3.2 pad_maximum_fusion
  29.6 3.8 %broadcast_select_fusion = (bf16[1024,896]{1,0:T(8,128)(2,1)}, bf16[1024,896]{1,0:T(8,128)(2,1)}) fusion(bf16[1024,896]{1,0:T(8,128)(2,1)} %collective-permute-done.2, pred[]{:T(512)S(6)} %eq.113, bf16[1,1,1024,896]{3,2,1,0:T(8,128)(2,1)S(1)} %copy-done.13), kind=kLoop, calls=%fused_computation.9 | loop fusion | flops 1835008 | bytes 7340033 | tf_op jit(solution)/shard_map/jit(_where)/select_n | solution.py:143
  33.4 16.5 %all-to-all-done = bf16[16,32,1024]{2,1,0:T(8,128)(2,1)S(1)} async-done(((bf16[16,32,1024]{2,1,0:T(8,128)(2,1)}), bf16[16,32,1024]{2,1,0:T(8,128)(2,1)S(1)}, u32[]{:S(2)}, u32[]{:S(2)}) %all-to-all-start) | async-done | bytes 1048608 | tf_op jit(solution)/shard_map/all_to_all | solution.py:21
  52.9 22.4 %all_to_all.70 = bf16[16,32,896]{2,1,0:T(8,128)(2,1)S(1)} all-to-all(bf16[16,32,896]{2,1,0:T(8,128)(2,1)S(1)} %pad_maximum_fusion.2), channel_id=1, replica_groups=mesh['dp'=8,'expert'=16,'pipe'=2] {'expert'}, dimensions={0} | all-to-all | bytes 1835008 | tf_op jit(solution)/shard_map/all_to_all | solution.py:21
  75.4 2.3 convolution_convert_fusion.1
  77.7 3.6 all-to-all-start.2
  81.3 3.0 convolution_convert_fusion.3
  84.3 26.2 %all-to-all-done.2 = bf16[8,32,2048]{2,1,0:T(8,128)(2,1)S(1)} async-done(((bf16[8,32,2048]{2,1,0:T(8,128)(2,1)}), bf16[8,32,2048]{2,1,0:T(8,128)(2,1)S(1)}, u32[]{:S(2)}, u32[]{:S(2)}) %all-to-all-start.2) | async-done | bytes 1048608 | tf_op jit(solution)/shard_map/all_to_all | solution.py:21
  111.6 3.5 all-to-all-start.3
  115.3 5.3 %reduce-scatter.2.cloned.1.call-done = bf16[32,1024]{1,0:T(8,128)(2,1)} async-done(((bf16[256,1024]{1,0:T(8,128)(2,1)}), bf16[32,1024]{1,0:T(8,128)(2,1)}) %reduce-scatter.2.cloned.1.call-update) | async-done | bytes 65552 | tf_op jit(solution)/shard_map/reduce_scatter | solution.py:190
  120.6 11.5 %all-to-all-done.3 = bf16[8,32,1024]{2,1,0:T(8,128)(2,1)S(1)} async-done(((bf16[8,32,1024]{2,1,0:T(8,128)(2,1)}), bf16[8,32,1024]{2,1,0:T(8,128)(2,1)S(1)}, u32[]{:S(2)}, u32[]{:S(2)}) %all-to-all-start.3) | async-done | bytes 524320 | tf_op jit(solution)/shard_map/all_to_all | solution.py:21
  132.1 3.0 convolution_convert_fusion.6
  135.1 4.4 %all-to-all-start.4 = ((bf16[16,16,896]{2,1,0:T(8,128)(2,1)}), bf16[16,16,896]{2,1,0:T(8,128)(2,1)S(1)}, u32[]{:S(2)}, u32[]{:S(2)}) async-start(bf16[16,16,896]{2,1,0:T(8,128)(2,1)} %bitcast.146), calls=%async_computation.5 | async-start | bytes 917504 | tf_op jit(solution)/shard_map/all_to_all | solution.py:21
  140.7 8.6 %all-to-all-done.4 = bf16[16,16,896]{2,1,0:T(8,128)(2,1)S(1)} async-done(((bf16[16,16,896]{2,1,0:T(8,128)(2,1)}), bf16[16,16,896]{2,1,0:T(8,128)(2,1)S(1)}, u32[]{:S(2)}, u32[]{:S(2)}) %all-to-all-start.4) | async-done | bytes 458784 | tf_op jit(solution)/shard_map/all_to_all | solution.py:21
  149.3 1.5 fusion.7
  151.7 11.8 %all_to_all.71 = bf16[16,16,896]{2,1,0:T(8,128)(2,1)S(1)} all-to-all(bf16[16,16,896]{2,1,0:T(8,128)(2,1)S(1)} %bitcast.128), channel_id=1, replica_groups=mesh['dp'=8,'expert'=16,'pipe'=2] {'expert'}, dimensions={0} | all-to-all | bytes 917504 | tf_op jit(solution)/shard_map/all_to_all | solution.py:21
  163.5 3.3 convolution_convert_fusion
  166.8 27.5 %all_to_all.72 = bf16[8,32,2048]{2,1,0:T(8,128)(2,1)S(1)} all-to-all(bf16[8,32,2048]{2,1,0:T(8,128)(2,1)S(1)} %bitcast.141), channel_id=1, replica_groups=mesh['dp'=8,'expert'=16,'pipe'=2] {'dp'}, dimensions={0} | all-to-all | bytes 2097152 | tf_op jit(solution)/shard_map/all_to_all | solution.py:21
  196.3 4.0 %all-to-all-start.7 = ((bf16[8,32,2048]{2,1,0:T(8,128)(2,1)}), bf16[8,32,2048]{2,1,0:T(8,128)(2,1)S(1)}, u32[]{:S(2)}, u32[]{:S(2)}) async-start(bf16[8,32,2048]{2,1,0:T(8,128)(2,1)} %broadcast_in_dim.21), calls=%async_computation.8 | async-start | bytes 2097152 | tf_op jit(solution)/shard_map/all_to_all | solution.py:21
  200.5 1.5 pad.4
  202.0 25.5 %all-to-all-done.7 = bf16[8,32,2048]{2,1,0:T(8,128)(2,1)S(1)} async-done(((bf16[8,32,2048]{2,1,0:T(8,128)(2,1)}), bf16[8,32,2048]{2,1,0:T(8,128)(2,1)S(1)}, u32[]{:S(2)}, u32[]{:S(2)}) %all-to-all-start.7) | async-done | bytes 1048608 | tf_op jit(solution)/shard_map/all_to_all | solution.py:21
  227.6 3.7 convolution_convert_fusion.9
  231.3 11.3 %all_to_all.73 = bf16[16,16,896]{2,1,0:T(8,128)(2,1)S(1)} all-to-all(bf16[16,16,896]{2,1,0:T(8,128)(2,1)S(1)} %bitcast.147), channel_id=1, replica_groups=mesh['dp'=8,'expert'=16,'pipe'=2] {'expert'}, dimensions={0} | all-to-all | bytes 917504 | tf_op jit(solution)/shard_map/all_to_all | solution.py:21
  242.9 1.1 fusion.5
  244.0 3.6 all-to-all-start.9
  248.7 7.4 %all-to-all-done.9 = bf16[16,16,896]{2,1,0:T(8,128)(2,1)S(1)} async-done(((bf16[16,16,896]{2,1,0:T(8,128)(2,1)}), bf16[16,16,896]{2,1,0:T(8,128)(2,1)S(1)}, u32[]{:S(2)}, u32[]{:S(2)}) %all-to-all-start.9) | async-done | bytes 458784 | tf_op jit(solution)/shard_map/all_to_all | solution.py:21
  256.2 2.4 convolution_convert_fusion.2
  258.6 14.8 %all_to_all.74 = bf16[8,32,1024]{2,1,0:T(8,128)(2,1)S(1)} all-to-all(bf16[8,32,1024]{2,1,0:T(8,128)(2,1)S(1)} %bitcast.143), channel_id=1, replica_groups=mesh['dp'=8,'expert'=16,'pipe'=2] {'dp'}, dimensions={0} | all-to-all | bytes 1048576 | tf_op jit(solution)/shard_map/all_to_all | solution.py:21
  274.6 4.2 %all-to-all-start.11 = ((bf16[8,32,2048]{2,1,0:T(8,128)(2,1)}), bf16[8,32,2048]{2,1,0:T(8,128)(2,1)}, u32[]{:S(2)}, u32[]{:S(2)}) async-start(bf16[8,32,2048]{2,1,0:T(8,128)(2,1)} %broadcast_in_dim.22), calls=%async_computation.12 | async-start | bytes 2097152 | tf_op jit(solution)/shard_map/all_to_all | solution.py:21
  279.8 11.4 %collective-permute-start.3 = (bf16[256,896]{1,0:T(8,128)(2,1)}, bf16[256,896]{1,0:T(8,128)(2,1)}, u32[]{:S(2)}, u32[]{:S(2)}) collective-permute-start(bf16[256,896]{1,0:T(8,128)(2,1)} %broadcast_select_fusion.10), channel_id=1, source_target_pairs={{0,1},{1,0},{2,3},{3,2},{4,5},{5,4},{6,7},{7,6},{8,9},{9,8},{10,11... | collective-permute-start | bytes 1376264 | tf_op jit(solution)/shard_map/ppermute | solution.py:25
  291.2 2.2 convolution_convert_fusion.4
  293.4 3.4 all-to-all-done.11
  296.9 3.6 convolution_convert_fusion.8
  301.5 4.3 %all-to-all-start.12 = ((bf16[16,32,896]{2,1,0:T(8,128)(2,1)}), bf16[16,32,896]{2,1,0:T(8,128)(2,1)}, u32[]{:S(2)}, u32[]{:S(2)}) async-start(bf16[16,32,896]{2,1,0:T(8,128)(2,1)} %pad_maximum_fusion.3), calls=%async_computation.13 | async-start | bytes 1835008 | tf_op jit(solution)/shard_map/all_to_all | solution.py:21
  306.7 12.4 %collective-permute-start.5 = (bf16[256,1024]{1,0:T(8,128)(2,1)}, bf16[256,1024]{1,0:T(8,128)(2,1)}, u32[]{:S(2)}, u32[]{:S(2)}) collective-permute-start(bf16[256,1024]{1,0:T(8,128)(2,1)} %broadcast_select_fusion.8), channel_id=1, source_target_pairs={{0,1},{1,0},{2,3},{3,2},{4,5},{5,4},{6,7},{7,6},{8,9},{9,8},{10,11... | collective-permute-start | bytes 1572872 | tf_op jit(solution)/shard_map/ppermute | solution.py:25
  320.0 2.7 broadcast_select_fusion.6
  323.2 1.3 fusion.53
  326.6 10.9 %all-to-all-start.13 = ((bf16[16,32,896]{2,1,0:T(8,128)(2,1)}), bf16[16,32,896]{2,1,0:T(8,128)(2,1)S(1)}, u32[]{:S(2)}, u32[]{:S(2)}) async-start(bf16[16,32,896]{2,1,0:T(8,128)(2,1)} %bitcast.119), calls=%async_computation.14 | async-start | bytes 1835008 | tf_op jit(solution)/shard_map/all_to_all | solution.py:21
  338.4 3.2 fusion.2
  343.0 3.1 fusion
  346.1 3.1 fusion.1
  349.2 13.7 %all-to-all-done.13 = bf16[16,32,896]{2,1,0:T(8,128)(2,1)S(1)} async-done(((bf16[16,32,896]{2,1,0:T(8,128)(2,1)}), bf16[16,32,896]{2,1,0:T(8,128)(2,1)S(1)}, u32[]{:S(2)}, u32[]{:S(2)}) %all-to-all-start.13) | async-done | bytes 917536 | tf_op jit(solution)/shard_map/all_to_all | solution.py:21
  (92 shorter events, 22.8 us)
Async XLA Ops:
  7.2 14.8 %collective-permute-start.1 = (bf16[896,1024]{1,0:T(8,128)(2,1)}, bf16[896,1024]{1,0:T(8,128)(2,1)}, u32[]{:S(2)}, u32[]{:S(2)}) collective-permute-start(bf16[896,1024]{1,0:T(8,128)(2,1)} %bitcast.129), channel_id=1, source_target_pairs={{0,1},{1,0},{2,3},{3,2},{4,5},{5,4},{6,7},{7,6},{8,9},{9,8},{10,11... | collective-permute-start | bytes 5505032 | tf_op jit(solution)/shard_map/ppermute | solution.py:25
  10.5 13.9 %collective-permute-start = (bf16[896,1024]{1,0:T(8,128)(2,1)}, bf16[896,1024]{1,0:T(8,128)(2,1)}, u32[]{:S(2)}, u32[]{:S(2)}) collective-permute-start(bf16[896,1024]{1,0:T(8,128)(2,1)} %bitcast.130), channel_id=1, source_target_pairs={{0,1},{1,0},{2,3},{3,2},{4,5},{5,4},{6,7},{7,6},{8,9},{9,8},{10,11... | collective-permute-start | bytes 5505032 | tf_op jit(solution)/shard_map/ppermute | solution.py:25
  10.6 19.0 %collective-permute-start.2 = (bf16[1024,896]{1,0:T(8,128)(2,1)}, bf16[1024,896]{1,0:T(8,128)(2,1)}, u32[]{:S(2)}, u32[]{:S(2)}) collective-permute-start(bf16[1024,896]{1,0:T(8,128)(2,1)} %bitcast.131), channel_id=1, source_target_pairs={{0,1},{1,0},{2,3},{3,2},{4,5},{5,4},{6,7},{7,6},{8,9},{9,8},{10,11... | collective-permute-start | bytes 5505032 | tf_op jit(solution)/shard_map/ppermute | solution.py:25
  12.6 1.2 copy-start
  15.1 34.8 %all-to-all-start = ((bf16[16,32,1024]{2,1,0:T(8,128)(2,1)}), bf16[16,32,1024]{2,1,0:T(8,128)(2,1)S(1)}, u32[]{:S(2)}, u32[]{:S(2)}) async-start(bf16[16,32,1024]{2,1,0:T(8,128)(2,1)} %bitcast.3), calls=%async_computation | async-start | bytes 2097152 | tf_op jit(solution)/shard_map/all_to_all | solution.py:21
  21.9 2.6 copy-start.12
  26.3 3.3 copy-start.13
  52.9 22.5 %copy-start.9 = (bf16[896,2048]{1,0:T(8,128)(2,1)S(1)}, bf16[896,2048]{1,0:T(8,128)(2,1)}, u32[]{:S(2)}) copy-start(bf16[896,2048]{1,0:T(8,128)(2,1)} %get-tuple-element.14) | copy-start | bytes 11010052
  77.7 32.8 %all-to-all-start.2 = ((bf16[8,32,2048]{2,1,0:T(8,128)(2,1)}), bf16[8,32,2048]{2,1,0:T(8,128)(2,1)S(1)}, u32[]{:S(2)}, u32[]{:S(2)}) async-start(bf16[8,32,2048]{2,1,0:T(8,128)(2,1)} %bitcast.140), calls=%async_computation.2 | async-start | bytes 2097152 | tf_op jit(solution)/shard_map/all_to_all | solution.py:21
  81.2 39.3 %reduce-scatter.2.cloned.1.call-start = ((), (), s32[]{:S(2)}) async-start(), calls=%async_computation.15 | async-start | bytes 589824 | tf_op jit(solution)/shard_map/reduce_scatter | solution.py:190
  110.6 24.4 %copy-start.10 = (f32[32,2048]{1,0:T(8,128)}, f32[32,2048]{1,0:T(8,128)S(1)}, u32[]{:S(2)}) copy-start(f32[32,2048]{1,0:T(8,128)S(1)} %convert_reduce_fusion.1) | copy-start | bytes 786436
  111.6 20.5 %all-to-all-start.3 = ((bf16[8,32,1024]{2,1,0:T(8,128)(2,1)}), bf16[8,32,1024]{2,1,0:T(8,128)(2,1)S(1)}, u32[]{:S(2)}, u32[]{:S(2)}) async-start(bf16[8,32,1024]{2,1,0:T(8,128)(2,1)} %broadcast_in_dim.20), calls=%async_computation.3 | async-start | bytes 1048576 | tf_op jit(solution)/shard_map/all_to_all | solution.py:21
  135.1 14.2 %all-to-all-start.4 = ((bf16[16,16,896]{2,1,0:T(8,128)(2,1)}), bf16[16,16,896]{2,1,0:T(8,128)(2,1)S(1)}, u32[]{:S(2)}, u32[]{:S(2)}) async-start(bf16[16,16,896]{2,1,0:T(8,128)(2,1)} %bitcast.146), calls=%async_computation.5 | async-start | bytes 917504 | tf_op jit(solution)/shard_map/all_to_all | solution.py:21
  150.9 0.8 copy-start.7
  166.8 27.7 %copy-start.15 = (bf16[32,1024]{1,0:T(8,128)(2,1)S(1)}, bf16[32,1024]{1,0:T(8,128)(2,1)}, u32[]{:S(2)}) copy-start(bf16[32,1024]{1,0:T(8,128)(2,1)} %reduce-scatter.2.cloned.1.call-done) | copy-start | bytes 196612
  196.3 31.3 %all-to-all-start.7 = ((bf16[8,32,2048]{2,1,0:T(8,128)(2,1)}), bf16[8,32,2048]{2,1,0:T(8,128)(2,1)S(1)}, u32[]{:S(2)}, u32[]{:S(2)}) async-start(bf16[8,32,2048]{2,1,0:T(8,128)(2,1)} %broadcast_in_dim.21), calls=%async_computation.8 | async-start | bytes 2097152 | tf_op jit(solution)/shard_map/all_to_all | solution.py:21
  200.3 47.3 %all-gather.2.cloned.1.call-start = ((), (), s32[]{:S(2)}) async-start(), calls=%async_computation.16 | async-start | bytes 1179648 | tf_op jit(solution)/shard_map/all_gather | solution.py:200
  227.6 3.7 %copy-start.1 = (bf16[8,32,2048]{2,1,0:T(8,128)(2,1)}, bf16[8,32,2048]{2,1,0:T(8,128)(2,1)S(1)}, u32[]{:S(2)}) copy-start(bf16[8,32,2048]{2,1,0:T(8,128)(2,1)S(1)} %all-to-all-done.7) | copy-start | bytes 3145732
  242.9 4.7 %copy-start.5 = (bf16[256,896]{1,0:T(8,128)(2,1)}, bf16[256,896]{1,0:T(8,128)(2,1)S(1)}, u32[]{:S(2)}) copy-start(bf16[256,896]{1,0:T(8,128)(2,1)S(1)} %fusion.4) | copy-start | bytes 1376260
  244.0 12.1 %all-to-all-start.9 = ((bf16[16,16,896]{2,1,0:T(8,128)(2,1)}), bf16[16,16,896]{2,1,0:T(8,128)(2,1)S(1)}, u32[]{:S(2)}, u32[]{:S(2)}) async-start(bf16[16,16,896]{2,1,0:T(8,128)(2,1)} %bitcast.26), calls=%async_computation.10 | async-start | bytes 917504 | tf_op jit(solution)/shard_map/all_to_all | solution.py:21
  256.2 63.0 %copy-start.4 = (bf16[16,16,896]{2,1,0:T(8,128)(2,1)}, bf16[16,16,896]{2,1,0:T(8,128)(2,1)S(1)}, u32[]{:S(2)}) copy-start(bf16[16,16,896]{2,1,0:T(8,128)(2,1)S(1)} %all-to-all-done.9) | copy-start | bytes 1376260
  256.2 17.3 %copy-start.11 = (f32[32,2048]{1,0:T(8,128)S(1)}, f32[32,2048]{1,0:T(8,128)}, u32[]{:S(2)}) copy-start(f32[32,2048]{1,0:T(8,128)} %copy-done.10) | copy-start | bytes 786436
  274.6 22.2 %all-to-all-start.11 = ((bf16[8,32,2048]{2,1,0:T(8,128)(2,1)}), bf16[8,32,2048]{2,1,0:T(8,128)(2,1)}, u32[]{:S(2)}, u32[]{:S(2)}) async-start(bf16[8,32,2048]{2,1,0:T(8,128)(2,1)} %broadcast_in_dim.22), calls=%async_computation.12 | async-start | bytes 2097152 | tf_op jit(solution)/shard_map/all_to_all | solution.py:21
  279.8 63.2 %collective-permute-start.3 = (bf16[256,896]{1,0:T(8,128)(2,1)}, bf16[256,896]{1,0:T(8,128)(2,1)}, u32[]{:S(2)}, u32[]{:S(2)}) collective-permute-start(bf16[256,896]{1,0:T(8,128)(2,1)} %broadcast_select_fusion.10), channel_id=1, source_target_pairs={{0,1},{1,0},{2,3},{3,2},{4,5},{5,4},{6,7},{7,6},{8,9},{9,8},{10,11... | collective-permute-start | bytes 1376264 | tf_op jit(solution)/shard_map/ppermute | solution.py:25
  301.5 21.7 %all-to-all-start.12 = ((bf16[16,32,896]{2,1,0:T(8,128)(2,1)}), bf16[16,32,896]{2,1,0:T(8,128)(2,1)}, u32[]{:S(2)}, u32[]{:S(2)}) async-start(bf16[16,32,896]{2,1,0:T(8,128)(2,1)} %pad_maximum_fusion.3), calls=%async_computation.13 | async-start | bytes 1835008 | tf_op jit(solution)/shard_map/all_to_all | solution.py:21
  305.8 14.2 %copy-start.2 = (bf16[8,32,2048]{2,1,0:T(8,128)(2,1)S(1)}, bf16[8,32,2048]{2,1,0:T(8,128)(2,1)}, u32[]{:S(2)}) copy-start(bf16[8,32,2048]{2,1,0:T(8,128)(2,1)} %copy-done.1) | copy-start | bytes 3145732
  306.7 31.6 %collective-permute-start.5 = (bf16[256,1024]{1,0:T(8,128)(2,1)}, bf16[256,1024]{1,0:T(8,128)(2,1)}, u32[]{:S(2)}, u32[]{:S(2)}) collective-permute-start(bf16[256,1024]{1,0:T(8,128)(2,1)} %broadcast_select_fusion.8), channel_id=1, source_target_pairs={{0,1},{1,0},{2,3},{3,2},{4,5},{5,4},{6,7},{7,6},{8,9},{9,8},{10,11... | collective-permute-start | bytes 1572872 | tf_op jit(solution)/shard_map/ppermute | solution.py:25
  320.0 18.3 %collective-permute-start.6 = (bf16[256,896]{1,0:T(8,128)(2,1)}, bf16[256,896]{1,0:T(8,128)(2,1)}, u32[]{:S(2)}, u32[]{:S(2)}) collective-permute-start(bf16[256,896]{1,0:T(8,128)(2,1)} %broadcast_select_fusion.9), channel_id=1, source_target_pairs={{0,1},{1,0},{2,3},{3,2},{4,5},{5,4},{6,7},{7,6},{8,9},{9,8},{10,11... | collective-permute-start | bytes 1376264 | tf_op jit(solution)/shard_map/ppermute | solution.py:25
  322.7 1.8 copy-start.8
  322.7 2.4 copy-start.6
  322.7 20.3 %collective-permute-start.4 = (bf16[256,2048]{1,0:T(8,128)(2,1)}, bf16[256,2048]{1,0:T(8,128)(2,1)}, u32[]{:S(2)}, u32[]{:S(2)}) collective-permute-start(bf16[256,2048]{1,0:T(8,128)(2,1)} %get-tuple-element.28), channel_id=1, source_target_pairs={{0,1},{1,0},{2,3},{3,2},{4,5},{5,4},{6,7},{7,6},{8,9},{9,8},{10,11... | collective-permute-start | bytes 3145736 | tf_op jit(solution)/shard_map/ppermute | solution.py:25
  323.2 1.3 copy-start.14
  326.6 36.3 %all-to-all-start.13 = ((bf16[16,32,896]{2,1,0:T(8,128)(2,1)}), bf16[16,32,896]{2,1,0:T(8,128)(2,1)S(1)}, u32[]{:S(2)}, u32[]{:S(2)}) async-start(bf16[16,32,896]{2,1,0:T(8,128)(2,1)} %bitcast.119), calls=%async_computation.14 | async-start | bytes 1835008 | tf_op jit(solution)/shard_map/all_to_all | solution.py:21
  338.3 3.3 copy-start.3
Sparse Core Ops, SparseCore 0:
  85.2 35.3 reduce-scatter.1
  203.1 39.6 all-gather.1

commit v3 on v2

--- a/solution.py
+++ b/solution.py
@@ -197,15 +197,20 @@
     sums1 = sum_over_dp(dot(rows1, gate_up[1], (1, 0)).astype(bf16), groups)
     gate1, up1 = halves(sums1)
     own_hidden1 = (jax.nn.silu(gate1) * up1).astype(bf16)
-    hidden1 = lax.all_gather(jnp.pad(own_hidden1, ((0, 0), (0, hidden_width))), "dp", axis=0, tiled=True)[:, :hidden_width]
+    beside = jnp.concatenate([own_hidden1, sums0.astype(bf16)], axis=1)
+    beside = lax.all_gather(beside, "dp", axis=0, tiled=True)
     grads1 = gather_over_dp(gradients_of(grad_hidden1, gate1, up1), groups)
     back1 = to_experts(dot(grads1, gate_up[1], (1, 1)).astype(bf16), experts)
     upstream = (cotangent.astype(f32) + dot(tables[1][0], back1, (0, 0))).astype(bf16)
     grad_out0 = to_experts((placed(0, upstream) * scales[0]).astype(bf16), experts)
-    grad_out0, hidden1 = lax.optimization_barrier((grad_out0, hidden1))
+    grad_out0, beside = lax.optimization_barrier((grad_out0, beside))
+    hidden1, all_gate0, all_up0 = [
+        beside[:, i * hidden_width : (i + 1) * hidden_width] for i in range(3)
+    ]
     partial0 = dot(grad_out0, down[0], (1, 1)).astype(bf16)
     grad_hidden0 = sum_over_dp(partial0, groups)
-    grads0 = gather_over_dp(gradients_of(grad_hidden0, gate0, up0), groups)
+    all_grad_hidden0 = gather_over_dp(grad_hidden0.astype(bf16), groups)
+    grads0 = gradients_of(all_grad_hidden0.astype(f32), all_gate0.astype(f32), all_up0.astype(f32))
     out1 = dot(hidden1, down[1], (1, 0)).astype(bf16)
     result1, back0 = two_to_experts(out1, dot(grads0, gate_up[0], (1, 1)).astype(bf16))
     output = mixed_in(1, middle, result1)

time: 372 us -> 368 us (0.989)
  blocking collectives: 87.8 us -> 100 us
  waiting for transfers between devices: 118 us -> 107 us
  starting transfers between devices: 73.9 us -> 66.1 us
    all_to_all x5 -> x6, blocking collectives: 87.8 us -> 100 us  [swap(): return lax.all_to_all(values, axes, split_axis=0, concat_axis=0, tiled=True)]
    all_to_all x9 -> x8, waiting for transfers between devices: 113 us -> 102 us  [swap(): return lax.all_to_all(values, axes, split_axis=0, concat_axis=0, tiled=True)]
    ppermute x7, starting transfers between devices: 28.2 us -> 24.3 us  [trade_cores(): return lax.ppermute(values, 'pipe', [(0, 1), (1, 0)])]
    all_to_all x9 -> x8, starting transfers between devices: 45.4 us -> 41.5 us  [swap(): return lax.all_to_all(values, axes, split_axis=0, concat_axis=0, tiled=True)]
  transfers between devices with their start and end apart: 18 -> 17, of which waited for: 9 -> 7; matrix products, arithmetic and copies ran while one was open for 14% -> 15% of each run, Pallas kernels for 0% -> 0%
where the time goes in v3:
time: 368 us; the launch traced here: 366 us
  waiting for transfers between devices  107 us (29%)
  blocking collectives  100 us (27%)
  starting transfers between devices  66.1 us (18%)
  matrix products  44.7 us (12%)
  other arithmetic  22.3 us (6%)
  between operations  14.6 us (4%)
  local copies, waits for them, and re-layouts  9.07 us (2%)
    all_to_all x8, waiting for transfers between devices, swap(): return lax.all_to_all(values, axes, split_axis=0, concat_axis=0, tiled=True)  102 us
    all_to_all x6, blocking collectives, swap(): return lax.all_to_all(values, axes, split_axis=0, concat_axis=0, tiled=True)  100 us
    dot_general x28, matrix products, dot(): lax.dot_general(a, b, ((contract[:1], contract[1:]), ((), ())), preferred...  42.5 us
    all_to_all x8, starting transfers between devices, swap(): return lax.all_to_all(values, axes, split_axis=0, concat_axis=0, tiled=True)  41.5 us
    ppermute x7, starting transfers between devices, trade_cores(): return lax.ppermute(values, 'pipe', [(0, 1), (1, 0)])  24.3 us
    select_n x3, other arithmetic, shards(): jnp.where(first, b, a)  7.42 us
  transfers between devices with their start and end apart: 17, of which 7 were waited for; matrix products, arithmetic and copies ran while one was open for 15% of the time, Pallas kernels for 0%

profile of v3, /device:TPU:1, one launch (start us, length us, event | category | flops | bytes accessed | tf_op | source)
XLA Modules:
  0.0 366.2 jit_solution(17345149533332090272)
XLA Ops:
  7.2 3.3 collective-permute-start.1
  12.6 1.2 copy-done
  13.7 1.3 pack.1
  15.1 6.9 %all-to-all-start = ((bf16[16,32,1024]{2,1,0:T(8,128)(2,1)}), bf16[16,32,1024]{2,1,0:T(8,128)(2,1)S(1)}, u32[]{:S(2)}, u32[]{:S(2)}) async-start(bf16[16,32,1024]{2,1,0:T(8,128)(2,1)} %bitcast.3), calls=%async_computation | async-start | bytes 2097152 | tf_op jit(solution)/shard_map/all_to_all | solution.py:21
  22.0 1.9 broadcast_select_fusion.2
  24.0 1.7 broadcast_select_fusion.3
  25.8 3.3 pad_maximum_fusion
  29.0 3.8 %broadcast_select_fusion = (bf16[1024,896]{1,0:T(8,128)(2,1)}, bf16[1024,896]{1,0:T(8,128)(2,1)}) fusion(bf16[1024,896]{1,0:T(8,128)(2,1)} %collective-permute-done.2, pred[]{:T(512)S(6)} %eq.113, bf16[1,1,1024,896]{3,2,1,0:T(8,128)(2,1)S(1)} %copy-done.15), kind=kLoop, calls=%fused_computation.9 | loop fusion | flops 1835008 | bytes 7340033 | tf_op jit(solution)/shard_map/jit(_where)/select_n | solution.py:143
  32.8 17.0 %all-to-all-done = bf16[16,32,1024]{2,1,0:T(8,128)(2,1)S(1)} async-done(((bf16[16,32,1024]{2,1,0:T(8,128)(2,1)}), bf16[16,32,1024]{2,1,0:T(8,128)(2,1)S(1)}, u32[]{:S(2)}, u32[]{:S(2)}) %all-to-all-start) | async-done | bytes 1048608 | tf_op jit(solution)/shard_map/all_to_all | solution.py:21
  52.9 22.4 %all_to_all.70 = bf16[16,32,896]{2,1,0:T(8,128)(2,1)S(1)} all-to-all(bf16[16,32,896]{2,1,0:T(8,128)(2,1)S(1)} %pad_maximum_fusion.3), channel_id=1, replica_groups=mesh['dp'=8,'expert'=16,'pipe'=2] {'expert'}, dimensions={0} | all-to-all | bytes 1835008 | tf_op jit(solution)/shard_map/all_to_all | solution.py:21
  75.5 2.3 convolution_convert_fusion.1
  77.7 3.6 all-to-all-start.2
  81.3 3.0 convolution_convert_fusion.3
  84.4 26.2 %all-to-all-done.2 = bf16[8,32,2048]{2,1,0:T(8,128)(2,1)S(1)} async-done(((bf16[8,32,2048]{2,1,0:T(8,128)(2,1)}), bf16[8,32,2048]{2,1,0:T(8,128)(2,1)S(1)}, u32[]{:S(2)}, u32[]{:S(2)}) %all-to-all-start.2) | async-done | bytes 1048608 | tf_op jit(solution)/shard_map/all_to_all | solution.py:21
  111.6 3.5 all-to-all-start.3
  115.4 4.5 %reduce-scatter.2.cloned.1.call-done = bf16[32,1024]{1,0:T(8,128)(2,1)} async-done(((bf16[256,1024]{1,0:T(8,128)(2,1)}), bf16[32,1024]{1,0:T(8,128)(2,1)}) %reduce-scatter.2.cloned.1.call-update) | async-done | bytes 65552 | tf_op jit(solution)/shard_map/reduce_scatter | solution.py:190
  119.9 12.3 %all-to-all-done.3 = bf16[8,32,1024]{2,1,0:T(8,128)(2,1)S(1)} async-done(((bf16[8,32,1024]{2,1,0:T(8,128)(2,1)}), bf16[8,32,1024]{2,1,0:T(8,128)(2,1)S(1)}, u32[]{:S(2)}, u32[]{:S(2)}) %all-to-all-start.3) | async-done | bytes 524320 | tf_op jit(solution)/shard_map/all_to_all | solution.py:21
  132.1 3.0 convolution_convert_fusion.6
  135.1 4.4 %all-to-all-start.4 = ((bf16[16,16,896]{2,1,0:T(8,128)(2,1)}), bf16[16,16,896]{2,1,0:T(8,128)(2,1)S(1)}, u32[]{:S(2)}, u32[]{:S(2)}) async-start(bf16[16,16,896]{2,1,0:T(8,128)(2,1)} %bitcast.146), calls=%async_computation.5 | async-start | bytes 917504 | tf_op jit(solution)/shard_map/all_to_all | solution.py:21
  140.8 8.5 %all-to-all-done.4 = bf16[16,16,896]{2,1,0:T(8,128)(2,1)S(1)} async-done(((bf16[16,16,896]{2,1,0:T(8,128)(2,1)}), bf16[16,16,896]{2,1,0:T(8,128)(2,1)S(1)}, u32[]{:S(2)}, u32[]{:S(2)}) %all-to-all-start.4) | async-done | bytes 458784 | tf_op jit(solution)/shard_map/all_to_all | solution.py:21
  149.3 1.5 fusion.7
  151.6 11.7 %all_to_all.71 = bf16[16,16,896]{2,1,0:T(8,128)(2,1)S(1)} all-to-all(bf16[16,16,896]{2,1,0:T(8,128)(2,1)S(1)} %bitcast.128), channel_id=1, replica_groups=mesh['dp'=8,'expert'=16,'pipe'=2] {'expert'}, dimensions={0} | all-to-all | bytes 917504 | tf_op jit(solution)/shard_map/all_to_all | solution.py:21
  163.2 3.3 convolution_convert_fusion
  166.6 28.6 %all_to_all.72 = bf16[8,32,2048]{2,1,0:T(8,128)(2,1)S(1)} all-to-all(bf16[8,32,2048]{2,1,0:T(8,128)(2,1)S(1)} %bitcast.141), channel_id=1, replica_groups=mesh['dp'=8,'expert'=16,'pipe'=2] {'dp'}, dimensions={0} | all-to-all | bytes 2097152 | tf_op jit(solution)/shard_map/all_to_all | solution.py:21
  196.5 3.8 %all-to-all-start.7 = ((bf16[8,32,2048]{2,1,0:T(8,128)(2,1)}), bf16[8,32,2048]{2,1,0:T(8,128)(2,1)S(1)}, u32[]{:S(2)}, u32[]{:S(2)}) async-start(bf16[8,32,2048]{2,1,0:T(8,128)(2,1)} %broadcast_in_dim.21), calls=%async_computation.8 | async-start | bytes 2097152 | tf_op jit(solution)/shard_map/all_to_all | solution.py:21
  202.2 25.7 %all-to-all-done.7 = bf16[8,32,2048]{2,1,0:T(8,128)(2,1)S(1)} async-done(((bf16[8,32,2048]{2,1,0:T(8,128)(2,1)}), bf16[8,32,2048]{2,1,0:T(8,128)(2,1)S(1)}, u32[]{:S(2)}, u32[]{:S(2)}) %all-to-all-start.7) | async-done | bytes 1048608 | tf_op jit(solution)/shard_map/all_to_all | solution.py:21
  227.9 3.4 convolution_convert_fusion.9
  231.3 11.2 %all_to_all.73 = bf16[16,16,896]{2,1,0:T(8,128)(2,1)S(1)} all-to-all(bf16[16,16,896]{2,1,0:T(8,128)(2,1)S(1)} %bitcast.147), channel_id=1, replica_groups=mesh['dp'=8,'expert'=16,'pipe'=2] {'expert'}, dimensions={0} | all-to-all | bytes 917504 | tf_op jit(solution)/shard_map/all_to_all | solution.py:21
  243.6 11.2 %all_to_all.74 = bf16[16,16,896]{2,1,0:T(8,128)(2,1)S(1)} all-to-all(bf16[16,16,896]{2,1,0:T(8,128)(2,1)S(1)} %bitcast.125), channel_id=1, replica_groups=mesh['dp'=8,'expert'=16,'pipe'=2] {'expert'}, dimensions={0} | all-to-all | bytes 917504 | tf_op jit(solution)/shard_map/all_to_all | solution.py:21
  254.8 2.4 convolution_convert_fusion.2
  257.2 15.2 %all_to_all.75 = bf16[8,32,1024]{2,1,0:T(8,128)(2,1)} all-to-all(bf16[8,32,1024]{2,1,0:T(8,128)(2,1)S(1)} %bitcast.143), channel_id=1, replica_groups=mesh['dp'=8,'expert'=16,'pipe'=2] {'dp'}, dimensions={0} | all-to-all | bytes 1048576 | tf_op jit(solution)/shard_map/all_to_all | solution.py:21
  272.5 1.1 reduce_sum.52
  274.4 4.2 %all-to-all-start.11 = ((bf16[8,32,1024]{2,1,0:T(8,128)(2,1)}), bf16[8,32,1024]{2,1,0:T(8,128)(2,1)}, u32[]{:S(2)}, u32[]{:S(2)}) async-start(bf16[8,32,1024]{2,1,0:T(8,128)(2,1)} %broadcast_in_dim.22), calls=%async_computation.12 | async-start | bytes 1048576 | tf_op jit(solution)/shard_map/all_to_all | solution.py:21
  279.5 10.7 %collective-permute-start.3 = (bf16[256,896]{1,0:T(8,128)(2,1)}, bf16[256,896]{1,0:T(8,128)(2,1)}, u32[]{:S(2)}, u32[]{:S(2)}) collective-permute-start(bf16[256,896]{1,0:T(8,128)(2,1)} %broadcast_select_fusion.10), channel_id=1, source_target_pairs={{0,1},{1,0},{2,3},{3,2},{4,5},{5,4},{6,7},{7,6},{8,9},{9,8},{10,11... | collective-permute-start | bytes 1376264 | tf_op jit(solution)/shard_map/ppermute | solution.py:25
  290.2 3.2 convolution_convert_fusion.4
  293.4 1.9 fusion.15
  295.4 3.8 %convolution_convert_fusion.8 = bf16[256,896]{1,0:T(8,128)(2,1)S(1)} fusion(bf16[896,2048]{1,0:T(8,128)(2,1)} %get-tuple-element.14, bf16[256,1024]{1,0:T(8,128)(2,1)S(1)} %get-tuple-element.31, bf16[256,1024]{1,0:T(8,128)(2,1)S(1)} %get-tuple-element.30), kind=kOutput, calls=%fused_computation.40 | convolution fusion | flops 941850624 | bytes 5177344 | tf_op jit(solution)/shard_map/dot_general | solution.py:29
  300.2 4.3 %all-to-all-start.12 = ((bf16[16,32,896]{2,1,0:T(8,128)(2,1)}), bf16[16,32,896]{2,1,0:T(8,128)(2,1)}, u32[]{:S(2)}, u32[]{:S(2)}) async-start(bf16[16,32,896]{2,1,0:T(8,128)(2,1)} %pad_maximum_fusion.4), calls=%async_computation.13 | async-start | bytes 1835008 | tf_op jit(solution)/shard_map/all_to_all | solution.py:21
  304.6 2.0 broadcast_select_fusion.8
  306.5 9.2 %collective-permute-start.5 = (bf16[256,1024]{1,0:T(8,128)(2,1)}, bf16[256,1024]{1,0:T(8,128)(2,1)}, u32[]{:S(2)}, u32[]{:S(2)}) collective-permute-start(bf16[256,1024]{1,0:T(8,128)(2,1)} %broadcast_select_fusion.8), channel_id=1, source_target_pairs={{0,1},{1,0},{2,3},{3,2},{4,5},{5,4},{6,7},{7,6},{8,9},{9,8},{10,11... | collective-permute-start | bytes 1572872 | tf_op jit(solution)/shard_map/ppermute | solution.py:25
  316.6 1.5 broadcast_select_fusion.6
  318.7 1.3 fusion.66
  322.0 11.0 %all-to-all-start.13 = ((bf16[16,32,896]{2,1,0:T(8,128)(2,1)}), bf16[16,32,896]{2,1,0:T(8,128)(2,1)S(1)}, u32[]{:S(2)}, u32[]{:S(2)}) async-start(bf16[16,32,896]{2,1,0:T(8,128)(2,1)} %bitcast.118), calls=%async_computation.14 | async-start | bytes 1835008 | tf_op jit(solution)/shard_map/all_to_all | solution.py:21
  333.0 1.9 fusion.28
  335.0 3.2 fusion.2
  339.5 3.1 fusion
  342.6 3.1 fusion.1
  345.7 12.6 %all-to-all-done.13 = bf16[16,32,896]{2,1,0:T(8,128)(2,1)S(1)} async-done(((bf16[16,32,896]{2,1,0:T(8,128)(2,1)}), bf16[16,32,896]{2,1,0:T(8,128)(2,1)S(1)}, u32[]{:S(2)}, u32[]{:S(2)}) %all-to-all-start.13) | async-done | bytes 917536 | tf_op jit(solution)/shard_map/all_to_all | solution.py:21
  (106 shorter events, 21.5 us)
Async XLA Ops:
  7.2 14.8 %collective-permute-start.1 = (bf16[896,1024]{1,0:T(8,128)(2,1)}, bf16[896,1024]{1,0:T(8,128)(2,1)}, u32[]{:S(2)}, u32[]{:S(2)}) collective-permute-start(bf16[896,1024]{1,0:T(8,128)(2,1)} %bitcast.129), channel_id=1, source_target_pairs={{0,1},{1,0},{2,3},{3,2},{4,5},{5,4},{6,7},{7,6},{8,9},{9,8},{10,11... | collective-permute-start | bytes 5505032 | tf_op jit(solution)/shard_map/ppermute | solution.py:25
  10.5 13.4 %collective-permute-start = (bf16[896,1024]{1,0:T(8,128)(2,1)}, bf16[896,1024]{1,0:T(8,128)(2,1)}, u32[]{:S(2)}, u32[]{:S(2)}) collective-permute-start(bf16[896,1024]{1,0:T(8,128)(2,1)} %bitcast.130), channel_id=1, source_target_pairs={{0,1},{1,0},{2,3},{3,2},{4,5},{5,4},{6,7},{7,6},{8,9},{9,8},{10,11... | collective-permute-start | bytes 5505032 | tf_op jit(solution)/shard_map/ppermute | solution.py:25
  10.6 18.4 %collective-permute-start.2 = (bf16[1024,896]{1,0:T(8,128)(2,1)}, bf16[1024,896]{1,0:T(8,128)(2,1)}, u32[]{:S(2)}, u32[]{:S(2)}) collective-permute-start(bf16[1024,896]{1,0:T(8,128)(2,1)} %bitcast.131), channel_id=1, source_target_pairs={{0,1},{1,0},{2,3},{3,2},{4,5},{5,4},{6,7},{7,6},{8,9},{9,8},{10,11... | collective-permute-start | bytes 5505032 | tf_op jit(solution)/shard_map/ppermute | solution.py:25
  12.6 1.2 copy-start
  13.7 8.2 %copy-start.13 = (bf16[1,1,896,1024]{3,2,1,0:T(8,128)(2,1)S(1)}, bf16[1,1,896,1024]{3,2,1,0:T(8,128)(2,1)}, u32[]{:S(2)}) copy-start(bf16[1,1,896,1024]{3,2,1,0:T(8,128)(2,1)} %param.10) | copy-start | bytes 5505028
  15.1 34.8 %all-to-all-start = ((bf16[16,32,1024]{2,1,0:T(8,128)(2,1)}), bf16[16,32,1024]{2,1,0:T(8,128)(2,1)S(1)}, u32[]{:S(2)}, u32[]{:S(2)}) async-start(bf16[16,32,1024]{2,1,0:T(8,128)(2,1)} %bitcast.3), calls=%async_computation | async-start | bytes 2097152 | tf_op jit(solution)/shard_map/all_to_all | solution.py:21
  22.0 2.1 copy-start.14
  25.7 3.3 copy-start.15
  50.8 2.0 copy-start.19
  51.1 191.7 %copy-start.17 = (pred[256,256]{0,1:T(32,128)(4,1)}, pred[256,256]{0,1:T(32,128)(4,1)S(1)}, u32[]{:S(2)}) copy-start(pred[256,256]{0,1:T(32,128)(4,1)S(1)} %fusion.12) | copy-start | bytes 196612
  52.9 22.5 %copy-start.7 = (bf16[896,2048]{1,0:T(8,128)(2,1)S(1)}, bf16[896,2048]{1,0:T(8,128)(2,1)}, u32[]{:S(2)}) copy-start(bf16[896,2048]{1,0:T(8,128)(2,1)} %get-tuple-element.14) | copy-start | bytes 11010052
  75.4 240.3 %copy-start.1 = (bf16[16,16,896]{2,1,0:T(8,128)(2,1)}, bf16[16,16,896]{2,1,0:T(8,128)(2,1)S(1)}, u32[]{:S(2)}) copy-start(bf16[16,16,896]{2,1,0:T(8,128)(2,1)S(1)} %get-tuple-element.38) | copy-start | bytes 1376260
  77.7 32.9 %all-to-all-start.2 = ((bf16[8,32,2048]{2,1,0:T(8,128)(2,1)}), bf16[8,32,2048]{2,1,0:T(8,128)(2,1)S(1)}, u32[]{:S(2)}, u32[]{:S(2)}) async-start(bf16[8,32,2048]{2,1,0:T(8,128)(2,1)} %bitcast.140), calls=%async_computation.2 | async-start | bytes 2097152 | tf_op jit(solution)/shard_map/all_to_all | solution.py:21
  81.3 38.6 %reduce-scatter.2.cloned.1.call-start = ((), (), s32[]{:S(2)}) async-start(), calls=%async_computation.15 | async-start | bytes 589824 | tf_op jit(solution)/shard_map/reduce_scatter | solution.py:190
  110.7 24.4 %copy-start.8 = (f32[32,2048]{1,0:T(8,128)}, f32[32,2048]{1,0:T(8,128)S(1)}, u32[]{:S(2)}) copy-start(f32[32,2048]{1,0:T(8,128)S(1)} %convert_reduce_fusion.1) | copy-start | bytes 786436
  111.6 20.5 %all-to-all-start.3 = ((bf16[8,32,1024]{2,1,0:T(8,128)(2,1)}), bf16[8,32,1024]{2,1,0:T(8,128)(2,1)S(1)}, u32[]{:S(2)}, u32[]{:S(2)}) async-start(bf16[8,32,1024]{2,1,0:T(8,128)(2,1)} %broadcast_in_dim.20), calls=%async_computation.3 | async-start | bytes 1048576 | tf_op jit(solution)/shard_map/all_to_all | solution.py:21
  135.1 15.7 %copy-start.20 = (pred[256,256]{0,1:T(32,128)(4,1)S(1)}, pred[256,256]{0,1:T(32,128)(4,1)}, u32[]{:S(2)}) copy-start(pred[256,256]{0,1:T(32,128)(4,1)} %copy-done.19) | copy-start | bytes 196612
  135.1 14.1 %all-to-all-start.4 = ((bf16[16,16,896]{2,1,0:T(8,128)(2,1)}), bf16[16,16,896]{2,1,0:T(8,128)(2,1)S(1)}, u32[]{:S(2)}, u32[]{:S(2)}) async-start(bf16[16,16,896]{2,1,0:T(8,128)(2,1)} %bitcast.146), calls=%async_computation.5 | async-start | bytes 917504 | tf_op jit(solution)/shard_map/all_to_all | solution.py:21
  150.8 0.8 copy-start.5
  166.5 28.8 %copy-start.23 = (bf16[32,1024]{1,0:T(8,128)(2,1)S(1)}, bf16[32,1024]{1,0:T(8,128)(2,1)}, u32[]{:S(2)}) copy-start(bf16[32,1024]{1,0:T(8,128)(2,1)} %reduce-scatter.2.cloned.1.call-done) | copy-start | bytes 196612
  196.5 31.4 %all-to-all-start.7 = ((bf16[8,32,2048]{2,1,0:T(8,128)(2,1)}), bf16[8,32,2048]{2,1,0:T(8,128)(2,1)S(1)}, u32[]{:S(2)}, u32[]{:S(2)}) async-start(bf16[8,32,2048]{2,1,0:T(8,128)(2,1)} %broadcast_in_dim.21), calls=%async_computation.8 | async-start | bytes 2097152 | tf_op jit(solution)/shard_map/all_to_all | solution.py:21
  200.3 54.5 %all-gather.2.cloned.1.call-start = ((), (), s32[]{:S(2)}) async-start(), calls=%async_computation.16 | async-start | bytes 1769472 | tf_op jit(solution)/shard_map/all_gather | solution.py:201
  227.9 14.6 %copy-start.21 = (pred[256,256]{0,1:T(32,128)(4,1)S(1)}, pred[256,256]{0,1:T(32,128)(4,1)}, u32[]{:S(2)}) copy-start(pred[256,256]{0,1:T(32,128)(4,1)} %copy-done.19) | copy-start | bytes 196612
  242.8 0.8 copy-start.3
  254.8 60.9 %copy-start.2 = (bf16[16,16,896]{2,1,0:T(8,128)(2,1)}, bf16[16,16,896]{2,1,0:T(8,128)(2,1)S(1)}, u32[]{:S(2)}) copy-start(bf16[16,16,896]{2,1,0:T(8,128)(2,1)S(1)} %all_to_all.74) | copy-start | bytes 1376260
  274.4 18.9 %all-to-all-start.11 = ((bf16[8,32,1024]{2,1,0:T(8,128)(2,1)}), bf16[8,32,1024]{2,1,0:T(8,128)(2,1)}, u32[]{:S(2)}, u32[]{:S(2)}) async-start(bf16[8,32,1024]{2,1,0:T(8,128)(2,1)} %broadcast_in_dim.22), calls=%async_computation.12 | async-start | bytes 1048576 | tf_op jit(solution)/shard_map/all_to_all | solution.py:21
  279.5 60.0 %collective-permute-start.3 = (bf16[256,896]{1,0:T(8,128)(2,1)}, bf16[256,896]{1,0:T(8,128)(2,1)}, u32[]{:S(2)}, u32[]{:S(2)}) collective-permute-start(bf16[256,896]{1,0:T(8,128)(2,1)} %broadcast_select_fusion.10), channel_id=1, source_target_pairs={{0,1},{1,0},{2,3},{3,2},{4,5},{5,4},{6,7},{7,6},{8,9},{9,8},{10,11... | collective-permute-start | bytes 1376264 | tf_op jit(solution)/shard_map/ppermute | solution.py:25
  295.3 3.9 %copy-start.9 = (bf16[256,1024]{1,0:T(8,128)(2,1)}, bf16[256,1024]{1,0:T(8,128)(2,1)S(1)}, u32[]{:S(2)}) copy-start(bf16[256,1024]{1,0:T(8,128)(2,1)S(1)} %get-tuple-element.30) | copy-start | bytes 1572868
  295.3 3.9 %copy-start.11 = (bf16[256,1024]{1,0:T(8,128)(2,1)}, bf16[256,1024]{1,0:T(8,128)(2,1)S(1)}, u32[]{:S(2)}) copy-start(bf16[256,1024]{1,0:T(8,128)(2,1)S(1)} %get-tuple-element.31) | copy-start | bytes 1572868
  295.3 3.9 %copy-start.22 = (bf16[256,896]{1,0:T(8,128)(2,1)S(1)}, bf16[256,896]{1,0:T(8,128)(2,1)}, u32[]{:S(2)}) copy-start(bf16[256,896]{1,0:T(8,128)(2,1)} %convolution_convert_fusion.4) | copy-start | bytes 1376260
  300.2 18.5 %all-to-all-start.12 = ((bf16[16,32,896]{2,1,0:T(8,128)(2,1)}), bf16[16,32,896]{2,1,0:T(8,128)(2,1)}, u32[]{:S(2)}, u32[]{:S(2)}) async-start(bf16[16,32,896]{2,1,0:T(8,128)(2,1)} %pad_maximum_fusion.4), calls=%async_computation.13 | async-start | bytes 1835008 | tf_op jit(solution)/shard_map/all_to_all | solution.py:21
  304.5 12.1 %copy-start.10 = (bf16[256,1024]{1,0:T(8,128)(2,1)S(1)}, bf16[256,1024]{1,0:T(8,128)(2,1)}, u32[]{:S(2)}) copy-start(bf16[256,1024]{1,0:T(8,128)(2,1)} %copy-done.9) | copy-start | bytes 1572868
  304.5 12.1 %copy-start.12 = (bf16[256,1024]{1,0:T(8,128)(2,1)S(1)}, bf16[256,1024]{1,0:T(8,128)(2,1)}, u32[]{:S(2)}) copy-start(bf16[256,1024]{1,0:T(8,128)(2,1)} %copy-done.11) | copy-start | bytes 1572868
  306.5 28.5 %collective-permute-start.5 = (bf16[256,1024]{1,0:T(8,128)(2,1)}, bf16[256,1024]{1,0:T(8,128)(2,1)}, u32[]{:S(2)}, u32[]{:S(2)}) collective-permute-start(bf16[256,1024]{1,0:T(8,128)(2,1)} %broadcast_select_fusion.8), channel_id=1, source_target_pairs={{0,1},{1,0},{2,3},{3,2},{4,5},{5,4},{6,7},{7,6},{8,9},{9,8},{10,11... | collective-permute-start | bytes 1572872 | tf_op jit(solution)/shard_map/ppermute | solution.py:25
  316.6 18.4 %collective-permute-start.6 = (bf16[256,896]{1,0:T(8,128)(2,1)}, bf16[256,896]{1,0:T(8,128)(2,1)}, u32[]{:S(2)}, u32[]{:S(2)}) collective-permute-start(bf16[256,896]{1,0:T(8,128)(2,1)} %broadcast_select_fusion.9), channel_id=1, source_target_pairs={{0,1},{1,0},{2,3},{3,2},{4,5},{5,4},{6,7},{7,6},{8,9},{9,8},{10,11... | collective-permute-start | bytes 1376264 | tf_op jit(solution)/shard_map/ppermute | solution.py:25
  318.2 1.8 copy-start.6
  318.2 2.4 copy-start.4
  318.2 2.4 copy-start.18
  318.2 21.4 %collective-permute-start.4 = (bf16[256,2048]{1,0:T(8,128)(2,1)}, bf16[256,2048]{1,0:T(8,128)(2,1)}, u32[]{:S(2)}, u32[]{:S(2)}) collective-permute-start(bf16[256,2048]{1,0:T(8,128)(2,1)} %get-tuple-element.28), channel_id=1, source_target_pairs={{0,1},{1,0},{2,3},{3,2},{4,5},{5,4},{6,7},{7,6},{8,9},{9,8},{10,11... | collective-permute-start | bytes 3145736 | tf_op jit(solution)/shard_map/ppermute | solution.py:25
  318.7 1.3 copy-start.16
  322.0 36.3 %all-to-all-start.13 = ((bf16[16,32,896]{2,1,0:T(8,128)(2,1)}), bf16[16,32,896]{2,1,0:T(8,128)(2,1)S(1)}, u32[]{:S(2)}, u32[]{:S(2)}) async-start(bf16[16,32,896]{2,1,0:T(8,128)(2,1)} %bitcast.118), calls=%async_computation.14 | async-start | bytes 1835008 | tf_op jit(solution)/shard_map/all_to_all | solution.py:21
Sparse Core Ops, SparseCore 0:
  85.2 34.6 reduce-scatter.1
  203.6 42.4 all-gather.1

commit v4 on v3

--- a/solution.py
+++ b/solution.py
@@ -46,24 +46,28 @@
 
 
 def pack_body(experts, groups, io, ids, weights, sent):
-    micro, tokens, width = io.shape
-    part = width // groups
-    column = lax.broadcasted_iota(i32, (tokens, ROUTE_COLUMNS), 1)
+    micro, top, tokens = ids.shape
+    part = io.shape[2] // groups
+    dims = (ROUTE_COLUMNS, tokens)
+    column = lax.broadcasted_iota(i32, dims, 0)
     expert, kind = column % experts, column // experts
-    later = lax.broadcasted_iota(i32, (tokens, tokens), 0)
-    earlier = (lax.broadcasted_iota(i32, (tokens, tokens), 1) < later).astype(f32).astype(bf16)
+    square = (tokens, tokens)
+    row, lane = lax.broadcasted_iota(i32, square, 0), lax.broadcasted_iota(i32, square, 1)
+    earlier = (row < lane).astype(f32).astype(bf16)
+    same = (row == lane).astype(f32).astype(bf16)
     for m in range(micro):
-        chosen = jnp.zeros((tokens, ROUTE_COLUMNS), f32)
-        weight = jnp.zeros((tokens, ROUTE_COLUMNS), f32)
-        for k in range(ids.shape[2]):
-            hit = ids[m, :, k : k + 1] == expert
+        chosen = jnp.zeros(dims, f32)
+        weight = jnp.zeros(dims, f32)
+        for k in range(top):
+            hit = ids[m, k : k + 1, :] == expert
             chosen = jnp.where(hit, 1.0, chosen)
-            weight = jnp.where(hit, weights[m, :, k : k + 1], weight)
-        before = dot(earlier, chosen.astype(bf16), (1, 0))
+            weight = jnp.where(hit, weights[m, k : k + 1, :], weight)
+        before = dot(chosen.astype(bf16), earlier, (1, 0))
         code = jnp.where((chosen > 0.0) & (before < CAPACITY), before + 1.0, 0.0)
         high, middle, low = [piece.astype(f32) for piece in exact_parts(weight)]
         values = jnp.where(kind == 0, code, jnp.where(kind == 1, high, jnp.where(kind == 2, middle, low)))
         values = jnp.where(kind < 4, values, 0.0).astype(bf16)
+        values = dot(same, values, (1, 1)).astype(bf16)
         for d in range(groups):
             sent[d, m, :, :part] = io[m, :, d * part : (d + 1) * part]
             sent[d, m, :, part:] = values
@@ -148,7 +152,7 @@
     sent = local(
         functools.partial(pack_body, experts, groups),
         (groups, micro, tokens, part + ROUTE_COLUMNS),
-        (layer_io[0], route_ids[0], route_weights[0]),
+        (layer_io[0], route_ids[0].swapaxes(1, 2), route_weights[0].swapaxes(1, 2)),
         "pack",
     )
     got = swap(sent.reshape(groups * micro, tokens, part + ROUTE_COLUMNS), ("dp", "pipe"))

time: 368 us -> 368 us (level)
  transfers between devices with their start and end apart: 17 -> 17, of which waited for: 7 -> 7; matrix products, arithmetic and copies ran while one was open for 15% -> 14% of each run, Pallas kernels for 0% -> 0%
where the time goes in v4:
time: 368 us; the launch traced here: 366 us
  waiting for transfers between devices  107 us (29%)
  blocking collectives  100 us (27%)
  starting transfers between devices  66.3 us (18%)
  matrix products  44.7 us (12%)
  other arithmetic  22.2 us (6%)
  between operations  14.6 us (4%)
  local copies, waits for them, and re-layouts  8.92 us (2%)
    all_to_all x8, waiting for transfers between devices, swap(): return lax.all_to_all(values, axes, split_axis=0, concat_axis=0, tiled=True)  102 us
    all_to_all x6, blocking collectives, swap(): return lax.all_to_all(values, axes, split_axis=0, concat_axis=0, tiled=True)  100 us
    dot_general x28, matrix products, dot(): lax.dot_general(a, b, ((contract[:1], contract[1:]), ((), ())), preferred...  42.5 us
    all_to_all x8, starting transfers between devices, swap(): return lax.all_to_all(values, axes, split_axis=0, concat_axis=0, tiled=True)  41.7 us
    ppermute x7, starting transfers between devices, trade_cores(): return lax.ppermute(values, 'pipe', [(0, 1), (1, 0)])  24.3 us
    select_n x3, other arithmetic, shards(): jnp.where(first, b, a)  7.42 us
  transfers between devices with their start and end apart: 17, of which 7 were waited for; matrix products, arithmetic and copies ran while one was open for 14% of the time, Pallas kernels for 0%

profile of v4, /device:TPU:1, one launch (start us, length us, event | category | flops | bytes accessed | tf_op | source)
XLA Modules:
  0.0 366.2 jit_solution(5256999176382068510)
XLA Ops:
  7.2 3.3 collective-permute-start.1
  11.0 1.2 copy-done
  13.6 1.3 pack.1
  14.9 6.9 %all-to-all-start = ((bf16[16,32,1024]{2,1,0:T(8,128)(2,1)}), bf16[16,32,1024]{2,1,0:T(8,128)(2,1)S(1)}, u32[]{:S(2)}, u32[]{:S(2)}) async-start(bf16[16,32,1024]{2,1,0:T(8,128)(2,1)} %bitcast.5), calls=%async_computation | async-start | bytes 2097152 | tf_op jit(solution)/shard_map/all_to_all | solution.py:21
  21.8 1.9 broadcast_select_fusion.2
  23.8 1.7 broadcast_select_fusion.3
  25.6 3.2 pad_maximum_fusion
  28.8 3.8 %broadcast_select_fusion = (bf16[1024,896]{1,0:T(8,128)(2,1)}, bf16[1024,896]{1,0:T(8,128)(2,1)}) fusion(bf16[1024,896]{1,0:T(8,128)(2,1)} %collective-permute-done.2, pred[]{:T(512)S(6)} %eq.113, bf16[1,1,1024,896]{3,2,1,0:T(8,128)(2,1)S(1)} %copy-done.17), kind=kLoop, calls=%fused_computation.9 | loop fusion | flops 1835008 | bytes 7340033 | tf_op jit(solution)/shard_map/jit(_where)/select_n | solution.py:147
  32.6 17.0 %all-to-all-done = bf16[16,32,1024]{2,1,0:T(8,128)(2,1)S(1)} async-done(((bf16[16,32,1024]{2,1,0:T(8,128)(2,1)}), bf16[16,32,1024]{2,1,0:T(8,128)(2,1)S(1)}, u32[]{:S(2)}, u32[]{:S(2)}) %all-to-all-start) | async-done | bytes 1048608 | tf_op jit(solution)/shard_map/all_to_all | solution.py:21
  52.7 22.4 %all_to_all.70 = bf16[16,32,896]{2,1,0:T(8,128)(2,1)S(1)} all-to-all(bf16[16,32,896]{2,1,0:T(8,128)(2,1)S(1)} %pad_maximum_fusion.3), channel_id=1, replica_groups=mesh['dp'=8,'expert'=16,'pipe'=2] {'expert'}, dimensions={0} | all-to-all | bytes 1835008 | tf_op jit(solution)/shard_map/all_to_all | solution.py:21
  75.3 2.3 convolution_convert_fusion.1
  77.6 3.6 all-to-all-start.2
  81.2 3.0 convolution_convert_fusion.3
  84.2 26.2 %all-to-all-done.2 = bf16[8,32,2048]{2,1,0:T(8,128)(2,1)S(1)} async-done(((bf16[8,32,2048]{2,1,0:T(8,128)(2,1)}), bf16[8,32,2048]{2,1,0:T(8,128)(2,1)S(1)}, u32[]{:S(2)}, u32[]{:S(2)}) %all-to-all-start.2) | async-done | bytes 1048608 | tf_op jit(solution)/shard_map/all_to_all | solution.py:21
  111.5 3.5 all-to-all-start.3
  115.3 5.2 %reduce-scatter.2.cloned.1.call-done = bf16[32,1024]{1,0:T(8,128)(2,1)} async-done(((bf16[256,1024]{1,0:T(8,128)(2,1)}), bf16[32,1024]{1,0:T(8,128)(2,1)}) %reduce-scatter.2.cloned.1.call-update) | async-done | bytes 65552 | tf_op jit(solution)/shard_map/reduce_scatter | solution.py:194
  120.5 11.4 %all-to-all-done.3 = bf16[8,32,1024]{2,1,0:T(8,128)(2,1)S(1)} async-done(((bf16[8,32,1024]{2,1,0:T(8,128)(2,1)}), bf16[8,32,1024]{2,1,0:T(8,128)(2,1)S(1)}, u32[]{:S(2)}, u32[]{:S(2)}) %all-to-all-start.3) | async-done | bytes 524320 | tf_op jit(solution)/shard_map/all_to_all | solution.py:21
  131.8 3.0 convolution_convert_fusion.6
  134.8 4.6 %all-to-all-start.4 = ((bf16[16,16,896]{2,1,0:T(8,128)(2,1)}), bf16[16,16,896]{2,1,0:T(8,128)(2,1)S(1)}, u32[]{:S(2)}, u32[]{:S(2)}) async-start(bf16[16,16,896]{2,1,0:T(8,128)(2,1)} %bitcast.150), calls=%async_computation.5 | async-start | bytes 917504 | tf_op jit(solution)/shard_map/all_to_all | solution.py:21
  140.6 8.6 %all-to-all-done.4 = bf16[16,16,896]{2,1,0:T(8,128)(2,1)S(1)} async-done(((bf16[16,16,896]{2,1,0:T(8,128)(2,1)}), bf16[16,16,896]{2,1,0:T(8,128)(2,1)S(1)}, u32[]{:S(2)}, u32[]{:S(2)}) %all-to-all-start.4) | async-done | bytes 458784 | tf_op jit(solution)/shard_map/all_to_all | solution.py:21
  149.3 1.5 fusion.7
  151.6 11.9 %all_to_all.71 = bf16[16,16,896]{2,1,0:T(8,128)(2,1)S(1)} all-to-all(bf16[16,16,896]{2,1,0:T(8,128)(2,1)S(1)} %bitcast.132), channel_id=1, replica_groups=mesh['dp'=8,'expert'=16,'pipe'=2] {'expert'}, dimensions={0} | all-to-all | bytes 917504 | tf_op jit(solution)/shard_map/all_to_all | solution.py:21
  163.5 3.3 convolution_convert_fusion
  166.8 28.4 %all_to_all.72 = bf16[8,32,2048]{2,1,0:T(8,128)(2,1)S(1)} all-to-all(bf16[8,32,2048]{2,1,0:T(8,128)(2,1)S(1)} %bitcast.145), channel_id=1, replica_groups=mesh['dp'=8,'expert'=16,'pipe'=2] {'dp'}, dimensions={0} | all-to-all | bytes 2097152 | tf_op jit(solution)/shard_map/all_to_all | solution.py:21
  196.5 3.7 %all-to-all-start.7 = ((bf16[8,32,2048]{2,1,0:T(8,128)(2,1)}), bf16[8,32,2048]{2,1,0:T(8,128)(2,1)S(1)}, u32[]{:S(2)}, u32[]{:S(2)}) async-start(bf16[8,32,2048]{2,1,0:T(8,128)(2,1)} %broadcast_in_dim.21), calls=%async_computation.8 | async-start | bytes 2097152 | tf_op jit(solution)/shard_map/all_to_all | solution.py:21
  202.2 25.7 %all-to-all-done.7 = bf16[8,32,2048]{2,1,0:T(8,128)(2,1)S(1)} async-done(((bf16[8,32,2048]{2,1,0:T(8,128)(2,1)}), bf16[8,32,2048]{2,1,0:T(8,128)(2,1)S(1)}, u32[]{:S(2)}, u32[]{:S(2)}) %all-to-all-start.7) | async-done | bytes 1048608 | tf_op jit(solution)/shard_map/all_to_all | solution.py:21
  227.9 3.4 convolution_convert_fusion.9
  231.2 11.2 %all_to_all.73 = bf16[16,16,896]{2,1,0:T(8,128)(2,1)S(1)} all-to-all(bf16[16,16,896]{2,1,0:T(8,128)(2,1)S(1)} %bitcast.151), channel_id=1, replica_groups=mesh['dp'=8,'expert'=16,'pipe'=2] {'expert'}, dimensions={0} | all-to-all | bytes 917504 | tf_op jit(solution)/shard_map/all_to_all | solution.py:21
  243.6 11.2 %all_to_all.74 = bf16[16,16,896]{2,1,0:T(8,128)(2,1)S(1)} all-to-all(bf16[16,16,896]{2,1,0:T(8,128)(2,1)S(1)} %bitcast.129), channel_id=1, replica_groups=mesh['dp'=8,'expert'=16,'pipe'=2] {'expert'}, dimensions={0} | all-to-all | bytes 917504 | tf_op jit(solution)/shard_map/all_to_all | solution.py:21
  254.8 2.4 convolution_convert_fusion.2
  257.2 15.2 %all_to_all.75 = bf16[8,32,1024]{2,1,0:T(8,128)(2,1)} all-to-all(bf16[8,32,1024]{2,1,0:T(8,128)(2,1)S(1)} %bitcast.147), channel_id=1, replica_groups=mesh['dp'=8,'expert'=16,'pipe'=2] {'dp'}, dimensions={0} | all-to-all | bytes 1048576 | tf_op jit(solution)/shard_map/all_to_all | solution.py:21
  272.4 1.1 reduce_sum.52
  274.4 4.2 %all-to-all-start.11 = ((bf16[8,32,1024]{2,1,0:T(8,128)(2,1)}), bf16[8,32,1024]{2,1,0:T(8,128)(2,1)}, u32[]{:S(2)}, u32[]{:S(2)}) async-start(bf16[8,32,1024]{2,1,0:T(8,128)(2,1)} %broadcast_in_dim.22), calls=%async_computation.12 | async-start | bytes 1048576 | tf_op jit(solution)/shard_map/all_to_all | solution.py:21
  279.5 10.7 %collective-permute-start.3 = (bf16[256,896]{1,0:T(8,128)(2,1)}, bf16[256,896]{1,0:T(8,128)(2,1)}, u32[]{:S(2)}, u32[]{:S(2)}) collective-permute-start(bf16[256,896]{1,0:T(8,128)(2,1)} %broadcast_select_fusion.10), channel_id=1, source_target_pairs={{0,1},{1,0},{2,3},{3,2},{4,5},{5,4},{6,7},{7,6},{8,9},{9,8},{10,11... | collective-permute-start | bytes 1376264 | tf_op jit(solution)/shard_map/ppermute | solution.py:25
  290.2 3.2 convolution_convert_fusion.4
  293.4 1.9 fusion.15
  295.3 3.8 %convolution_convert_fusion.8 = bf16[256,896]{1,0:T(8,128)(2,1)S(1)} fusion(bf16[896,2048]{1,0:T(8,128)(2,1)} %get-tuple-element.14, bf16[256,1024]{1,0:T(8,128)(2,1)S(1)} %get-tuple-element.31, bf16[256,1024]{1,0:T(8,128)(2,1)S(1)} %get-tuple-element.30), kind=kOutput, calls=%fused_computation.40 | convolution fusion | flops 941850624 | bytes 5177344 | tf_op jit(solution)/shard_map/dot_general | solution.py:29
  300.2 4.3 %all-to-all-start.12 = ((bf16[16,32,896]{2,1,0:T(8,128)(2,1)}), bf16[16,32,896]{2,1,0:T(8,128)(2,1)}, u32[]{:S(2)}, u32[]{:S(2)}) async-start(bf16[16,32,896]{2,1,0:T(8,128)(2,1)} %pad_maximum_fusion.4), calls=%async_computation.13 | async-start | bytes 1835008 | tf_op jit(solution)/shard_map/all_to_all | solution.py:21
  304.6 2.0 broadcast_select_fusion.8
  306.5 9.2 %collective-permute-start.5 = (bf16[256,1024]{1,0:T(8,128)(2,1)}, bf16[256,1024]{1,0:T(8,128)(2,1)}, u32[]{:S(2)}, u32[]{:S(2)}) collective-permute-start(bf16[256,1024]{1,0:T(8,128)(2,1)} %broadcast_select_fusion.8), channel_id=1, source_target_pairs={{0,1},{1,0},{2,3},{3,2},{4,5},{5,4},{6,7},{7,6},{8,9},{9,8},{10,11... | collective-permute-start | bytes 1572872 | tf_op jit(solution)/shard_map/ppermute | solution.py:25
  316.6 1.5 broadcast_select_fusion.6
  318.7 1.3 fusion.66
  322.0 11.0 %all-to-all-start.13 = ((bf16[16,32,896]{2,1,0:T(8,128)(2,1)}), bf16[16,32,896]{2,1,0:T(8,128)(2,1)S(1)}, u32[]{:S(2)}, u32[]{:S(2)}) async-start(bf16[16,32,896]{2,1,0:T(8,128)(2,1)} %bitcast.122), calls=%async_computation.14 | async-start | bytes 1835008 | tf_op jit(solution)/shard_map/all_to_all | solution.py:21
  333.0 1.9 fusion.28
  335.0 3.2 fusion.2
  339.5 3.1 fusion
  342.6 3.1 fusion.1
  345.7 12.6 %all-to-all-done.13 = bf16[16,32,896]{2,1,0:T(8,128)(2,1)S(1)} async-done(((bf16[16,32,896]{2,1,0:T(8,128)(2,1)}), bf16[16,32,896]{2,1,0:T(8,128)(2,1)S(1)}, u32[]{:S(2)}, u32[]{:S(2)}) %all-to-all-start.13) | async-done | bytes 917536 | tf_op jit(solution)/shard_map/all_to_all | solution.py:21
  (108 shorter events, 21.3 us)
Async XLA Ops:
  7.2 14.6 %collective-permute-start.1 = (bf16[896,1024]{1,0:T(8,128)(2,1)}, bf16[896,1024]{1,0:T(8,128)(2,1)}, u32[]{:S(2)}, u32[]{:S(2)}) collective-permute-start(bf16[896,1024]{1,0:T(8,128)(2,1)} %bitcast.133), channel_id=1, source_target_pairs={{0,1},{1,0},{2,3},{3,2},{4,5},{5,4},{6,7},{7,6},{8,9},{9,8},{10,11... | collective-permute-start | bytes 5505032 | tf_op jit(solution)/shard_map/ppermute | solution.py:25
  10.5 13.2 %collective-permute-start = (bf16[896,1024]{1,0:T(8,128)(2,1)}, bf16[896,1024]{1,0:T(8,128)(2,1)}, u32[]{:S(2)}, u32[]{:S(2)}) collective-permute-start(bf16[896,1024]{1,0:T(8,128)(2,1)} %bitcast.134), channel_id=1, source_target_pairs={{0,1},{1,0},{2,3},{3,2},{4,5},{5,4},{6,7},{7,6},{8,9},{9,8},{10,11... | collective-permute-start | bytes 5505032 | tf_op jit(solution)/shard_map/ppermute | solution.py:25
  10.6 18.2 %collective-permute-start.2 = (bf16[1024,896]{1,0:T(8,128)(2,1)}, bf16[1024,896]{1,0:T(8,128)(2,1)}, u32[]{:S(2)}, u32[]{:S(2)}) collective-permute-start(bf16[1024,896]{1,0:T(8,128)(2,1)} %bitcast.135), channel_id=1, source_target_pairs={{0,1},{1,0},{2,3},{3,2},{4,5},{5,4},{6,7},{7,6},{8,9},{9,8},{10,11... | collective-permute-start | bytes 5505032 | tf_op jit(solution)/shard_map/ppermute | solution.py:25
  11.0 1.2 copy-start
  12.2 0.7 copy-start.1
  12.9 0.7 copy-start.2
  13.6 8.2 %copy-start.15 = (bf16[1,1,896,1024]{3,2,1,0:T(8,128)(2,1)S(1)}, bf16[1,1,896,1024]{3,2,1,0:T(8,128)(2,1)}, u32[]{:S(2)}) copy-start(bf16[1,1,896,1024]{3,2,1,0:T(8,128)(2,1)} %param.10) | copy-start | bytes 5505028
  14.9 34.8 %all-to-all-start = ((bf16[16,32,1024]{2,1,0:T(8,128)(2,1)}), bf16[16,32,1024]{2,1,0:T(8,128)(2,1)S(1)}, u32[]{:S(2)}, u32[]{:S(2)}) async-start(bf16[16,32,1024]{2,1,0:T(8,128)(2,1)} %bitcast.5), calls=%async_computation | async-start | bytes 2097152 | tf_op jit(solution)/shard_map/all_to_all | solution.py:21
  21.8 2.1 copy-start.16
  25.6 3.3 copy-start.17
  50.6 2.0 copy-start.21
  50.9 191.8 %copy-start.19 = (pred[256,256]{0,1:T(32,128)(4,1)}, pred[256,256]{0,1:T(32,128)(4,1)S(1)}, u32[]{:S(2)}) copy-start(pred[256,256]{0,1:T(32,128)(4,1)S(1)} %fusion.12) | copy-start | bytes 196612
  52.7 22.5 %copy-start.9 = (bf16[896,2048]{1,0:T(8,128)(2,1)S(1)}, bf16[896,2048]{1,0:T(8,128)(2,1)}, u32[]{:S(2)}) copy-start(bf16[896,2048]{1,0:T(8,128)(2,1)} %get-tuple-element.14) | copy-start | bytes 11010052
  75.3 240.5 %copy-start.3 = (bf16[16,16,896]{2,1,0:T(8,128)(2,1)}, bf16[16,16,896]{2,1,0:T(8,128)(2,1)S(1)}, u32[]{:S(2)}) copy-start(bf16[16,16,896]{2,1,0:T(8,128)(2,1)S(1)} %get-tuple-element.38) | copy-start | bytes 1376260
  77.6 32.9 %all-to-all-start.2 = ((bf16[8,32,2048]{2,1,0:T(8,128)(2,1)}), bf16[8,32,2048]{2,1,0:T(8,128)(2,1)S(1)}, u32[]{:S(2)}, u32[]{:S(2)}) async-start(bf16[8,32,2048]{2,1,0:T(8,128)(2,1)} %bitcast.144), calls=%async_computation.2 | async-start | bytes 2097152 | tf_op jit(solution)/shard_map/all_to_all | solution.py:21
  81.1 39.3 %reduce-scatter.2.cloned.1.call-start = ((), (), s32[]{:S(2)}) async-start(), calls=%async_computation.15 | async-start | bytes 589824 | tf_op jit(solution)/shard_map/reduce_scatter | solution.py:194
  110.6 24.2 %copy-start.10 = (f32[32,2048]{1,0:T(8,128)}, f32[32,2048]{1,0:T(8,128)S(1)}, u32[]{:S(2)}) copy-start(f32[32,2048]{1,0:T(8,128)S(1)} %convert_reduce_fusion.1) | copy-start | bytes 786436
  111.5 20.3 %all-to-all-start.3 = ((bf16[8,32,1024]{2,1,0:T(8,128)(2,1)}), bf16[8,32,1024]{2,1,0:T(8,128)(2,1)S(1)}, u32[]{:S(2)}, u32[]{:S(2)}) async-start(bf16[8,32,1024]{2,1,0:T(8,128)(2,1)} %broadcast_in_dim.20), calls=%async_computation.3 | async-start | bytes 1048576 | tf_op jit(solution)/shard_map/all_to_all | solution.py:21
  134.8 16.0 %copy-start.22 = (pred[256,256]{0,1:T(32,128)(4,1)S(1)}, pred[256,256]{0,1:T(32,128)(4,1)}, u32[]{:S(2)}) copy-start(pred[256,256]{0,1:T(32,128)(4,1)} %copy-done.21) | copy-start | bytes 196612
  134.8 14.4 %all-to-all-start.4 = ((bf16[16,16,896]{2,1,0:T(8,128)(2,1)}), bf16[16,16,896]{2,1,0:T(8,128)(2,1)S(1)}, u32[]{:S(2)}, u32[]{:S(2)}) async-start(bf16[16,16,896]{2,1,0:T(8,128)(2,1)} %bitcast.150), calls=%async_computation.5 | async-start | bytes 917504 | tf_op jit(solution)/shard_map/all_to_all | solution.py:21
  150.8 0.8 copy-start.7
  166.8 28.5 %copy-start.25 = (bf16[32,1024]{1,0:T(8,128)(2,1)S(1)}, bf16[32,1024]{1,0:T(8,128)(2,1)}, u32[]{:S(2)}) copy-start(bf16[32,1024]{1,0:T(8,128)(2,1)} %reduce-scatter.2.cloned.1.call-done) | copy-start | bytes 196612
  196.5 31.3 %all-to-all-start.7 = ((bf16[8,32,2048]{2,1,0:T(8,128)(2,1)}), bf16[8,32,2048]{2,1,0:T(8,128)(2,1)S(1)}, u32[]{:S(2)}, u32[]{:S(2)}) async-start(bf16[8,32,2048]{2,1,0:T(8,128)(2,1)} %broadcast_in_dim.21), calls=%async_computation.8 | async-start | bytes 2097152 | tf_op jit(solution)/shard_map/all_to_all | solution.py:21
  200.3 54.5 %all-gather.2.cloned.1.call-start = ((), (), s32[]{:S(2)}) async-start(), calls=%async_computation.16 | async-start | bytes 1769472 | tf_op jit(solution)/shard_map/all_gather | solution.py:205
  227.9 14.6 %copy-start.23 = (pred[256,256]{0,1:T(32,128)(4,1)S(1)}, pred[256,256]{0,1:T(32,128)(4,1)}, u32[]{:S(2)}) copy-start(pred[256,256]{0,1:T(32,128)(4,1)} %copy-done.21) | copy-start | bytes 196612
  242.8 0.8 copy-start.5
  254.8 61.0 %copy-start.4 = (bf16[16,16,896]{2,1,0:T(8,128)(2,1)}, bf16[16,16,896]{2,1,0:T(8,128)(2,1)S(1)}, u32[]{:S(2)}) copy-start(bf16[16,16,896]{2,1,0:T(8,128)(2,1)S(1)} %all_to_all.74) | copy-start | bytes 1376260
  274.4 19.0 %all-to-all-start.11 = ((bf16[8,32,1024]{2,1,0:T(8,128)(2,1)}), bf16[8,32,1024]{2,1,0:T(8,128)(2,1)}, u32[]{:S(2)}, u32[]{:S(2)}) async-start(bf16[8,32,1024]{2,1,0:T(8,128)(2,1)} %broadcast_in_dim.22), calls=%async_computation.12 | async-start | bytes 1048576 | tf_op jit(solution)/shard_map/all_to_all | solution.py:21
  279.5 60.0 %collective-permute-start.3 = (bf16[256,896]{1,0:T(8,128)(2,1)}, bf16[256,896]{1,0:T(8,128)(2,1)}, u32[]{:S(2)}, u32[]{:S(2)}) collective-permute-start(bf16[256,896]{1,0:T(8,128)(2,1)} %broadcast_select_fusion.10), channel_id=1, source_target_pairs={{0,1},{1,0},{2,3},{3,2},{4,5},{5,4},{6,7},{7,6},{8,9},{9,8},{10,11... | collective-permute-start | bytes 1376264 | tf_op jit(solution)/shard_map/ppermute | solution.py:25
  295.3 3.9 %copy-start.11 = (bf16[256,1024]{1,0:T(8,128)(2,1)}, bf16[256,1024]{1,0:T(8,128)(2,1)S(1)}, u32[]{:S(2)}) copy-start(bf16[256,1024]{1,0:T(8,128)(2,1)S(1)} %get-tuple-element.30) | copy-start | bytes 1572868
  295.3 3.9 %copy-start.13 = (bf16[256,1024]{1,0:T(8,128)(2,1)}, bf16[256,1024]{1,0:T(8,128)(2,1)S(1)}, u32[]{:S(2)}) copy-start(bf16[256,1024]{1,0:T(8,128)(2,1)S(1)} %get-tuple-element.31) | copy-start | bytes 1572868
  295.3 3.9 %copy-start.24 = (bf16[256,896]{1,0:T(8,128)(2,1)S(1)}, bf16[256,896]{1,0:T(8,128)(2,1)}, u32[]{:S(2)}) copy-start(bf16[256,896]{1,0:T(8,128)(2,1)} %convolution_convert_fusion.4) | copy-start | bytes 1376260
  300.2 18.5 %all-to-all-start.12 = ((bf16[16,32,896]{2,1,0:T(8,128)(2,1)}), bf16[16,32,896]{2,1,0:T(8,128)(2,1)}, u32[]{:S(2)}, u32[]{:S(2)}) async-start(bf16[16,32,896]{2,1,0:T(8,128)(2,1)} %pad_maximum_fusion.4), calls=%async_computation.13 | async-start | bytes 1835008 | tf_op jit(solution)/shard_map/all_to_all | solution.py:21
  304.5 12.1 %copy-start.12 = (bf16[256,1024]{1,0:T(8,128)(2,1)S(1)}, bf16[256,1024]{1,0:T(8,128)(2,1)}, u32[]{:S(2)}) copy-start(bf16[256,1024]{1,0:T(8,128)(2,1)} %copy-done.11) | copy-start | bytes 1572868
  304.5 12.1 %copy-start.14 = (bf16[256,1024]{1,0:T(8,128)(2,1)S(1)}, bf16[256,1024]{1,0:T(8,128)(2,1)}, u32[]{:S(2)}) copy-start(bf16[256,1024]{1,0:T(8,128)(2,1)} %copy-done.13) | copy-start | bytes 1572868
  306.5 28.4 %collective-permute-start.5 = (bf16[256,1024]{1,0:T(8,128)(2,1)}, bf16[256,1024]{1,0:T(8,128)(2,1)}, u32[]{:S(2)}, u32[]{:S(2)}) collective-permute-start(bf16[256,1024]{1,0:T(8,128)(2,1)} %broadcast_select_fusion.8), channel_id=1, source_target_pairs={{0,1},{1,0},{2,3},{3,2},{4,5},{5,4},{6,7},{7,6},{8,9},{9,8},{10,11... | collective-permute-start | bytes 1572872 | tf_op jit(solution)/shard_map/ppermute | solution.py:25
  316.6 18.4 %collective-permute-start.6 = (bf16[256,896]{1,0:T(8,128)(2,1)}, bf16[256,896]{1,0:T(8,128)(2,1)}, u32[]{:S(2)}, u32[]{:S(2)}) collective-permute-start(bf16[256,896]{1,0:T(8,128)(2,1)} %broadcast_select_fusion.9), channel_id=1, source_target_pairs={{0,1},{1,0},{2,3},{3,2},{4,5},{5,4},{6,7},{7,6},{8,9},{9,8},{10,11... | collective-permute-start | bytes 1376264 | tf_op jit(solution)/shard_map/ppermute | solution.py:25
  318.1 1.8 copy-start.8
  318.1 2.4 copy-start.6
  318.2 2.4 copy-start.20
  318.2 21.4 %collective-permute-start.4 = (bf16[256,2048]{1,0:T(8,128)(2,1)}, bf16[256,2048]{1,0:T(8,128)(2,1)}, u32[]{:S(2)}, u32[]{:S(2)}) collective-permute-start(bf16[256,2048]{1,0:T(8,128)(2,1)} %get-tuple-element.28), channel_id=1, source_target_pairs={{0,1},{1,0},{2,3},{3,2},{4,5},{5,4},{6,7},{7,6},{8,9},{9,8},{10,11... | collective-permute-start | bytes 3145736 | tf_op jit(solution)/shard_map/ppermute | solution.py:25
  318.7 1.3 copy-start.18
  322.0 36.3 %all-to-all-start.13 = ((bf16[16,32,896]{2,1,0:T(8,128)(2,1)}), bf16[16,32,896]{2,1,0:T(8,128)(2,1)S(1)}, u32[]{:S(2)}, u32[]{:S(2)}) async-start(bf16[16,32,896]{2,1,0:T(8,128)(2,1)} %bitcast.122), calls=%async_computation.14 | async-start | bytes 1835008 | tf_op jit(solution)/shard_map/all_to_all | solution.py:21
Sparse Core Ops, SparseCore 0:
  85.1 35.3 reduce-scatter.1
  203.6 42.4 all-gather.1

commit v5 on v4

--- a/solution.py
+++ b/solution.py
@@ -11,7 +11,7 @@
 LAYERS = 2
 ROUTE_COLUMNS = 128
 
-highest = lax.Precision.HIGHEST
+combining = lax.Precision.HIGH
 bf16 = jnp.bfloat16
 f32 = jnp.float32
 i32 = jnp.int32
@@ -177,7 +177,7 @@
 
     def mixed_in(l, values, result):
         mixed = lax.dot_general(
-            tables[l][1], result.astype(f32), (((0,), (0,)), ((), ())), precision=highest
+            tables[l][1], result.astype(f32), (((0,), (0,)), ((), ())), precision=combining
         )
         return (values.astype(f32) + mixed).astype(bf16)
 

time: 368 us -> 368 us (level)
  no operation moved by 1% of the time
where the time goes in v5:
time: 368 us; the launch traced here: 366 us
  waiting for transfers between devices  107 us (29%)
  blocking collectives  100 us (27%)
  starting transfers between devices  66.3 us (18%)
  matrix products  44.4 us (12%)
  other arithmetic  22.2 us (6%)
  between operations  14.6 us (4%)
  local copies, waits for them, and re-layouts  8.92 us (2%)
    all_to_all x8, waiting for transfers between devices, swap(): return lax.all_to_all(values, axes, split_axis=0, concat_axis=0, tiled=True)  102 us
    all_to_all x6, blocking collectives, swap(): return lax.all_to_all(values, axes, split_axis=0, concat_axis=0, tiled=True)  100 us
    dot_general x28, matrix products, dot(): lax.dot_general(a, b, ((contract[:1], contract[1:]), ((), ())), preferred...  42.5 us
    all_to_all x8, starting transfers between devices, swap(): return lax.all_to_all(values, axes, split_axis=0, concat_axis=0, tiled=True)  41.7 us
    ppermute x7, starting transfers between devices, trade_cores(): return lax.ppermute(values, 'pipe', [(0, 1), (1, 0)])  24.3 us
    select_n x3, other arithmetic, shards(): jnp.where(first, b, a)  7.42 us
  transfers between devices with their start and end apart: 17, of which 7 were waited for; matrix products, arithmetic and copies ran while one was open for 14% of the time, Pallas kernels for 0%

profile of v5, /device:TPU:1, one launch (start us, length us, event | category | flops | bytes accessed | tf_op | source)
XLA Modules:
  0.0 365.9 jit_solution(16605677328364687571)
XLA Ops:
  7.2 3.3 collective-permute-start.1
  11.0 1.2 copy-done
  13.6 1.3 pack.1
  14.9 6.9 %all-to-all-start = ((bf16[16,32,1024]{2,1,0:T(8,128)(2,1)}), bf16[16,32,1024]{2,1,0:T(8,128)(2,1)S(1)}, u32[]{:S(2)}, u32[]{:S(2)}) async-start(bf16[16,32,1024]{2,1,0:T(8,128)(2,1)} %bitcast.5), calls=%async_computation | async-start | bytes 2097152 | tf_op jit(solution)/shard_map/all_to_all | solution.py:21
  21.8 1.9 broadcast_select_fusion.2
  23.8 1.7 broadcast_select_fusion.3
  25.6 3.2 pad_maximum_fusion
  28.8 3.8 %broadcast_select_fusion = (bf16[1024,896]{1,0:T(8,128)(2,1)}, bf16[1024,896]{1,0:T(8,128)(2,1)}) fusion(bf16[1024,896]{1,0:T(8,128)(2,1)} %collective-permute-done.2, pred[]{:T(512)S(6)} %eq.113, bf16[1,1,1024,896]{3,2,1,0:T(8,128)(2,1)S(1)} %copy-done.17), kind=kLoop, calls=%fused_computation.9 | loop fusion | flops 1835008 | bytes 7340033 | tf_op jit(solution)/shard_map/jit(_where)/select_n | solution.py:147
  32.6 17.0 %all-to-all-done = bf16[16,32,1024]{2,1,0:T(8,128)(2,1)S(1)} async-done(((bf16[16,32,1024]{2,1,0:T(8,128)(2,1)}), bf16[16,32,1024]{2,1,0:T(8,128)(2,1)S(1)}, u32[]{:S(2)}, u32[]{:S(2)}) %all-to-all-start) | async-done | bytes 1048608 | tf_op jit(solution)/shard_map/all_to_all | solution.py:21
  52.7 22.4 %all_to_all.70 = bf16[16,32,896]{2,1,0:T(8,128)(2,1)S(1)} all-to-all(bf16[16,32,896]{2,1,0:T(8,128)(2,1)S(1)} %pad_maximum_fusion.3), channel_id=1, replica_groups=mesh['dp'=8,'expert'=16,'pipe'=2] {'expert'}, dimensions={0} | all-to-all | bytes 1835008 | tf_op jit(solution)/shard_map/all_to_all | solution.py:21
  75.3 2.3 convolution_convert_fusion.1
  77.6 3.6 all-to-all-start.2
  81.2 3.0 convolution_convert_fusion.3
  84.2 26.2 %all-to-all-done.2 = bf16[8,32,2048]{2,1,0:T(8,128)(2,1)S(1)} async-done(((bf16[8,32,2048]{2,1,0:T(8,128)(2,1)}), bf16[8,32,2048]{2,1,0:T(8,128)(2,1)S(1)}, u32[]{:S(2)}, u32[]{:S(2)}) %all-to-all-start.2) | async-done | bytes 1048608 | tf_op jit(solution)/shard_map/all_to_all | solution.py:21
  111.5 3.5 all-to-all-start.3
  115.3 5.2 %reduce-scatter.2.cloned.1.call-done = bf16[32,1024]{1,0:T(8,128)(2,1)} async-done(((bf16[256,1024]{1,0:T(8,128)(2,1)}), bf16[32,1024]{1,0:T(8,128)(2,1)}) %reduce-scatter.2.cloned.1.call-update) | async-done | bytes 65552 | tf_op jit(solution)/shard_map/reduce_scatter | solution.py:194
  120.5 11.4 %all-to-all-done.3 = bf16[8,32,1024]{2,1,0:T(8,128)(2,1)S(1)} async-done(((bf16[8,32,1024]{2,1,0:T(8,128)(2,1)}), bf16[8,32,1024]{2,1,0:T(8,128)(2,1)S(1)}, u32[]{:S(2)}, u32[]{:S(2)}) %all-to-all-start.3) | async-done | bytes 524320 | tf_op jit(solution)/shard_map/all_to_all | solution.py:21
  131.8 3.0 convolution_convert_fusion.6
  134.8 4.6 %all-to-all-start.4 = ((bf16[16,16,896]{2,1,0:T(8,128)(2,1)}), bf16[16,16,896]{2,1,0:T(8,128)(2,1)S(1)}, u32[]{:S(2)}, u32[]{:S(2)}) async-start(bf16[16,16,896]{2,1,0:T(8,128)(2,1)} %bitcast.150), calls=%async_computation.5 | async-start | bytes 917504 | tf_op jit(solution)/shard_map/all_to_all | solution.py:21
  140.6 8.6 %all-to-all-done.4 = bf16[16,16,896]{2,1,0:T(8,128)(2,1)S(1)} async-done(((bf16[16,16,896]{2,1,0:T(8,128)(2,1)}), bf16[16,16,896]{2,1,0:T(8,128)(2,1)S(1)}, u32[]{:S(2)}, u32[]{:S(2)}) %all-to-all-start.4) | async-done | bytes 458784 | tf_op jit(solution)/shard_map/all_to_all | solution.py:21
  149.3 1.4 fusion.7
  151.5 11.9 %all_to_all.71 = bf16[16,16,896]{2,1,0:T(8,128)(2,1)S(1)} all-to-all(bf16[16,16,896]{2,1,0:T(8,128)(2,1)S(1)} %bitcast.132), channel_id=1, replica_groups=mesh['dp'=8,'expert'=16,'pipe'=2] {'expert'}, dimensions={0} | all-to-all | bytes 917504 | tf_op jit(solution)/shard_map/all_to_all | solution.py:21
  163.3 3.3 convolution_convert_fusion
  166.6 28.4 %all_to_all.72 = bf16[8,32,2048]{2,1,0:T(8,128)(2,1)S(1)} all-to-all(bf16[8,32,2048]{2,1,0:T(8,128)(2,1)S(1)} %bitcast.145), channel_id=1, replica_groups=mesh['dp'=8,'expert'=16,'pipe'=2] {'dp'}, dimensions={0} | all-to-all | bytes 2097152 | tf_op jit(solution)/shard_map/all_to_all | solution.py:21
  196.4 3.7 %all-to-all-start.7 = ((bf16[8,32,2048]{2,1,0:T(8,128)(2,1)}), bf16[8,32,2048]{2,1,0:T(8,128)(2,1)S(1)}, u32[]{:S(2)}, u32[]{:S(2)}) async-start(bf16[8,32,2048]{2,1,0:T(8,128)(2,1)} %broadcast_in_dim.21), calls=%async_computation.8 | async-start | bytes 2097152 | tf_op jit(solution)/shard_map/all_to_all | solution.py:21
  202.0 25.7 %all-to-all-done.7 = bf16[8,32,2048]{2,1,0:T(8,128)(2,1)S(1)} async-done(((bf16[8,32,2048]{2,1,0:T(8,128)(2,1)}), bf16[8,32,2048]{2,1,0:T(8,128)(2,1)S(1)}, u32[]{:S(2)}, u32[]{:S(2)}) %all-to-all-start.7) | async-done | bytes 1048608 | tf_op jit(solution)/shard_map/all_to_all | solution.py:21
  227.7 3.4 convolution_convert_fusion.9
  231.1 11.2 %all_to_all.73 = bf16[16,16,896]{2,1,0:T(8,128)(2,1)S(1)} all-to-all(bf16[16,16,896]{2,1,0:T(8,128)(2,1)S(1)} %bitcast.151), channel_id=1, replica_groups=mesh['dp'=8,'expert'=16,'pipe'=2] {'expert'}, dimensions={0} | all-to-all | bytes 917504 | tf_op jit(solution)/shard_map/all_to_all | solution.py:21
  243.4 11.2 %all_to_all.74 = bf16[16,16,896]{2,1,0:T(8,128)(2,1)S(1)} all-to-all(bf16[16,16,896]{2,1,0:T(8,128)(2,1)S(1)} %bitcast.129), channel_id=1, replica_groups=mesh['dp'=8,'expert'=16,'pipe'=2] {'expert'}, dimensions={0} | all-to-all | bytes 917504 | tf_op jit(solution)/shard_map/all_to_all | solution.py:21
  254.7 2.4 convolution_convert_fusion.2
  257.1 15.2 %all_to_all.75 = bf16[8,32,1024]{2,1,0:T(8,128)(2,1)} all-to-all(bf16[8,32,1024]{2,1,0:T(8,128)(2,1)S(1)} %bitcast.147), channel_id=1, replica_groups=mesh['dp'=8,'expert'=16,'pipe'=2] {'dp'}, dimensions={0} | all-to-all | bytes 1048576 | tf_op jit(solution)/shard_map/all_to_all | solution.py:21
  272.3 1.1 reduce_sum.52
  274.3 4.2 %all-to-all-start.11 = ((bf16[8,32,1024]{2,1,0:T(8,128)(2,1)}), bf16[8,32,1024]{2,1,0:T(8,128)(2,1)}, u32[]{:S(2)}, u32[]{:S(2)}) async-start(bf16[8,32,1024]{2,1,0:T(8,128)(2,1)} %broadcast_in_dim.22), calls=%async_computation.12 | async-start | bytes 1048576 | tf_op jit(solution)/shard_map/all_to_all | solution.py:21
  279.3 10.8 %collective-permute-start.3 = (bf16[256,896]{1,0:T(8,128)(2,1)}, bf16[256,896]{1,0:T(8,128)(2,1)}, u32[]{:S(2)}, u32[]{:S(2)}) collective-permute-start(bf16[256,896]{1,0:T(8,128)(2,1)} %broadcast_select_fusion.10), channel_id=1, source_target_pairs={{0,1},{1,0},{2,3},{3,2},{4,5},{5,4},{6,7},{7,6},{8,9},{9,8},{10,11... | collective-permute-start | bytes 1376264 | tf_op jit(solution)/shard_map/ppermute | solution.py:25
  290.1 3.2 convolution_convert_fusion.4
  293.3 1.9 fusion.15
  295.2 3.8 %convolution_convert_fusion.8 = bf16[256,896]{1,0:T(8,128)(2,1)S(1)} fusion(bf16[896,2048]{1,0:T(8,128)(2,1)} %get-tuple-element.14, bf16[256,1024]{1,0:T(8,128)(2,1)S(1)} %get-tuple-element.31, bf16[256,1024]{1,0:T(8,128)(2,1)S(1)} %get-tuple-element.30), kind=kOutput, calls=%fused_computation.40 | convolution fusion | flops 941850624 | bytes 5177344 | tf_op jit(solution)/shard_map/dot_general | solution.py:29
  300.1 4.3 %all-to-all-start.12 = ((bf16[16,32,896]{2,1,0:T(8,128)(2,1)}), bf16[16,32,896]{2,1,0:T(8,128)(2,1)}, u32[]{:S(2)}, u32[]{:S(2)}) async-start(bf16[16,32,896]{2,1,0:T(8,128)(2,1)} %pad_maximum_fusion.4), calls=%async_computation.13 | async-start | bytes 1835008 | tf_op jit(solution)/shard_map/all_to_all | solution.py:21
  304.4 2.0 broadcast_select_fusion.8
  306.4 9.2 %collective-permute-start.5 = (bf16[256,1024]{1,0:T(8,128)(2,1)}, bf16[256,1024]{1,0:T(8,128)(2,1)}, u32[]{:S(2)}, u32[]{:S(2)}) collective-permute-start(bf16[256,1024]{1,0:T(8,128)(2,1)} %broadcast_select_fusion.8), channel_id=1, source_target_pairs={{0,1},{1,0},{2,3},{3,2},{4,5},{5,4},{6,7},{7,6},{8,9},{9,8},{10,11... | collective-permute-start | bytes 1572872 | tf_op jit(solution)/shard_map/ppermute | solution.py:25
  316.5 1.5 broadcast_select_fusion.6
  318.5 1.3 fusion.66
  321.8 11.0 %all-to-all-start.13 = ((bf16[16,32,896]{2,1,0:T(8,128)(2,1)}), bf16[16,32,896]{2,1,0:T(8,128)(2,1)S(1)}, u32[]{:S(2)}, u32[]{:S(2)}) async-start(bf16[16,32,896]{2,1,0:T(8,128)(2,1)} %bitcast.122), calls=%async_computation.14 | async-start | bytes 1835008 | tf_op jit(solution)/shard_map/all_to_all | solution.py:21
  332.8 1.9 fusion.28
  334.7 3.2 fusion.2
  339.3 3.1 fusion
  342.4 3.1 fusion.1
  345.5 12.6 %all-to-all-done.13 = bf16[16,32,896]{2,1,0:T(8,128)(2,1)S(1)} async-done(((bf16[16,32,896]{2,1,0:T(8,128)(2,1)}), bf16[16,32,896]{2,1,0:T(8,128)(2,1)S(1)}, u32[]{:S(2)}, u32[]{:S(2)}) %all-to-all-start.13) | async-done | bytes 917536 | tf_op jit(solution)/shard_map/all_to_all | solution.py:21
  (108 shorter events, 21.2 us)
Async XLA Ops:
  7.2 14.6 %collective-permute-start.1 = (bf16[896,1024]{1,0:T(8,128)(2,1)}, bf16[896,1024]{1,0:T(8,128)(2,1)}, u32[]{:S(2)}, u32[]{:S(2)}) collective-permute-start(bf16[896,1024]{1,0:T(8,128)(2,1)} %bitcast.133), channel_id=1, source_target_pairs={{0,1},{1,0},{2,3},{3,2},{4,5},{5,4},{6,7},{7,6},{8,9},{9,8},{10,11... | collective-permute-start | bytes 5505032 | tf_op jit(solution)/shard_map/ppermute | solution.py:25
  10.5 13.2 %collective-permute-start = (bf16[896,1024]{1,0:T(8,128)(2,1)}, bf16[896,1024]{1,0:T(8,128)(2,1)}, u32[]{:S(2)}, u32[]{:S(2)}) collective-permute-start(bf16[896,1024]{1,0:T(8,128)(2,1)} %bitcast.134), channel_id=1, source_target_pairs={{0,1},{1,0},{2,3},{3,2},{4,5},{5,4},{6,7},{7,6},{8,9},{9,8},{10,11... | collective-permute-start | bytes 5505032 | tf_op jit(solution)/shard_map/ppermute | solution.py:25
  10.6 18.2 %collective-permute-start.2 = (bf16[1024,896]{1,0:T(8,128)(2,1)}, bf16[1024,896]{1,0:T(8,128)(2,1)}, u32[]{:S(2)}, u32[]{:S(2)}) collective-permute-start(bf16[1024,896]{1,0:T(8,128)(2,1)} %bitcast.135), channel_id=1, source_target_pairs={{0,1},{1,0},{2,3},{3,2},{4,5},{5,4},{6,7},{7,6},{8,9},{9,8},{10,11... | collective-permute-start | bytes 5505032 | tf_op jit(solution)/shard_map/ppermute | solution.py:25
  11.0 1.2 copy-start
  12.2 0.7 copy-start.1
  12.9 0.7 copy-start.2
  13.6 8.2 %copy-start.15 = (bf16[1,1,896,1024]{3,2,1,0:T(8,128)(2,1)S(1)}, bf16[1,1,896,1024]{3,2,1,0:T(8,128)(2,1)}, u32[]{:S(2)}) copy-start(bf16[1,1,896,1024]{3,2,1,0:T(8,128)(2,1)} %param.10) | copy-start | bytes 5505028
  14.9 34.8 %all-to-all-start = ((bf16[16,32,1024]{2,1,0:T(8,128)(2,1)}), bf16[16,32,1024]{2,1,0:T(8,128)(2,1)S(1)}, u32[]{:S(2)}, u32[]{:S(2)}) async-start(bf16[16,32,1024]{2,1,0:T(8,128)(2,1)} %bitcast.5), calls=%async_computation | async-start | bytes 2097152 | tf_op jit(solution)/shard_map/all_to_all | solution.py:21
  21.8 2.1 copy-start.16
  25.6 3.3 copy-start.17
  50.6 2.0 copy-start.21
  50.9 191.7 %copy-start.19 = (pred[256,256]{0,1:T(32,128)(4,1)}, pred[256,256]{0,1:T(32,128)(4,1)S(1)}, u32[]{:S(2)}) copy-start(pred[256,256]{0,1:T(32,128)(4,1)S(1)} %fusion.12) | copy-start | bytes 196612
  52.7 22.5 %copy-start.9 = (bf16[896,2048]{1,0:T(8,128)(2,1)S(1)}, bf16[896,2048]{1,0:T(8,128)(2,1)}, u32[]{:S(2)}) copy-start(bf16[896,2048]{1,0:T(8,128)(2,1)} %get-tuple-element.14) | copy-start | bytes 11010052
  75.3 240.4 %copy-start.3 = (bf16[16,16,896]{2,1,0:T(8,128)(2,1)}, bf16[16,16,896]{2,1,0:T(8,128)(2,1)S(1)}, u32[]{:S(2)}) copy-start(bf16[16,16,896]{2,1,0:T(8,128)(2,1)S(1)} %get-tuple-element.38) | copy-start | bytes 1376260
  77.6 32.9 %all-to-all-start.2 = ((bf16[8,32,2048]{2,1,0:T(8,128)(2,1)}), bf16[8,32,2048]{2,1,0:T(8,128)(2,1)S(1)}, u32[]{:S(2)}, u32[]{:S(2)}) async-start(bf16[8,32,2048]{2,1,0:T(8,128)(2,1)} %bitcast.144), calls=%async_computation.2 | async-start | bytes 2097152 | tf_op jit(solution)/shard_map/all_to_all | solution.py:21
  81.1 39.3 %reduce-scatter.2.cloned.1.call-start = ((), (), s32[]{:S(2)}) async-start(), calls=%async_computation.15 | async-start | bytes 589824 | tf_op jit(solution)/shard_map/reduce_scatter | solution.py:194
  110.6 24.2 %copy-start.10 = (f32[32,2048]{1,0:T(8,128)}, f32[32,2048]{1,0:T(8,128)S(1)}, u32[]{:S(2)}) copy-start(f32[32,2048]{1,0:T(8,128)S(1)} %convert_reduce_fusion.1) | copy-start | bytes 786436
  111.5 20.3 %all-to-all-start.3 = ((bf16[8,32,1024]{2,1,0:T(8,128)(2,1)}), bf16[8,32,1024]{2,1,0:T(8,128)(2,1)S(1)}, u32[]{:S(2)}, u32[]{:S(2)}) async-start(bf16[8,32,1024]{2,1,0:T(8,128)(2,1)} %broadcast_in_dim.20), calls=%async_computation.3 | async-start | bytes 1048576 | tf_op jit(solution)/shard_map/all_to_all | solution.py:21
  134.8 15.9 %copy-start.22 = (pred[256,256]{0,1:T(32,128)(4,1)S(1)}, pred[256,256]{0,1:T(32,128)(4,1)}, u32[]{:S(2)}) copy-start(pred[256,256]{0,1:T(32,128)(4,1)} %copy-done.21) | copy-start | bytes 196612
  134.8 14.4 %all-to-all-start.4 = ((bf16[16,16,896]{2,1,0:T(8,128)(2,1)}), bf16[16,16,896]{2,1,0:T(8,128)(2,1)S(1)}, u32[]{:S(2)}, u32[]{:S(2)}) async-start(bf16[16,16,896]{2,1,0:T(8,128)(2,1)} %bitcast.150), calls=%async_computation.5 | async-start | bytes 917504 | tf_op jit(solution)/shard_map/all_to_all | solution.py:21
  150.7 0.8 copy-start.7
  166.6 28.5 %copy-start.25 = (bf16[32,1024]{1,0:T(8,128)(2,1)S(1)}, bf16[32,1024]{1,0:T(8,128)(2,1)}, u32[]{:S(2)}) copy-start(bf16[32,1024]{1,0:T(8,128)(2,1)} %reduce-scatter.2.cloned.1.call-done) | copy-start | bytes 196612
  196.4 31.3 %all-to-all-start.7 = ((bf16[8,32,2048]{2,1,0:T(8,128)(2,1)}), bf16[8,32,2048]{2,1,0:T(8,128)(2,1)S(1)}, u32[]{:S(2)}, u32[]{:S(2)}) async-start(bf16[8,32,2048]{2,1,0:T(8,128)(2,1)} %broadcast_in_dim.21), calls=%async_computation.8 | async-start | bytes 2097152 | tf_op jit(solution)/shard_map/all_to_all | solution.py:21
  200.1 54.5 %all-gather.2.cloned.1.call-start = ((), (), s32[]{:S(2)}) async-start(), calls=%async_computation.16 | async-start | bytes 1769472 | tf_op jit(solution)/shard_map/all_gather | solution.py:205
  227.7 14.6 %copy-start.23 = (pred[256,256]{0,1:T(32,128)(4,1)S(1)}, pred[256,256]{0,1:T(32,128)(4,1)}, u32[]{:S(2)}) copy-start(pred[256,256]{0,1:T(32,128)(4,1)} %copy-done.21) | copy-start | bytes 196612
  242.6 0.8 copy-start.5
  254.6 61.0 %copy-start.4 = (bf16[16,16,896]{2,1,0:T(8,128)(2,1)}, bf16[16,16,896]{2,1,0:T(8,128)(2,1)S(1)}, u32[]{:S(2)}) copy-start(bf16[16,16,896]{2,1,0:T(8,128)(2,1)S(1)} %all_to_all.74) | copy-start | bytes 1376260
  274.3 19.0 %all-to-all-start.11 = ((bf16[8,32,1024]{2,1,0:T(8,128)(2,1)}), bf16[8,32,1024]{2,1,0:T(8,128)(2,1)}, u32[]{:S(2)}, u32[]{:S(2)}) async-start(bf16[8,32,1024]{2,1,0:T(8,128)(2,1)} %broadcast_in_dim.22), calls=%async_computation.12 | async-start | bytes 1048576 | tf_op jit(solution)/shard_map/all_to_all | solution.py:21
  279.3 59.9 %collective-permute-start.3 = (bf16[256,896]{1,0:T(8,128)(2,1)}, bf16[256,896]{1,0:T(8,128)(2,1)}, u32[]{:S(2)}, u32[]{:S(2)}) collective-permute-start(bf16[256,896]{1,0:T(8,128)(2,1)} %broadcast_select_fusion.10), channel_id=1, source_target_pairs={{0,1},{1,0},{2,3},{3,2},{4,5},{5,4},{6,7},{7,6},{8,9},{9,8},{10,11... | collective-permute-start | bytes 1376264 | tf_op jit(solution)/shard_map/ppermute | solution.py:25
  295.2 3.9 %copy-start.11 = (bf16[256,1024]{1,0:T(8,128)(2,1)}, bf16[256,1024]{1,0:T(8,128)(2,1)S(1)}, u32[]{:S(2)}) copy-start(bf16[256,1024]{1,0:T(8,128)(2,1)S(1)} %get-tuple-element.30) | copy-start | bytes 1572868
  295.2 3.9 %copy-start.13 = (bf16[256,1024]{1,0:T(8,128)(2,1)}, bf16[256,1024]{1,0:T(8,128)(2,1)S(1)}, u32[]{:S(2)}) copy-start(bf16[256,1024]{1,0:T(8,128)(2,1)S(1)} %get-tuple-element.31) | copy-start | bytes 1572868
  295.2 3.9 %copy-start.24 = (bf16[256,896]{1,0:T(8,128)(2,1)S(1)}, bf16[256,896]{1,0:T(8,128)(2,1)}, u32[]{:S(2)}) copy-start(bf16[256,896]{1,0:T(8,128)(2,1)} %convolution_convert_fusion.4) | copy-start | bytes 1376260
  300.1 18.5 %all-to-all-start.12 = ((bf16[16,32,896]{2,1,0:T(8,128)(2,1)}), bf16[16,32,896]{2,1,0:T(8,128)(2,1)}, u32[]{:S(2)}, u32[]{:S(2)}) async-start(bf16[16,32,896]{2,1,0:T(8,128)(2,1)} %pad_maximum_fusion.4), calls=%async_computation.13 | async-start | bytes 1835008 | tf_op jit(solution)/shard_map/all_to_all | solution.py:21
  304.4 12.1 %copy-start.12 = (bf16[256,1024]{1,0:T(8,128)(2,1)S(1)}, bf16[256,1024]{1,0:T(8,128)(2,1)}, u32[]{:S(2)}) copy-start(bf16[256,1024]{1,0:T(8,128)(2,1)} %copy-done.11) | copy-start | bytes 1572868
  304.4 12.1 %copy-start.14 = (bf16[256,1024]{1,0:T(8,128)(2,1)S(1)}, bf16[256,1024]{1,0:T(8,128)(2,1)}, u32[]{:S(2)}) copy-start(bf16[256,1024]{1,0:T(8,128)(2,1)} %copy-done.13) | copy-start | bytes 1572868
  306.4 28.3 %collective-permute-start.5 = (bf16[256,1024]{1,0:T(8,128)(2,1)}, bf16[256,1024]{1,0:T(8,128)(2,1)}, u32[]{:S(2)}, u32[]{:S(2)}) collective-permute-start(bf16[256,1024]{1,0:T(8,128)(2,1)} %broadcast_select_fusion.8), channel_id=1, source_target_pairs={{0,1},{1,0},{2,3},{3,2},{4,5},{5,4},{6,7},{7,6},{8,9},{9,8},{10,11... | collective-permute-start | bytes 1572872 | tf_op jit(solution)/shard_map/ppermute | solution.py:25
  316.5 18.2 %collective-permute-start.6 = (bf16[256,896]{1,0:T(8,128)(2,1)}, bf16[256,896]{1,0:T(8,128)(2,1)}, u32[]{:S(2)}, u32[]{:S(2)}) collective-permute-start(bf16[256,896]{1,0:T(8,128)(2,1)} %broadcast_select_fusion.9), channel_id=1, source_target_pairs={{0,1},{1,0},{2,3},{3,2},{4,5},{5,4},{6,7},{7,6},{8,9},{9,8},{10,11... | collective-permute-start | bytes 1376264 | tf_op jit(solution)/shard_map/ppermute | solution.py:25
  318.0 1.8 copy-start.8
  318.0 2.3 copy-start.6
  318.0 2.3 copy-start.20
  318.0 21.2 %collective-permute-start.4 = (bf16[256,2048]{1,0:T(8,128)(2,1)}, bf16[256,2048]{1,0:T(8,128)(2,1)}, u32[]{:S(2)}, u32[]{:S(2)}) collective-permute-start(bf16[256,2048]{1,0:T(8,128)(2,1)} %get-tuple-element.28), channel_id=1, source_target_pairs={{0,1},{1,0},{2,3},{3,2},{4,5},{5,4},{6,7},{7,6},{8,9},{9,8},{10,11... | collective-permute-start | bytes 3145736 | tf_op jit(solution)/shard_map/ppermute | solution.py:25
  318.5 1.3 copy-start.18
  321.8 36.3 %all-to-all-start.13 = ((bf16[16,32,896]{2,1,0:T(8,128)(2,1)}), bf16[16,32,896]{2,1,0:T(8,128)(2,1)S(1)}, u32[]{:S(2)}, u32[]{:S(2)}) async-start(bf16[16,32,896]{2,1,0:T(8,128)(2,1)} %bitcast.122), calls=%async_computation.14 | async-start | bytes 1835008 | tf_op jit(solution)/shard_map/all_to_all | solution.py:21
Sparse Core Ops, SparseCore 0:
  85.1 35.3 reduce-scatter.1
  203.5 42.4 all-gather.1
